TPU v7x, 128 devices: a whole 4x4x4 slice. The times are simulated.
128 devices in a mesh: group: 16 (over z, y), local: 8 (over x, core).
Axes of the slice: x: 4, y: 4, z: 4, core: 2. Of those that a mesh axis runs over, the one named last changes fastest.
Arguments:
- hidden: float32 [2, 128, 7168], P(None, ('group', 'local')), may hold values from -6 to 6
- routes: int32 [2, 128, 8], P(None, ('group', 'local')), may hold values from 0 to 31, as said below
- slots: int32 [2, 128, 8], P(None, ('group', 'local')), may hold values from -1 to 95, as said below
- route_weight: bfloat16 [2, 128, 8], P(None, ('group', 'local')), may hold values from 0.049804688 to 0.5
- expert_gate: bfloat16 [32, 7168, 2048], P('group', None, 'local'), may hold values from -0.0625 to 0.0625
- expert_up: bfloat16 [32, 7168, 2048], P('group', None, 'local'), may hold values from -0.0625 to 0.0625
- expert_down: bfloat16 [32, 2048, 7168], P('group', 'local'), may hold values from -0.125 to 0.125
- shared_gate: bfloat16 [7168, 2048], P(None, ('group', 'local')), may hold values from -0.0625 to 0.0625
- shared_up: bfloat16 [7168, 2048], P(None, ('group', 'local')), may hold values from -0.0625 to 0.0625
- shared_down: bfloat16 [2048, 7168], P(('group', 'local')), may hold values from -0.125 to 0.125
Outputs:
- moe_output: float32 [2, 128, 7168], P(None, ('group', 'local'))
Inputs may be any that keep to these rules, and one draw needn't show every extreme that they name: `routes`: each row names 8 different experts, all within at most 4 node groups, node group n holding experts 4 n to 4 n + 3. `slots`: the slot of a route is the number of earlier routes of the same step to the same expert (rows in order, then the routes of a row in order) if that number is under 96, else -1; in every step some expert is named by more than 96 routes.
All inputs are finite; a program needn't handle non-finite values.
Results may differ from a plain program's by a relative error of at most 0.005.
Values may be sent and summed in bfloat16 or wider, within the bound.
No kernel may reach another device: no remote copies, remote signals or barrier semaphores. Data moves between devices by JAX's collectives and lax.ppermute only.
A program may use at most 128 MiB of HBM per device.

v0:
```python
import jax
import jax.numpy as jnp
from jax import lax
from jax.sharding import PartitionSpec as P


def expert_block(rows, gate_w, up_w, down_w):
    gate_act = jnp.dot(rows, gate_w, preferred_element_type=jnp.float32)
    up_act = jnp.dot(rows, up_w, preferred_element_type=jnp.float32)
    units = (jax.nn.silu(gate_act) * up_act).astype(jnp.bfloat16)
    return jnp.dot(units, down_w, preferred_element_type=jnp.float32)


def fill_buffer(rounded, routes_flat, slots_flat, expert, capacity, per_row):
    count = routes_flat.shape[0]
    token_ids = jnp.arange(count, dtype=jnp.int32) // per_row
    match = (routes_flat == expert) & (slots_flat >= 0)
    hits = match[:, None] & (slots_flat[:, None] == jnp.arange(capacity, dtype=jnp.int32)[None, :])
    source = jnp.sum(jnp.where(hits, token_ids[:, None], 0), axis=0)
    present = jnp.any(hits, axis=0)
    return jnp.where(present[:, None], rounded[source], jnp.zeros((), jnp.bfloat16))


def body(
    hidden,
    routes,
    slots,
    route_weight,
    expert_gate,
    expert_up,
    expert_down,
    shared_gate,
    shared_up,
    shared_down,
):
    steps = hidden.shape[0]
    tok_dev = hidden.shape[1]
    per_row = routes.shape[2]
    groups = lax.axis_size("group")
    in_group = lax.axis_size("local")
    tokens = tok_dev * groups * in_group
    capacity = 3 * tokens // 4
    group_at = lax.axis_index("group")
    rounded = hidden.astype(jnp.bfloat16)

    def routed_term(all_rows, weights_all, routes_all, slots_all):
        routes_flat = routes_all.reshape(-1)
        slots_flat = slots_all.reshape(-1)
        outputs = jnp.concatenate(
            [
                expert_block(
                    fill_buffer(
                        all_rows, routes_flat, slots_flat, 2 * group_at + owned, capacity, per_row
                    ),
                    expert_gate[owned],
                    expert_up[owned],
                    expert_down[owned],
                )
                for owned in range(2)
            ],
            axis=0,
        )
        shared_full = expert_block(all_rows, shared_gate, shared_up, shared_down)
        columns = jnp.arange(2 * capacity, dtype=jnp.int32)

        def term(start, count):
            weight_rows = weights_all.astype(jnp.float32)
            local_expert = routes_all - 2 * group_at
            keep = (local_expert >= 0) & (local_expert < 2) & (slots_all >= 0)
            where_at = jnp.where(keep, local_expert * capacity + slots_all, -1)
            scale = jnp.where(keep, weight_rows, 0.0)
            mixing = jnp.sum(
                jnp.where(where_at[:, :, None] == columns[None, None, :], scale[:, :, None], 0.0),
                axis=1,
            )
            return shared_full + jnp.dot(
                mixing, outputs, precision=lax.Precision.HIGHEST, preferred_element_type=jnp.float32
            )

        return term

    results = []
    for index in range(steps):
        all_rows, weights_all, routes_all, slots_all = (
            lax.all_gather(rounded[index], ("group", "local"), axis=0, tiled=True),
            lax.all_gather(route_weight[index], ("group", "local"), axis=0, tiled=True),
            lax.all_gather(routes[index], ("group", "local"), axis=0, tiled=True),
            lax.all_gather(slots[index], ("group", "local"), axis=0, tiled=True),
        )
        term = routed_term(all_rows, weights_all, routes_all, slots_all)
        results.append(
            lax.psum_scatter(
                term(jnp.int32(0), tok_dev * lax.axis_size(("group", "local"))),
                ("group", "local"),
                scatter_dimension=0,
                tiled=True,
            )
        )
    return jnp.stack(results)


def solution(mesh):
    return jax.shard_map(
        body,
        mesh=mesh,
        in_specs=(
            P(None, ("group", "local"), None),
            P(None, ("group", "local"), None),
            P(None, ("group", "local"), None),
            P(None, ("group", "local"), None),
            P("group", None, "local"),
            P("group", None, "local"),
            P("group", "local", None),
            P(None, ("group", "local")),
            P(None, ("group", "local")),
            P(("group", "local"), None),
        ),
        out_specs=P(None, ("group", "local"), None),
        check_vma=False,
    )
```

profile of v0, /device:TPU:0, one launch (start us, length us, event | category | flops | bytes accessed | tf_op | source)
XLA Modules:
  0.0 446.9 jit_solution(6273196341621259572)
XLA Ops:
  6.5 0.9 convert_element_type.27
  9.7 33.1 %all-gather.7 = bf16[128,1,8]{2,1,0:T(2,128)(2,1)S(1)} all-gather(bf16[1,1,8]{2,1,0:T(2,128)(2,1)S(1)} %get-tuple-element.36), channel_id=9, replica_groups=mesh['group'=16,'local'=8] {'group','local'}, dimensions={0}, use_global_device_ids=true | all-gather | bytes 2064 | tf_op jit(solution)/shard_map/all_gather | solution.py:86
  43.5 29.6 %all-gather.6 = s32[128,1,8]{2,1,0:T(1,128)S(1)} all-gather(s32[1,1,8]{2,1,0:T(1,128)S(1)} %get-tuple-element.34), channel_id=8, replica_groups=mesh['group'=16,'local'=8] {'group','local'}, dimensions={0}, use_global_device_ids=true | all-gather | bytes 4128 | tf_op jit(solution)/shard_map/all_gather | solution.py:88
  73.8 29.4 %all-gather.5 = s32[128,1,8]{2,1,0:T(1,128)S(1)} all-gather(s32[1,1,8]{2,1,0:T(1,128)S(1)} %get-tuple-element.32), channel_id=7, replica_groups=mesh['group'=16,'local'=8] {'group','local'}, dimensions={0}, use_global_device_ids=true | all-gather | bytes 4128 | tf_op jit(solution)/shard_map/all_gather | solution.py:87
  103.1 29.2 %all-gather.3 = bf16[128,1,8]{2,1,0:T(2,128)(2,1)S(1)} all-gather(bf16[1,1,8]{2,1,0:T(2,128)(2,1)S(1)} %get-tuple-element.35), channel_id=5, replica_groups=mesh['group'=16,'local'=8] {'group','local'}, dimensions={0}, use_global_device_ids=true | all-gather | bytes 2064 | tf_op jit(solution)/shard_map/all_gather | solution.py:86
  132.4 29.2 %all-gather.2 = s32[128,1,8]{2,1,0:T(1,128)S(1)} all-gather(s32[1,1,8]{2,1,0:T(1,128)S(1)} %get-tuple-element.33), channel_id=4, replica_groups=mesh['group'=16,'local'=8] {'group','local'}, dimensions={0}, use_global_device_ids=true | all-gather | bytes 4128 | tf_op jit(solution)/shard_map/all_gather | solution.py:88
  161.6 29.3 %all-gather.1 = s32[128,1,8]{2,1,0:T(1,128)S(1)} all-gather(s32[1,1,8]{2,1,0:T(1,128)S(1)} %get-tuple-element.31), channel_id=3, replica_groups=mesh['group'=16,'local'=8] {'group','local'}, dimensions={0}, use_global_device_ids=true | all-gather | bytes 4128 | tf_op jit(solution)/shard_map/all_gather | solution.py:87
  191.9 1.2 add_select_fusion.1
  197.6 2.6 copy.37
  200.2 2.5 gather_fusion.3
  202.7 1.4 gather_fusion.2
  204.1 1.5 fusion.156
  205.6 3.9 fusion.14
  209.5 3.4 fusion.26
  213.0 7.4 %fusion.6 = f32[96,7168]{1,0:T(8,128)} fusion(bf16[2,256,7168]{2,1,0:T(8,128)(2,1)} %param.16, bf16[2,7168,256]{2,1,0:T(8,128)(2,1)} %param.15, bf16[96,7168]{1,0:T(8,128)(2,1)} %gather_fusion.3, pred[96]{0:T(512)(128)(4,1)} %get-tuple-element.18, f32[96,256]{1,0:T(8,128)} %fusion.14), kind=kOutput, calls=%fused_computation.12 | convolution fusion | flops 705478656 | bytes 11567616 | tf_op jit(solution)/shard_map/dot_general | solution.py:11
  220.3 6.9 %fusion.18 = f32[96,7168]{1,0:T(8,128)} fusion(bf16[2,256,7168]{2,1,0:T(8,128)(2,1)} %param.16, bf16[2,7168,256]{2,1,0:T(8,128)(2,1)} %param.15, bf16[96,7168]{1,0:T(8,128)(2,1)S(1)} %gather_fusion.2, pred[96]{0:T(512)(128)(4,1)} %get-tuple-element.17, f32[96,256]{1,0:T(8,128)} %fusion.26), kind=kOutput, calls=%fused_computation.24 | convolution fusion | flops 705478656 | bytes 11567616 | tf_op jit(solution)/shard_map/dot_general | solution.py:11
  227.2 2.7 copy.38
  229.9 1.3 copy-done.2
  231.7 4.2 fusion.68
  236.0 5.6 %fusion.69 = f32[128,7168]{1,0:T(8,128)} fusion(bf16[16,7168]{1,0:T(8,128)(2,1)S(1)} %copy-done, bf16[128,7168]{1,0:T(8,128)(2,1)} %bitcast.105, bf16[7168,16]{0,1:T(8,128)(2,1)S(1)} %copy-done.10, f32[128,16]{0,1:T(8,128)S(1)} %fusion.155), kind=kOutput, calls=%fused_computation.67 | convolution fusion | flops 58732544 | bytes 5971968 | tf_op jit(solution)/shard_map/dot_general | solution.py:11
  241.6 1.4 gather_fusion.1
  243.0 2.8 fusion.16
  245.8 6.8 %fusion.8 = f32[96,7168]{1,0:T(8,128)} fusion(bf16[2,256,7168]{2,1,0:T(8,128)(2,1)} %param.16, bf16[2,7168,256]{2,1,0:T(8,128)(2,1)} %param.15, bf16[96,7168]{1,0:T(8,128)(2,1)S(1)} %gather_fusion.1, pred[96]{0:T(512)(128)(4,1)S(1)} %copy-done.13, f32[96,256]{1,0:T(8,128)S(1)} %fusion.16), kind=kOutput, calls=%fused_computation.14 | convolution fusion | flops 705478656 | bytes 11567200 | tf_op jit(solution)/shard_map/dot_general | solution.py:11
  252.7 1.4 gather_fusion
  254.1 1.1 copy-done.8
  255.2 2.8 fusion.28
  258.0 7.4 %fusion.20 = f32[96,7168]{1,0:T(8,128)} fusion(bf16[2,256,7168]{2,1,0:T(8,128)(2,1)} %param.16, bf16[2,7168,256]{2,1,0:T(8,128)(2,1)} %param.15, bf16[96,7168]{1,0:T(8,128)(2,1)} %copy-done.8, pred[96]{0:T(512)(128)(4,1)S(1)} %copy-done.12, f32[96,256]{1,0:T(8,128)S(1)} %fusion.28), kind=kOutput, calls=%fused_computation.26 | convolution fusion | flops 705478656 | bytes 11567200 | tf_op jit(solution)/shard_map/dot_general | solution.py:11
  265.4 8.3 %convolution_add_fusion = f32[128,7168]{1,0:T(8,128)} fusion(f32[128,7168]{1,0:T(8,128)} %fusion.68, f32[128,192]{0,1:T(8,128)S(1)} %copy-done.11, f32[96,7168]{1,0:T(8,128)S(1)} %copy-done.5, f32[96,7168]{1,0:T(8,128)} %fusion.18), kind=kOutput, calls=%fused_computation.4 | convolution fusion | flops 2116222976 | bytes 12943360 | tf_op jit(solution)/shard_map/dot_general | solution.py:76
  273.8 5.9 %convolution_add_fusion.1 = f32[128,7168]{1,0:T(8,128)} fusion(f32[128,7168]{1,0:T(8,128)S(1)} %copy-done.4, f32[128,192]{0,1:T(8,128)S(1)} %select_reduce_fusion.1, f32[96,7168]{1,0:T(8,128)S(1)} %copy-done.6, f32[96,7168]{1,0:T(8,128)S(1)} %copy-done.7), kind=kOutput, calls=%fused_computation.5 | convolution fusion | flops 2116222976 | bytes 12943360 | tf_op jit(solution)/shard_map/dot_general | solution.py:76
  279.6 158.2 %all-reduce.5.cloned.1.call-done = (f32[128,7168]{1,0:T(8,128)}, f32[128,7168]{1,0:T(8,128)}) async-done(((f32[128,7168]{1,0:T(8,128)}, f32[128,7168]{1,0:T(8,128)}), (f32[128,7168]{1,0:T(8,128)}, f32[128,7168]{1,0:T(8,128)})) %all-reduce.5.cloned.1.call-update) | async-done | bytes 7340048
  437.8 1.0 dynamic-slice_bitcast_fusion
  438.8 1.0 dynamic-slice_bitcast_fusion.1
  (73 shorter events, 10.2 us)
Async XLA Ops:
  6.5 225.2 %copy-start = (bf16[16,7168]{1,0:T(8,128)(2,1)S(1)}, bf16[16,7168]{1,0:T(8,128)(2,1)}, u32[]{:S(2)}) copy-start(bf16[16,7168]{1,0:T(8,128)(2,1)} %param.19) | copy-start | bytes 688132
  6.5 191.1 %all-gather.13.cloned.1.call-start = ((), (), s32[]{:S(2)}) async-start(), calls=%async_computation.1 | async-start | bytes 3698688 | tf_op jit(solution)/shard_map/all_gather | solution.py:85
  8.1 219.1 %all-gather.11.cloned.1.call-start = ((), (), s32[]{:S(2)}) async-start(), calls=%async_computation | async-start | bytes 3698688 | tf_op jit(solution)/shard_map/all_gather | solution.py:85
  8.9 428.9 %all-reduce.5.cloned.1.call-start = ((), (), s32[]{:S(2)}) async-start(), calls=%async_computation.2 | async-start | bytes 14680064
  205.6 3.9 copy-start.14
  227.2 3.9 copy-start.9
  227.2 4.5 %copy-start.10 = (bf16[7168,16]{0,1:T(8,128)(2,1)S(1)}, bf16[7168,16]{0,1:T(8,128)(2,1)}, u32[]{:S(2)}) copy-start(bf16[7168,16]{0,1:T(8,128)(2,1)} %param.18) | copy-start | bytes 688132
  229.9 1.3 copy-start.2
  236.0 5.6 %copy-start.3 = (bf16[128,1,7168]{2,0,1:T(8,128)(2,1)S(1)}, bf16[128,1,7168]{2,0,1:T(8,128)(2,1)}, u32[]{:S(2)}) copy-start(bf16[128,1,7168]{2,0,1:T(8,128)(2,1)} %copy-done.2) | copy-start | bytes 5505028
  241.6 1.4 copy-start.13
  252.7 2.5 copy-start.12
  254.1 1.1 copy-start.8
  258.0 7.4 %copy-start.5 = (f32[96,7168]{1,0:T(8,128)S(1)}, f32[96,7168]{1,0:T(8,128)}, u32[]{:S(2)}) copy-start(f32[96,7168]{1,0:T(8,128)} %fusion.6) | copy-start | bytes 8257540
  258.0 7.4 %copy-start.11 = (f32[128,192]{0,1:T(8,128)S(1)}, f32[128,192]{0,1:T(8,128)}, u32[]{:S(2)}) copy-start(f32[128,192]{0,1:T(8,128)} %select_reduce_fusion) | copy-start | bytes 294916
  265.4 8.4 %copy-start.4 = (f32[128,7168]{1,0:T(8,128)S(1)}, f32[128,7168]{1,0:T(8,128)}, u32[]{:S(2)}) copy-start(f32[128,7168]{1,0:T(8,128)} %fusion.69) | copy-start | bytes 11010052
  265.4 8.4 %copy-start.6 = (f32[96,7168]{1,0:T(8,128)S(1)}, f32[96,7168]{1,0:T(8,128)}, u32[]{:S(2)}) copy-start(f32[96,7168]{1,0:T(8,128)} %fusion.8) | copy-start | bytes 8257540
  265.4 8.3 %copy-start.7 = (f32[96,7168]{1,0:T(8,128)S(1)}, f32[96,7168]{1,0:T(8,128)}, u32[]{:S(2)}) copy-start(f32[96,7168]{1,0:T(8,128)} %fusion.20) | copy-start | bytes 8257540
  279.6 160.8 %copy-start.1 = (bf16[16,7168]{1,0:T(8,128)(2,1)S(1)}, bf16[16,7168]{1,0:T(8,128)(2,1)}, u32[]{:S(2)}) copy-start(bf16[16,7168]{1,0:T(8,128)(2,1)} %param.19) | copy-start | bytes 688132
Sparse Core Ops, SparseCore 0:
  10.3 69.0 all-gather.12
  82.4 63.4 all-gather.10
  279.8 157.9 all-reduce.4
where the time goes:
time: 448 us; the launch traced here: 447 us
  blocking collectives  180 us (40%)
  waiting for transfers between devices  159 us (35%)
  matrix products  67.5 us (15%)
  local copies, waits for them, and re-layouts  20.5 us (5%)
  between operations  13.4 us (3%)
  other arithmetic  6.75 us (2%)
    unnamed x4, waiting for transfers between devices  159 us
    all_gather x2, blocking collectives, body(): lax.all_gather(route_weight[index], ('group', 'local'), axis=0, tiled=True)  62.3 us
    all_gather x2, blocking collectives, body(): lax.all_gather(slots[index], ('group', 'local'), axis=0, tiled=True)  58.8 us
    all_gather x2, blocking collectives, body(): lax.all_gather(routes[index], ('group', 'local'), axis=0, tiled=True)  58.7 us
    dot_general x6, matrix products, expert_block(): return jnp.dot(units, down_w, preferred_element_type=jnp.float32)  38.3 us
    dot_general x6, matrix products, expert_block(): gate_act = jnp.dot(rows, gate_w, preferred_element_type=jnp.float32)  15 us
    dot_general x2, matrix products, term(): jnp.dot(mixing, outputs, precision=lax.Precision.HIGHEST, preferred_eleme...  14.2 us
  transfers between devices with their start and end apart: 3, of which 1 were waited for; matrix products, arithmetic and copies ran while one was open for 9% of the time, Pallas kernels for 0%

commit v1 on v0

v1 whole, which is shorter than its diff:
```python
import jax
import jax.numpy as jnp
from jax import lax
from jax.experimental import pallas as pl
from jax.experimental.pallas import tpu as pltpu
from jax.sharding import PartitionSpec as P

AXES = ("group", "local")
SIZE = (4, 4, 4, 2)
ORDER = ((2, 1, 0), (0, 1, 2))
META = 128


def flat(place):
    index = 0
    for size, at in zip(SIZE, place):
        index = index * size + at
    return index


def places():
    return [(z, y, x, c) for z in range(4) for y in range(4) for x in range(4) for c in range(2)]


def moved(place, stage, by):
    axis = ORDER[place[3]][stage]
    return tuple((at + by) % 4 if dim == axis else at for dim, at in enumerate(place))


def fetch(block, stage, by):
    return lax.ppermute(block, AXES, [(flat(moved(p, stage, by)), flat(p)) for p in places()])


def send(block, stage, by):
    return lax.ppermute(block, AXES, [(flat(p), flat(moved(p, stage, by))) for p in places()])


def swap(block):
    return lax.ppermute(block, AXES, [(flat(p), flat(p[:3] + (1 - p[3],))) for p in places()])


STEP = 1024


def layer_kernel(first_ref, *refs):
    rows = refs[:8]
    metas = refs[8:16]
    gate, up, shared_gate, shared_up, down, shared_down = refs[16:22]
    own, other = refs[22:24]
    acc_gate, acc_up, acc_sg, acc_su, hid, shared_hid, scale = refs[24:]
    at = pl.program_id(0)
    half = pl.num_programs(0) // 2

    @pl.when(at == 0)
    def _():
        for ref in (acc_gate, acc_up, acc_sg, acc_su):
            ref[...] = jnp.zeros_like(ref)

    @pl.when(at < half)
    def _():
        x = jnp.concatenate([r[...] for r in rows], axis=0)
        for e in range(2):
            acc_gate[e] += jnp.dot(x, gate[e], preferred_element_type=jnp.float32)
            acc_up[e] += jnp.dot(x, up[e], preferred_element_type=jnp.float32)
        dims = (((1,), (1,)), ((), ()))
        acc_sg[...] += lax.dot_general(x, shared_gate[...], dims, preferred_element_type=jnp.float32)
        acc_su[...] += lax.dot_general(x, shared_up[...], dims, preferred_element_type=jnp.float32)

    @pl.when(at == half - 1)
    def _():
        weights = jnp.concatenate([m[...] for m in metas], axis=0).astype(jnp.float32)
        lane = lax.broadcasted_iota(jnp.int32, weights.shape, 1)
        for e in range(2):
            g = acc_gate[e]
            hid[e] = (g / (1.0 + jnp.exp(-g)) * acc_up[e]).astype(jnp.bfloat16)
            mine = jnp.where(lane == first_ref[0, 0] + e, weights, 0.0)
            scale[e] = jnp.broadcast_to(jnp.sum(mine, axis=1, keepdims=True), weights.shape)
        g = acc_sg[...]
        shared_hid[...] = (g / (1.0 + jnp.exp(-g)) * acc_su[...]).astype(jnp.bfloat16)

    @pl.when(at >= half)
    def _():
        total = jnp.dot(shared_hid[...], shared_down[...], preferred_element_type=jnp.float32)
        for e in range(2):
            part = jnp.dot(hid[e], down[e], preferred_element_type=jnp.float32)
            total = total + scale[e][:, :1] * part
        own[...] = total[:128]
        other[...] = total[128:].astype(jnp.bfloat16)


def layer(pieces, first, gate, up, down, shared_gate, shared_up, shared_down):
    width = down.shape[2]
    half = width // STEP
    units = gate.shape[2]
    shared = shared_down.shape[0]
    lead = lambda i: jnp.minimum(i, half - 1)
    trail = lambda i: jnp.maximum(i - half, 0)
    return pl.pallas_call(
        layer_kernel,
        grid=(2 * half,),
        out_shape=(
            jax.ShapeDtypeStruct((128, width), jnp.float32),
            jax.ShapeDtypeStruct((128, width), jnp.bfloat16),
        ),
        in_specs=[pl.BlockSpec(memory_space=pltpu.SMEM)]
        + [pl.BlockSpec((32, STEP), lambda i: (0, lead(i)))] * 8
        + [pl.BlockSpec((32, META), lambda i: (0, width // META))] * 8
        + [pl.BlockSpec((2, STEP, units), lambda i: (0, lead(i), 0))] * 2
        + [pl.BlockSpec((shared, STEP), lambda i: (0, lead(i)))] * 2
        + [
            pl.BlockSpec((2, units, STEP), lambda i: (0, 0, trail(i))),
            pl.BlockSpec((shared, STEP), lambda i: (0, trail(i))),
        ],
        out_specs=[pl.BlockSpec((128, STEP), lambda i: (0, trail(i)))] * 2,
        scratch_shapes=[
            pltpu.VMEM((2, 256, units), jnp.float32),
            pltpu.VMEM((2, 256, units), jnp.float32),
            pltpu.VMEM((256, shared), jnp.float32),
            pltpu.VMEM((256, shared), jnp.float32),
            pltpu.VMEM((2, 256, units), jnp.bfloat16),
            pltpu.VMEM((256, shared), jnp.bfloat16),
            pltpu.VMEM((2, 256, META), jnp.float32),
        ],
        compiler_params=pltpu.CompilerParams(vmem_limit_bytes=32 * 1024 * 1024),
        cost_estimate=pl.CostEstimate(
            flops=6 * 256 * width * (2 * units + shared),
            bytes_accessed=6 * width * (2 * units + shared) + 10 * 128 * width,
            transcendentals=256 * (2 * units + shared),
        ),
        name="layer",
    )(first, *pieces, *pieces, gate, up, shared_gate.T, shared_up.T, down, shared_down)


def body(
    hidden,
    routes,
    slots,
    route_weight,
    expert_gate,
    expert_up,
    expert_down,
    shared_gate,
    shared_up,
    shared_down,
):
    experts = jnp.arange(META, dtype=jnp.int32)
    weight = jnp.where(slots >= 0, route_weight.astype(jnp.float32), 0.0)
    dense = jnp.sum(
        jnp.where(routes[..., None] == experts, weight[..., None], 0.0), axis=2
    )
    block = jnp.concatenate([hidden, dense], axis=2)[:, 0].astype(jnp.bfloat16)

    for stage in range(2):
        block = jnp.concatenate([block] + [fetch(block, stage, by) for by in (1, 3, 2)], axis=0)
    mine = [block] + [fetch(block, 2, by) for by in (1, 3, 2)]
    pieces = mine + [swap(piece) for piece in mine]

    first = (2 * lax.axis_index("group")).astype(jnp.int32).reshape(1, 1)
    own, other = layer(
        pieces, first, expert_gate, expert_up, expert_down, shared_gate, shared_up, shared_down
    )
    total = own + swap(other).astype(jnp.float32)
    for stage, kind in ((2, jnp.bfloat16), (1, jnp.float32), (0, jnp.float32)):
        count = total.shape[0] // 4
        parts = [total[i * count : (i + 1) * count] for i in range(4)]
        got = [send(part.astype(kind), stage, by) for part, by in zip(parts[1:], (1, 3, 2))]
        total = parts[0]
        for part in got:
            total = total + part.astype(jnp.float32)
    return total[:, None, :]


def solution(mesh):
    return jax.shard_map(
        body,
        mesh=mesh,
        in_specs=(
            P(None, ("group", "local"), None),
            P(None, ("group", "local"), None),
            P(None, ("group", "local"), None),
            P(None, ("group", "local"), None),
            P("group", None, "local"),
            P("group", None, "local"),
            P("group", "local", None),
            P(None, ("group", "local")),
            P(None, ("group", "local")),
            P(("group", "local"), None),
        ),
        out_specs=P(None, ("group", "local"), None),
        check_vma=False,
    )
```

time: 448 us -> 108 us (0.24)
  blocking collectives: 180 us -> 0 us
  waiting for transfers between devices: 159 us -> 44.2 us
  matrix products: 67.5 us -> 0 us
  starting transfers between devices: 0.08 us -> 34.2 us
  Pallas kernels: 0 us -> 19 us
  between operations: 13.4 us -> 0.1 us
  local copies, waits for them, and re-layouts: 20.5 us -> 7.88 us
    all_gather x6 -> x0, blocking collectives: 180 us -> none  [the longest x2 62.3 us: body(): lax.all_gather(route_weight[index], ('group', 'local'), axis=0, tiled=True)]
    unnamed x4 -> x0, waiting for transfers between devices: 159 us -> none
    dot_general x14 -> x0, matrix products: 67.5 us -> none  [the longest x6 38.3 us: expert_block(): return jnp.dot(units, down_w, preferred_element_type=jnp.float32)]
    ppermute x0 -> x23, waiting for transfers between devices: none -> 44.2 us  [the longest x9 24.6 us: send(): lax.ppermute(block, AXES, [(flat(p), flat(moved(p, stage, by))) for p in...]
    ppermute x0 -> x23, starting transfers between devices: none -> 34.2 us  [the longest x9 20.1 us: fetch(): lax.ppermute(block, AXES, [(flat(moved(p, stage, by)), flat(p)) for p in...]
    pallas_call x0 -> x1, Pallas kernels: none -> 19 us  [layer(): pl.pallas_call(layer_kernel, grid=(2 * half,), out_shape=(jax.ShapeDtypeS...]
    gather x4 -> x0, local copies, waits for them, and re-layouts: 6.74 us -> none  [fill_buffer(): rounded[source]]
  transfers between devices with their start and end apart: 3 -> 23, of which waited for: 1 -> 16; matrix products, arithmetic and copies ran while one was open for 9% -> 0% of each run, Pallas kernels for 0% -> 0%
where the time goes in v1:
time: 108 us
  waiting for transfers between devices  44.2 us (41%)
  starting transfers between devices  34.2 us (32%)
  Pallas kernels  19 us (18%)
  local copies, waits for them, and re-layouts  7.88 us (7%)
  other arithmetic  2.48 us (2%)
    ppermute x9, waiting for transfers between devices, send(): lax.ppermute(block, AXES, [(flat(p), flat(moved(p, stage, by))) for p in...  24.6 us
    ppermute x9, starting transfers between devices, fetch(): lax.ppermute(block, AXES, [(flat(moved(p, stage, by)), flat(p)) for p in...  20.1 us
    pallas_call x1, Pallas kernels, layer(): pl.pallas_call(layer_kernel, grid=(2 * half,), out_shape=(jax.ShapeDtypeS...  19 us
    ppermute x9, waiting for transfers between devices, fetch(): lax.ppermute(block, AXES, [(flat(moved(p, stage, by)), flat(p)) for p in...  14 us
    ppermute x9, starting transfers between devices, send(): lax.ppermute(block, AXES, [(flat(p), flat(moved(p, stage, by))) for p in...  13.8 us
    unnamed x9, local copies, waits for them, and re-layouts  6.75 us
    ppermute x5, waiting for transfers between devices, swap(): lax.ppermute(block, AXES, [(flat(p), flat(p[:3] + (1 - p[3],))) for p in...  5.6 us
  transfers between devices with their start and end apart: 23, of which 16 were waited for; matrix products, arithmetic and copies ran while one was open for 0% of the time, Pallas kernels for 0%

profile of v1, /device:TPU:0, one launch (start us, length us, event | category | flops | bytes accessed | tf_op | source)
XLA Modules:
  0.0 107.8 jit_solution(10799622353544971336)
XLA Ops:
  2.3 3.2 %collective-permute-start.2 = (bf16[2,7296]{1,0:T(2,128)(2,1)S(1)}, bf16[2,7296]{1,0:T(2,128)(2,1)S(1)}, u32[]{:S(2)}, u32[]{:S(2)}) collective-permute-start(bf16[2,7296]{1,0:T(2,128)(2,1)S(1)} %maximum_bitcast_fusion), channel_id=1, source_target_pairs={{4,0},{65,1},{6,2},{67,3},{0,4},{69,5},{2,6},{71,7},{12,8},{73,9},... | collective-permute-start | bytes 87560 | tf_op jit(solution)/shard_map/ppermute | solution.py:31
  6.1 2.6 %collective-permute-start = (bf16[2,7296]{1,0:T(2,128)(2,1)S(1)}, bf16[2,7296]{1,0:T(2,128)(2,1)S(1)}, u32[]{:S(2)}, u32[]{:S(2)}) collective-permute-start(bf16[2,7296]{1,0:T(2,128)(2,1)S(1)} %maximum_bitcast_fusion), channel_id=1, source_target_pairs={{2,0},{33,1},{4,2},{35,3},{6,4},{37,5},{0,6},{39,7},{10,8},{41,9},... | collective-permute-start | bytes 87560 | tf_op jit(solution)/shard_map/ppermute | solution.py:31
  8.8 1.8 %collective-permute-done.1 = bf16[2,7296]{1,0:T(2,128)(2,1)S(1)} collective-permute-done((bf16[2,7296]{1,0:T(2,128)(2,1)S(1)}, bf16[2,7296]{1,0:T(2,128)(2,1)S(1)}, u32[]{:S(2)}, u32[]{:S(2)}) %collective-permute-start.1) | collective-permute-done | bytes 29216 | tf_op jit(solution)/shard_map/ppermute | solution.py:31
  10.8 3.3 %collective-permute-start.5 = (bf16[8,7296]{1,0:T(8,128)(2,1)S(1)}, bf16[8,7296]{1,0:T(8,128)(2,1)S(1)}, u32[]{:S(2)}, u32[]{:S(2)}) collective-permute-start(bf16[8,7296]{1,0:T(8,128)(2,1)S(1)} %pad_maximum_fusion), channel_id=1, source_target_pairs={{16,0},{17,1},{18,2},{19,3},{20,4},{21,5},{22,6},{23,7},{24,8},{25... | collective-permute-start | bytes 350216 | tf_op jit(solution)/shard_map/ppermute | solution.py:31
  14.7 2.6 %collective-permute-start.3 = (bf16[8,7296]{1,0:T(8,128)(2,1)S(1)}, bf16[8,7296]{1,0:T(8,128)(2,1)S(1)}, u32[]{:S(2)}, u32[]{:S(2)}) collective-permute-start(bf16[8,7296]{1,0:T(8,128)(2,1)S(1)} %pad_maximum_fusion), channel_id=1, source_target_pairs={{8,0},{9,1},{10,2},{11,3},{12,4},{13,5},{14,6},{15,7},{16,8},{17,9... | collective-permute-start | bytes 350216 | tf_op jit(solution)/shard_map/ppermute | solution.py:31
  17.3 0.9 collective-permute-done.5
  18.2 1.8 %collective-permute-done.4 = bf16[8,7296]{1,0:T(8,128)(2,1)S(1)} collective-permute-done((bf16[8,7296]{1,0:T(8,128)(2,1)S(1)}, bf16[8,7296]{1,0:T(8,128)(2,1)S(1)}, u32[]{:S(2)}, u32[]{:S(2)}) %collective-permute-start.4) | collective-permute-done | bytes 116768 | tf_op jit(solution)/shard_map/ppermute | solution.py:31
  20.3 4.0 %collective-permute-start.8 = (bf16[32,7296]{1,0:T(8,128)(2,1)S(1)}, bf16[32,7296]{1,0:T(8,128)(2,1)S(1)}, u32[]{:S(2)}, u32[]{:S(2)}) collective-permute-start(bf16[32,7296]{1,0:T(8,128)(2,1)S(1)} %concatenate.13.refs_0_.refs_8_), channel_id=1, source_target_pairs={{64,0},{5,1},{66,2},{7,3},{68,4},{1,5},{70,6},{3,7},{72,8},{13,9},... | collective-permute-start | bytes 1400840 | tf_op jit(solution)/shard_map/ppermute | solution.py:31
  24.3 1.0 collective-permute-start.7
  25.3 2.2 %collective-permute-start.6 = (bf16[32,7296]{1,0:T(8,128)(2,1)S(1)}, bf16[32,7296]{1,0:T(8,128)(2,1)S(1)}, u32[]{:S(2)}, u32[]{:S(2)}) collective-permute-start(bf16[32,7296]{1,0:T(8,128)(2,1)S(1)} %concatenate.13.refs_0_.refs_8_), channel_id=1, source_target_pairs={{32,0},{3,1},{34,2},{5,3},{36,4},{7,5},{38,6},{1,7},{40,8},{11,9},... | collective-permute-start | bytes 1400840 | tf_op jit(solution)/shard_map/ppermute | solution.py:31
  27.5 3.4 %collective-permute-done.8.refs_3_.refs_11_ = bf16[32,7296]{1,0:T(8,128)(2,1)S(1)} collective-permute-done((bf16[32,7296]{1,0:T(8,128)(2,1)S(1)}, bf16[32,7296]{1,0:T(8,128)(2,1)S(1)}, u32[]{:S(2)}, u32[]{:S(2)}) %collective-permute-start.8) | collective-permute-done | bytes 466976 | tf_op jit(solution)/shard_map/ppermute | solution.py:31
  30.9 4.9 %collective-permute-done.7.refs_2_.refs_10_ = bf16[32,7296]{1,0:T(8,128)(2,1)S(1)} collective-permute-done((bf16[32,7296]{1,0:T(8,128)(2,1)S(1)}, bf16[32,7296]{1,0:T(8,128)(2,1)S(1)}, u32[]{:S(2)}, u32[]{:S(2)}) %collective-permute-start.7) | collective-permute-done | bytes 466976 | tf_op jit(solution)/shard_map/ppermute | solution.py:31
  35.8 1.1 collective-permute-done.6.refs_1_.refs_9_
  37.6 1.2 %collective-permute-done.10.refs_5_.refs_13_ = bf16[32,7296]{1,0:T(8,128)(2,1)} collective-permute-done((bf16[32,7296]{1,0:T(8,128)(2,1)S(1)}, bf16[32,7296]{1,0:T(8,128)(2,1)}, u32[]{:S(2)}, u32[]{:S(2)}) %collective-permute-start.10) | collective-permute-done | bytes 466976 | tf_op jit(solution)/shard_map/ppermute | solution.py:39
  38.8 3.1 %copy-done = bf16[2,7168,256]{2,1,0:T(8,128)(2,1)S(1)} copy-done((bf16[2,7168,256]{2,1,0:T(8,128)(2,1)S(1)}, bf16[2,7168,256]{2,1,0:T(8,128)(2,1)}, u32[]{:S(2)}) %copy-start) | copy-done | bytes 7340056
  41.9 0.9 copy-done.1
  42.8 0.9 copy-done.2
  43.8 0.9 copy-done.3
  44.7 19.0 %layer.1 = (f32[128,7168]{1,0:T(8,128)S(1)}, bf16[128,7168]{1,0:T(8,128)(2,1)S(1)}) custom-call(s32[1,1]{1,0:T(1,128)} %bitcast.first_ref, bf16[32,7296]{1,0:T(8,128)(2,1)S(1)} %concatenate.13.refs_0_.refs_8_, bf16[32,7296]{1,0:T(8,128)(2,1)S(1)} %collective-permute-done.6.refs_1_.refs_9_, bf16[32,7296]{1,0:T(8,128)(2,1)S(1)} %collective-permute-done.7.refs_2_.refs_10_, ...), custom_call_target="tpu_custom_call" | custom-call | flops 5813305344 | bytes 31883264 | tf_op jit(solution)/shard_map/layer/pallas_call | solution.py:98
  63.9 3.7 %collective-permute-done.13 = bf16[128,7168]{1,0:T(8,128)(2,1)S(1)} collective-permute-done((bf16[128,7168]{1,0:T(8,128)(2,1)S(1)}, bf16[128,7168]{1,0:T(8,128)(2,1)S(1)}, u32[]{:S(2)}, u32[]{:S(2)}) %collective-permute-start.13) | collective-permute-done | bytes 1835040 | tf_op jit(solution)/shard_map/ppermute | solution.py:39
  68.3 1.7 %collective-permute-start.14 = (bf16[32,7168]{1,0:T(8,128)(2,1)S(1)}, bf16[32,7168]{1,0:T(8,128)(2,1)S(1)}, u32[]{:S(2)}, u32[]{:S(2)}) collective-permute-start(bf16[32,7168]{1,0:T(8,128)(2,1)S(1)} %get-tuple-element.11), channel_id=1, source_target_pairs={{0,32},{1,3},{2,34},{3,5},{4,36},{5,7},{6,38},{7,1},{8,40},{9,11},... | collective-permute-start | bytes 1376264 | tf_op jit(solution)/shard_map/ppermute | solution.py:35
  70.0 2.4 %collective-permute-start.16 = (bf16[32,7168]{1,0:T(8,128)(2,1)S(1)}, bf16[32,7168]{1,0:T(8,128)(2,1)S(1)}, u32[]{:S(2)}, u32[]{:S(2)}) collective-permute-start(bf16[32,7168]{1,0:T(8,128)(2,1)S(1)} %get-tuple-element.12), channel_id=1, source_target_pairs={{0,64},{1,5},{2,66},{3,7},{4,68},{5,1},{6,70},{7,3},{8,72},{9,13},... | collective-permute-start | bytes 1376264 | tf_op jit(solution)/shard_map/ppermute | solution.py:35
  72.4 1.2 %collective-permute-start.15 = (bf16[32,7168]{1,0:T(8,128)(2,1)S(1)}, bf16[32,7168]{1,0:T(8,128)(2,1)S(1)}, u32[]{:S(2)}, u32[]{:S(2)}) collective-permute-start(bf16[32,7168]{1,0:T(8,128)(2,1)S(1)} %get-tuple-element.13), channel_id=1, source_target_pairs={{0,96},{1,7},{2,98},{3,1},{4,100},{5,3},{6,102},{7,5},{8,104},{9,1... | collective-permute-start | bytes 1376264 | tf_op jit(solution)/shard_map/ppermute | solution.py:35
  73.7 4.4 %collective-permute-done.14 = bf16[32,7168]{1,0:T(8,128)(2,1)S(1)} collective-permute-done((bf16[32,7168]{1,0:T(8,128)(2,1)S(1)}, bf16[32,7168]{1,0:T(8,128)(2,1)S(1)}, u32[]{:S(2)}, u32[]{:S(2)}) %collective-permute-start.14) | collective-permute-done | bytes 458784 | tf_op jit(solution)/shard_map/ppermute | solution.py:35
  78.0 5.8 %collective-permute-done.16 = bf16[32,7168]{1,0:T(8,128)(2,1)S(1)} collective-permute-done((bf16[32,7168]{1,0:T(8,128)(2,1)S(1)}, bf16[32,7168]{1,0:T(8,128)(2,1)S(1)}, u32[]{:S(2)}, u32[]{:S(2)}) %collective-permute-start.16) | collective-permute-done | bytes 458784 | tf_op jit(solution)/shard_map/ppermute | solution.py:35
  84.4 4.4 %collective-permute-start.19 = (f32[8,7168]{1,0:T(8,128)S(1)}, f32[8,7168]{1,0:T(8,128)S(1)}, u32[]{:S(2)}, u32[]{:S(2)}) collective-permute-start(f32[8,7168]{1,0:T(8,128)S(1)} %get-tuple-element.15), channel_id=1, source_target_pairs={{0,16},{1,17},{2,18},{3,19},{4,20},{5,21},{6,22},{7,23},{8,24},{9,... | collective-permute-start | bytes 688136 | tf_op jit(solution)/shard_map/ppermute | solution.py:35
  88.8 4.1 %collective-permute-done.17 = f32[8,7168]{1,0:T(8,128)S(1)} collective-permute-done((f32[8,7168]{1,0:T(8,128)S(1)}, f32[8,7168]{1,0:T(8,128)S(1)}, u32[]{:S(2)}, u32[]{:S(2)}) %collective-permute-start.17) | collective-permute-done | bytes 229408 | tf_op jit(solution)/shard_map/ppermute | solution.py:35
  93.0 6.1 %collective-permute-done.19 = f32[8,7168]{1,0:T(8,128)S(1)} collective-permute-done((f32[8,7168]{1,0:T(8,128)S(1)}, f32[8,7168]{1,0:T(8,128)S(1)}, u32[]{:S(2)}, u32[]{:S(2)}) %collective-permute-start.19) | collective-permute-done | bytes 229408 | tf_op jit(solution)/shard_map/ppermute | solution.py:35
  99.3 3.6 %collective-permute-start.22 = (f32[2,7168]{1,0:T(2,128)S(1)}, f32[2,7168]{1,0:T(2,128)S(1)}, u32[]{:S(2)}, u32[]{:S(2)}) collective-permute-start(f32[2,7168]{1,0:T(2,128)S(1)} %get-tuple-element.18), channel_id=1, source_target_pairs={{0,4},{1,65},{2,6},{3,67},{4,0},{5,69},{6,2},{7,71},{8,12},{9,73},... | collective-permute-start | bytes 172040 | tf_op jit(solution)/shard_map/ppermute | solution.py:35
  102.9 1.8 %collective-permute-done.20 = f32[2,7168]{1,0:T(2,128)S(1)} collective-permute-done((f32[2,7168]{1,0:T(2,128)S(1)}, f32[2,7168]{1,0:T(2,128)S(1)}, u32[]{:S(2)}, u32[]{:S(2)}) %collective-permute-start.20) | collective-permute-done | bytes 57376 | tf_op jit(solution)/shard_map/ppermute | solution.py:35
  104.7 1.0 collective-permute-done.22
  105.7 1.4 %collective-permute-done.21 = f32[2,7168]{1,0:T(2,128)S(1)} collective-permute-done((f32[2,7168]{1,0:T(2,128)S(1)}, f32[2,7168]{1,0:T(2,128)S(1)}, u32[]{:S(2)}, u32[]{:S(2)}) %collective-permute-start.21) | collective-permute-done | bytes 57376 | tf_op jit(solution)/shard_map/ppermute | solution.py:35
  (37 shorter events, 7.2 us)
Async XLA Ops:
  2.3 6.4 %collective-permute-start.2 = (bf16[2,7296]{1,0:T(2,128)(2,1)S(1)}, bf16[2,7296]{1,0:T(2,128)(2,1)S(1)}, u32[]{:S(2)}, u32[]{:S(2)}) collective-permute-start(bf16[2,7296]{1,0:T(2,128)(2,1)S(1)} %maximum_bitcast_fusion), channel_id=1, source_target_pairs={{4,0},{65,1},{6,2},{67,3},{0,4},{69,5},{2,6},{71,7},{12,8},{73,9},... | collective-permute-start | bytes 87560 | tf_op jit(solution)/shard_map/ppermute | solution.py:31
  5.5 5.1 %collective-permute-start.1 = (bf16[2,7296]{1,0:T(2,128)(2,1)S(1)}, bf16[2,7296]{1,0:T(2,128)(2,1)S(1)}, u32[]{:S(2)}, u32[]{:S(2)}) collective-permute-start(bf16[2,7296]{1,0:T(2,128)(2,1)S(1)} %maximum_bitcast_fusion), channel_id=1, source_target_pairs={{6,0},{97,1},{0,2},{99,3},{2,4},{101,5},{4,6},{103,7},{14,8},{105,... | collective-permute-start | bytes 87560 | tf_op jit(solution)/shard_map/ppermute | solution.py:31
  6.1 4.5 %collective-permute-start = (bf16[2,7296]{1,0:T(2,128)(2,1)S(1)}, bf16[2,7296]{1,0:T(2,128)(2,1)S(1)}, u32[]{:S(2)}, u32[]{:S(2)}) collective-permute-start(bf16[2,7296]{1,0:T(2,128)(2,1)S(1)} %maximum_bitcast_fusion), channel_id=1, source_target_pairs={{2,0},{33,1},{4,2},{35,3},{6,4},{37,5},{0,6},{39,7},{10,8},{41,9},... | collective-permute-start | bytes 87560 | tf_op jit(solution)/shard_map/ppermute | solution.py:31
  10.8 7.5 %collective-permute-start.5 = (bf16[8,7296]{1,0:T(8,128)(2,1)S(1)}, bf16[8,7296]{1,0:T(8,128)(2,1)S(1)}, u32[]{:S(2)}, u32[]{:S(2)}) collective-permute-start(bf16[8,7296]{1,0:T(8,128)(2,1)S(1)} %pad_maximum_fusion), channel_id=1, source_target_pairs={{16,0},{17,1},{18,2},{19,3},{20,4},{21,5},{22,6},{23,7},{24,8},{25... | collective-permute-start | bytes 350216 | tf_op jit(solution)/shard_map/ppermute | solution.py:31
  14.0 6.0 %collective-permute-start.4 = (bf16[8,7296]{1,0:T(8,128)(2,1)S(1)}, bf16[8,7296]{1,0:T(8,128)(2,1)S(1)}, u32[]{:S(2)}, u32[]{:S(2)}) collective-permute-start(bf16[8,7296]{1,0:T(8,128)(2,1)S(1)} %pad_maximum_fusion), channel_id=1, source_target_pairs={{24,0},{25,1},{26,2},{27,3},{28,4},{29,5},{30,6},{31,7},{0,8},{1,9... | collective-permute-start | bytes 350216 | tf_op jit(solution)/shard_map/ppermute | solution.py:31
  14.7 5.3 %collective-permute-start.3 = (bf16[8,7296]{1,0:T(8,128)(2,1)S(1)}, bf16[8,7296]{1,0:T(8,128)(2,1)S(1)}, u32[]{:S(2)}, u32[]{:S(2)}) collective-permute-start(bf16[8,7296]{1,0:T(8,128)(2,1)S(1)} %pad_maximum_fusion), channel_id=1, source_target_pairs={{8,0},{9,1},{10,2},{11,3},{12,4},{13,5},{14,6},{15,7},{16,8},{17,9... | collective-permute-start | bytes 350216 | tf_op jit(solution)/shard_map/ppermute | solution.py:31
  20.3 10.6 %collective-permute-start.8 = (bf16[32,7296]{1,0:T(8,128)(2,1)S(1)}, bf16[32,7296]{1,0:T(8,128)(2,1)S(1)}, u32[]{:S(2)}, u32[]{:S(2)}) collective-permute-start(bf16[32,7296]{1,0:T(8,128)(2,1)S(1)} %concatenate.13.refs_0_.refs_8_), channel_id=1, source_target_pairs={{64,0},{5,1},{66,2},{7,3},{68,4},{1,5},{70,6},{3,7},{72,8},{13,9},... | collective-permute-start | bytes 1400840 | tf_op jit(solution)/shard_map/ppermute | solution.py:31
  24.3 11.5 %collective-permute-start.7 = (bf16[32,7296]{1,0:T(8,128)(2,1)S(1)}, bf16[32,7296]{1,0:T(8,128)(2,1)S(1)}, u32[]{:S(2)}, u32[]{:S(2)}) collective-permute-start(bf16[32,7296]{1,0:T(8,128)(2,1)S(1)} %concatenate.13.refs_0_.refs_8_), channel_id=1, source_target_pairs={{96,0},{7,1},{98,2},{1,3},{100,4},{3,5},{102,6},{5,7},{104,8},{15,... | collective-permute-start | bytes 1400840 | tf_op jit(solution)/shard_map/ppermute | solution.py:31
  25.3 11.6 %collective-permute-start.6 = (bf16[32,7296]{1,0:T(8,128)(2,1)S(1)}, bf16[32,7296]{1,0:T(8,128)(2,1)S(1)}, u32[]{:S(2)}, u32[]{:S(2)}) collective-permute-start(bf16[32,7296]{1,0:T(8,128)(2,1)S(1)} %concatenate.13.refs_0_.refs_8_), channel_id=1, source_target_pairs={{32,0},{3,1},{34,2},{5,3},{36,4},{7,5},{38,6},{1,7},{40,8},{11,9},... | collective-permute-start | bytes 1400840 | tf_op jit(solution)/shard_map/ppermute | solution.py:31
  27.5 9.4 %collective-permute-start.9 = (bf16[32,7296]{1,0:T(8,128)(2,1)S(1)}, bf16[32,7296]{1,0:T(8,128)(2,1)S(1)}, u32[]{:S(2)}, u32[]{:S(2)}) collective-permute-start(bf16[32,7296]{1,0:T(8,128)(2,1)S(1)} %concatenate.13.refs_0_.refs_8_), channel_id=1, source_target_pairs={{0,1},{1,0},{2,3},{3,2},{4,5},{5,4},{6,7},{7,6},{8,9},{9,8},{10,11... | collective-permute-start | bytes 1400840 | tf_op jit(solution)/shard_map/ppermute | solution.py:39
  30.9 6.0 %collective-permute-start.12 = (bf16[32,7296]{1,0:T(8,128)(2,1)S(1)}, bf16[32,7296]{1,0:T(8,128)(2,1)S(1)}, u32[]{:S(2)}, u32[]{:S(2)}) collective-permute-start(bf16[32,7296]{1,0:T(8,128)(2,1)S(1)} %collective-permute-done.8.refs_3_.refs_11_), channel_id=1, source_target_pairs={{0,1},{1,0},{2,3},{3,2},{4,5},{5,4},{6,7},{7,6},{8,9},{9,8},{10,11... | collective-permute-start | bytes 1400840 | tf_op jit(solution)/shard_map/ppermute | solution.py:39
  35.8 1.8 %collective-permute-start.11 = (bf16[32,7296]{1,0:T(8,128)(2,1)S(1)}, bf16[32,7296]{1,0:T(8,128)(2,1)S(1)}, u32[]{:S(2)}, u32[]{:S(2)}) collective-permute-start(bf16[32,7296]{1,0:T(8,128)(2,1)S(1)} %collective-permute-done.7.refs_2_.refs_10_), channel_id=1, source_target_pairs={{0,1},{1,0},{2,3},{3,2},{4,5},{5,4},{6,7},{7,6},{8,9},{9,8},{10,11... | collective-permute-start | bytes 1400840 | tf_op jit(solution)/shard_map/ppermute | solution.py:39
  36.9 2.0 %collective-permute-start.10 = (bf16[32,7296]{1,0:T(8,128)(2,1)S(1)}, bf16[32,7296]{1,0:T(8,128)(2,1)}, u32[]{:S(2)}, u32[]{:S(2)}) collective-permute-start(bf16[32,7296]{1,0:T(8,128)(2,1)S(1)} %collective-permute-done.6.refs_1_.refs_9_), channel_id=1, source_target_pairs={{0,1},{1,0},{2,3},{3,2},{4,5},{5,4},{6,7},{7,6},{8,9},{9,8},{10,11... | collective-permute-start | bytes 1400840 | tf_op jit(solution)/shard_map/ppermute | solution.py:39
  38.8 3.1 %copy-start = (bf16[2,7168,256]{2,1,0:T(8,128)(2,1)S(1)}, bf16[2,7168,256]{2,1,0:T(8,128)(2,1)}, u32[]{:S(2)}) copy-start(bf16[2,7168,256]{2,1,0:T(8,128)(2,1)} %refs_16_.1) | copy-start | bytes 22020100
  41.9 0.9 copy-start.1
  42.8 0.9 copy-start.2
  43.8 0.9 copy-start.3
  63.7 3.9 %collective-permute-start.13 = (bf16[128,7168]{1,0:T(8,128)(2,1)S(1)}, bf16[128,7168]{1,0:T(8,128)(2,1)S(1)}, u32[]{:S(2)}, u32[]{:S(2)}) collective-permute-start(bf16[128,7168]{1,0:T(8,128)(2,1)S(1)} %get-tuple-element.8), channel_id=1, source_target_pairs={{0,1},{1,0},{2,3},{3,2},{4,5},{5,4},{6,7},{7,6},{8,9},{9,8},{10,11... | collective-permute-start | bytes 5505032 | tf_op jit(solution)/shard_map/ppermute | solution.py:39
  68.3 9.8 %collective-permute-start.14 = (bf16[32,7168]{1,0:T(8,128)(2,1)S(1)}, bf16[32,7168]{1,0:T(8,128)(2,1)S(1)}, u32[]{:S(2)}, u32[]{:S(2)}) collective-permute-start(bf16[32,7168]{1,0:T(8,128)(2,1)S(1)} %get-tuple-element.11), channel_id=1, source_target_pairs={{0,32},{1,3},{2,34},{3,5},{4,36},{5,7},{6,38},{7,1},{8,40},{9,11},... | collective-permute-start | bytes 1376264 | tf_op jit(solution)/shard_map/ppermute | solution.py:35
  70.0 13.8 %collective-permute-start.16 = (bf16[32,7168]{1,0:T(8,128)(2,1)S(1)}, bf16[32,7168]{1,0:T(8,128)(2,1)S(1)}, u32[]{:S(2)}, u32[]{:S(2)}) collective-permute-start(bf16[32,7168]{1,0:T(8,128)(2,1)S(1)} %get-tuple-element.12), channel_id=1, source_target_pairs={{0,64},{1,5},{2,66},{3,7},{4,68},{5,1},{6,70},{7,3},{8,72},{9,13},... | collective-permute-start | bytes 1376264 | tf_op jit(solution)/shard_map/ppermute | solution.py:35
  72.4 11.4 %collective-permute-start.15 = (bf16[32,7168]{1,0:T(8,128)(2,1)S(1)}, bf16[32,7168]{1,0:T(8,128)(2,1)S(1)}, u32[]{:S(2)}, u32[]{:S(2)}) collective-permute-start(bf16[32,7168]{1,0:T(8,128)(2,1)S(1)} %get-tuple-element.13), channel_id=1, source_target_pairs={{0,96},{1,7},{2,98},{3,1},{4,100},{5,3},{6,102},{7,5},{8,104},{9,1... | collective-permute-start | bytes 1376264 | tf_op jit(solution)/shard_map/ppermute | solution.py:35
  84.1 8.9 %collective-permute-start.17 = (f32[8,7168]{1,0:T(8,128)S(1)}, f32[8,7168]{1,0:T(8,128)S(1)}, u32[]{:S(2)}, u32[]{:S(2)}) collective-permute-start(f32[8,7168]{1,0:T(8,128)S(1)} %get-tuple-element.14), channel_id=1, source_target_pairs={{0,8},{1,9},{2,10},{3,11},{4,12},{5,13},{6,14},{7,15},{8,16},{9,17... | collective-permute-start | bytes 688136 | tf_op jit(solution)/shard_map/ppermute | solution.py:35
  84.4 14.7 %collective-permute-start.19 = (f32[8,7168]{1,0:T(8,128)S(1)}, f32[8,7168]{1,0:T(8,128)S(1)}, u32[]{:S(2)}, u32[]{:S(2)}) collective-permute-start(f32[8,7168]{1,0:T(8,128)S(1)} %get-tuple-element.15), channel_id=1, source_target_pairs={{0,16},{1,17},{2,18},{3,19},{4,20},{5,21},{6,22},{7,23},{8,24},{9,... | collective-permute-start | bytes 688136 | tf_op jit(solution)/shard_map/ppermute | solution.py:35
  88.8 10.2 %collective-permute-start.18 = (f32[8,7168]{1,0:T(8,128)S(1)}, f32[8,7168]{1,0:T(8,128)S(1)}, u32[]{:S(2)}, u32[]{:S(2)}) collective-permute-start(f32[8,7168]{1,0:T(8,128)S(1)} %get-tuple-element.16), channel_id=1, source_target_pairs={{0,24},{1,25},{2,26},{3,27},{4,28},{5,29},{6,30},{7,31},{8,0},{9,1... | collective-permute-start | bytes 688136 | tf_op jit(solution)/shard_map/ppermute | solution.py:35
  99.2 5.5 %collective-permute-start.20 = (f32[2,7168]{1,0:T(2,128)S(1)}, f32[2,7168]{1,0:T(2,128)S(1)}, u32[]{:S(2)}, u32[]{:S(2)}) collective-permute-start(f32[2,7168]{1,0:T(2,128)S(1)} %get-tuple-element.17), channel_id=1, source_target_pairs={{0,2},{1,33},{2,4},{3,35},{4,6},{5,37},{6,0},{7,39},{8,10},{9,41},... | collective-permute-start | bytes 172040 | tf_op jit(solution)/shard_map/ppermute | solution.py:35
  99.3 6.4 %collective-permute-start.22 = (f32[2,7168]{1,0:T(2,128)S(1)}, f32[2,7168]{1,0:T(2,128)S(1)}, u32[]{:S(2)}, u32[]{:S(2)}) collective-permute-start(f32[2,7168]{1,0:T(2,128)S(1)} %get-tuple-element.18), channel_id=1, source_target_pairs={{0,4},{1,65},{2,6},{3,67},{4,0},{5,69},{6,2},{7,71},{8,12},{9,73},... | collective-permute-start | bytes 172040 | tf_op jit(solution)/shard_map/ppermute | solution.py:35
  102.9 4.2 %collective-permute-start.21 = (f32[2,7168]{1,0:T(2,128)S(1)}, f32[2,7168]{1,0:T(2,128)S(1)}, u32[]{:S(2)}, u32[]{:S(2)}) collective-permute-start(f32[2,7168]{1,0:T(2,128)S(1)} %get-tuple-element.19), channel_id=1, source_target_pairs={{0,6},{1,97},{2,0},{3,99},{4,2},{5,101},{6,4},{7,103},{8,14},{9,10... | collective-permute-start | bytes 172040 | tf_op jit(solution)/shard_map/ppermute | solution.py:35

commit v2 on v1

v2 whole, which is shorter than its diff:
```python
import jax
import jax.numpy as jnp
from jax import lax
from jax.experimental import pallas as pl
from jax.experimental.pallas import tpu as pltpu
from jax.sharding import PartitionSpec as P

AXES = ("group", "local")
SIZE = (4, 4, 4, 2)
ORDER = ((2, 1, 0), (1, 0, 2))
META = 128


def flat(place):
    index = 0
    for size, at in zip(SIZE, place):
        index = index * size + at
    return index


def places():
    return [(z, y, x, c) for z in range(4) for y in range(4) for x in range(4) for c in range(2)]


def moved(place, stage, by):
    axis = ORDER[place[3]][stage]
    return tuple((at + by) % 4 if dim == axis else at for dim, at in enumerate(place))


def fetch(block, stage, by):
    return lax.ppermute(block, AXES, [(flat(moved(p, stage, by)), flat(p)) for p in places()])


def send(block, stage, by):
    return lax.ppermute(block, AXES, [(flat(p), flat(moved(p, stage, by))) for p in places()])


def swap(block):
    return lax.ppermute(block, AXES, [(flat(p), flat(p[:3] + (1 - p[3],))) for p in places()])


KSTEP = 3584
NSTEP = 1792
AHEAD = 4


def layer_kernel(first_ref, *refs):
    pieces = refs[:8]
    gate, up, shared_gate, shared_up, down, shared_down = refs[8:14]
    own, other = refs[14:16]
    gate_buf, up_buf, down_buf, sgu_buf, sd_buf, acts, hid, shared_hid, scale, sems = refs[16:]
    width = shared_down.shape[1]
    shared = shared_down.shape[0]
    steps = width // KSTEP
    cuts = width // NSTEP

    loads = []
    for e in range(2):
        for source, target in ((gate, gate_buf), (up, up_buf)):
            for k in range(steps):
                rows = pl.ds(k * KSTEP, KSTEP)
                loads.append((source.at[e, rows], target.at[e, rows]))
        if e == 0:
            loads.append((shared_gate, sgu_buf.at[:shared]))
            loads.append((shared_up, sgu_buf.at[shared:]))
            loads.append((shared_down, sd_buf))
    for n in range(cuts):
        columns = pl.ds(n * NSTEP, NSTEP)
        loads.append((down.at[:, :, columns], down_buf.at[:, :, columns]))
    copies = [pltpu.make_async_copy(s, t, sems.at[i]) for i, (s, t) in enumerate(loads)]
    for copy in copies[:AHEAD]:
        copy.start()
    waited = [0]

    def arrived():
        copies[waited[0]].wait()
        if waited[0] + AHEAD < len(copies):
            copies[waited[0] + AHEAD].start()
        waited[0] += 1

    def rows_of(k, size):
        return jnp.concatenate([p[:, k * size : (k + 1) * size] for p in pieces], axis=0)

    def silu_mul(g, u):
        return (g / (1.0 + jnp.exp(-g)) * u).astype(jnp.bfloat16)

    block = pl.when(first_ref[0, 0] >= 0)

    @block
    def _():
        weights = jnp.concatenate([p[:, width:] for p in pieces], axis=0).astype(jnp.float32)
        lane = lax.broadcasted_iota(jnp.int32, weights.shape, 1)
        for e in range(2):
            mine = jnp.where(lane == first_ref[0, 0] + e, weights, 0.0)
            scale[e] = jnp.broadcast_to(jnp.sum(mine, axis=1, keepdims=True), weights.shape)

    for e in range(2):
        for m, buf in enumerate((gate_buf, up_buf)):
            for k in range(steps):
                arrived()

                @block
                def _(e=e, m=m, k=k, buf=buf):
                    part = jnp.dot(
                        rows_of(k, KSTEP),
                        buf[e, k * KSTEP : (k + 1) * KSTEP],
                        preferred_element_type=jnp.float32,
                    )
                    acts[m] = part if k == 0 else acts[m] + part

        if e == 0:
            arrived()
            arrived()
            arrived()

        @block
        def _(e=e):
            hid[e] = silu_mul(acts[0], acts[1])
            if e == 0:
                dims = (((1,), (1,)), ((), ()))
                both = None
                for k in range(steps):
                    part = lax.dot_general(
                        rows_of(k, KSTEP),
                        sgu_buf[:, k * KSTEP : (k + 1) * KSTEP],
                        dims,
                        preferred_element_type=jnp.float32,
                    )
                    both = part if both is None else both + part
                shared_hid[...] = silu_mul(both[:, :shared], both[:, shared:])

    for n in range(cuts):
        arrived()

        @block
        def _(n=n):
            columns = slice(n * NSTEP, (n + 1) * NSTEP)
            total = jnp.dot(shared_hid[...], sd_buf[:, columns], preferred_element_type=jnp.float32)
            for e in range(2):
                part = jnp.dot(hid[e], down_buf[e, :, columns], preferred_element_type=jnp.float32)
                total = total + scale[e][:, :1] * part
            own[:, columns] = total[:128]
            other[:, columns] = total[128:].astype(jnp.bfloat16)


def layer(pieces, first, gate, up, down, shared_gate, shared_up, shared_down):
    width = down.shape[2]
    units = gate.shape[2]
    shared = shared_down.shape[0]
    vmem = pl.BlockSpec(memory_space=pltpu.VMEM)
    hbm = pl.BlockSpec(memory_space=pl.ANY)
    return pl.pallas_call(
        layer_kernel,
        out_shape=(
            jax.ShapeDtypeStruct((128, width), jnp.float32),
            jax.ShapeDtypeStruct((128, width), jnp.bfloat16),
        ),
        in_specs=[pl.BlockSpec(memory_space=pltpu.SMEM)]
        + [vmem] * 8
        + [hbm] * 6,
        out_specs=[vmem] * 2,
        scratch_shapes=[
            pltpu.VMEM(gate.shape, jnp.bfloat16),
            pltpu.VMEM(up.shape, jnp.bfloat16),
            pltpu.VMEM(down.shape, jnp.bfloat16),
            pltpu.VMEM((2 * shared, width), jnp.bfloat16),
            pltpu.VMEM((shared, width), jnp.bfloat16),
            pltpu.VMEM((2, 256, units), jnp.float32),
            pltpu.VMEM((2, 256, units), jnp.bfloat16),
            pltpu.VMEM((256, shared), jnp.bfloat16),
            pltpu.VMEM((2, 256, META), jnp.float32),
            pltpu.SemaphoreType.DMA((4 * width // KSTEP + 3 + width // NSTEP,)),
        ],
        compiler_params=pltpu.CompilerParams(vmem_limit_bytes=32 * 1024 * 1024),
        cost_estimate=pl.CostEstimate(
            flops=6 * 256 * width * (2 * units + shared),
            bytes_accessed=6 * width * (2 * units + shared) + 10 * 128 * width,
            transcendentals=256 * (2 * units + shared),
        ),
        name="layer",
    )(
        first,
        *pieces,
        *[
            pltpu.with_memory_space_constraint(a, pltpu.HBM)
            for a in (gate, up, shared_gate.T, shared_up.T, down, shared_down)
        ],
    )


def body(
    hidden,
    routes,
    slots,
    route_weight,
    expert_gate,
    expert_up,
    expert_down,
    shared_gate,
    shared_up,
    shared_down,
):
    experts = jnp.arange(META, dtype=jnp.int32)
    weight = jnp.where(slots >= 0, route_weight.astype(jnp.float32), 0.0)
    dense = jnp.sum(
        jnp.where(routes[..., None] == experts, weight[..., None], 0.0), axis=2
    )
    block = jnp.concatenate([hidden, dense], axis=2)[:, 0].astype(jnp.bfloat16)

    for stage in range(2):
        block = jnp.concatenate([block] + [fetch(block, stage, by) for by in (1, 3, 2)], axis=0)
    mine = [block] + [fetch(block, 2, by) for by in (1, 3, 2)]
    pieces = mine + [swap(piece) for piece in mine]

    first = (2 * lax.axis_index("group")).astype(jnp.int32).reshape(1, 1)
    own, other = layer(
        pieces, first, expert_gate, expert_up, expert_down, shared_gate, shared_up, shared_down
    )
    total = own + swap(other).astype(jnp.float32)
    for stage, kind in ((2, jnp.bfloat16), (1, jnp.bfloat16), (0, jnp.float32)):
        count = total.shape[0] // 4
        parts = [total[i * count : (i + 1) * count] for i in range(4)]
        got = [send(part.astype(kind), stage, by) for part, by in zip(parts[1:], (1, 3, 2))]
        total = parts[0]
        for part in got:
            total = total + part.astype(jnp.float32)
    return total[:, None, :]


def solution(mesh):
    return jax.shard_map(
        body,
        mesh=mesh,
        in_specs=(
            P(None, ("group", "local"), None),
            P(None, ("group", "local"), None),
            P(None, ("group", "local"), None),
            P(None, ("group", "local"), None),
            P("group", None, "local"),
            P("group", None, "local"),
            P("group", "local", None),
            P(None, ("group", "local")),
            P(None, ("group", "local")),
            P(("group", "local"), None),
        ),
        out_specs=P(None, ("group", "local"), None),
        check_vma=False,
    )
```

time: 108 us -> 91.6 us (0.85)
  Pallas kernels: 19 us -> 12.8 us
  local copies, waits for them, and re-layouts: 7.88 us -> 1.96 us
  waiting for transfers between devices: 44.2 us -> 38.7 us
  starting transfers between devices: 34.2 us -> 35.3 us
    pallas_call x1, Pallas kernels: 19 us -> 12.8 us  [layer(): pl.pallas_call(layer_kernel, out_shape=(jax.ShapeDtypeStruct((128, width)...]
    unnamed x9 -> x1, local copies, waits for them, and re-layouts: 6.75 us -> 0.85 us
    ppermute x9, waiting for transfers between devices: 24.6 us -> 19.1 us  [send(): lax.ppermute(block, AXES, [(flat(p), flat(moved(p, stage, by))) for p in...]
    ppermute x9, starting transfers between devices: 13.8 us -> 14.9 us  [send(): lax.ppermute(block, AXES, [(flat(p), flat(moved(p, stage, by))) for p in...]
where the time goes in v2:
time: 91.6 us; the launch traced here: 91.3 us
  waiting for transfers between devices  38.7 us (42%)
  starting transfers between devices  35.3 us (39%)
  Pallas kernels  12.8 us (14%)
  other arithmetic  2.44 us (3%)
  local copies, waits for them, and re-layouts  1.96 us (2%)
    ppermute x9, starting transfers between devices, fetch(): lax.ppermute(block, AXES, [(flat(moved(p, stage, by)), flat(p)) for p in...  20.1 us
    ppermute x9, waiting for transfers between devices, send(): lax.ppermute(block, AXES, [(flat(p), flat(moved(p, stage, by))) for p in...  19.1 us
    ppermute x9, starting transfers between devices, send(): lax.ppermute(block, AXES, [(flat(p), flat(moved(p, stage, by))) for p in...  14.9 us
    ppermute x9, waiting for transfers between devices, fetch(): lax.ppermute(block, AXES, [(flat(moved(p, stage, by)), flat(p)) for p in...  14 us
    pallas_call x1, Pallas kernels, layer(): pl.pallas_call(layer_kernel, out_shape=(jax.ShapeDtypeStruct((128, width)...  12.8 us
    ppermute x5, waiting for transfers between devices, swap(): lax.ppermute(block, AXES, [(flat(p), flat(p[:3] + (1 - p[3],))) for p in...  5.6 us
  transfers between devices with their start and end apart: 23, of which 16 were waited for; matrix products, arithmetic and copies ran while one was open for 0% of the time, Pallas kernels for 0%

profile of v2, /device:TPU:0, one launch (start us, length us, event | category | flops | bytes accessed | tf_op | source)
XLA Modules:
  0.0 91.3 jit_solution(7293306572627389345)
XLA Ops:
  0.0 0.8 copy.18
  0.9 0.7 fusion.7
  1.5 0.8 select_reduce_fusion
  2.3 3.2 %collective-permute-start.2 = (bf16[2,7296]{1,0:T(2,128)(2,1)S(1)}, bf16[2,7296]{1,0:T(2,128)(2,1)S(1)}, u32[]{:S(2)}, u32[]{:S(2)}) collective-permute-start(bf16[2,7296]{1,0:T(2,128)(2,1)S(1)} %maximum_bitcast_fusion), channel_id=1, source_target_pairs={{4,0},{17,1},{6,2},{19,3},{0,4},{21,5},{2,6},{23,7},{12,8},{25,9},... | collective-permute-start | bytes 87560 | tf_op jit(solution)/shard_map/ppermute | solution.py:31
  6.1 2.6 %collective-permute-start = (bf16[2,7296]{1,0:T(2,128)(2,1)S(1)}, bf16[2,7296]{1,0:T(2,128)(2,1)S(1)}, u32[]{:S(2)}, u32[]{:S(2)}) collective-permute-start(bf16[2,7296]{1,0:T(2,128)(2,1)S(1)} %maximum_bitcast_fusion), channel_id=1, source_target_pairs={{2,0},{9,1},{4,2},{11,3},{6,4},{13,5},{0,6},{15,7},{10,8},{17,9},{... | collective-permute-start | bytes 87560 | tf_op jit(solution)/shard_map/ppermute | solution.py:31
  8.8 1.8 %collective-permute-done.1 = bf16[2,7296]{1,0:T(2,128)(2,1)S(1)} collective-permute-done((bf16[2,7296]{1,0:T(2,128)(2,1)S(1)}, bf16[2,7296]{1,0:T(2,128)(2,1)S(1)}, u32[]{:S(2)}, u32[]{:S(2)}) %collective-permute-start.1) | collective-permute-done | bytes 29216 | tf_op jit(solution)/shard_map/ppermute | solution.py:31
  10.8 3.3 %collective-permute-start.5 = (bf16[8,7296]{1,0:T(8,128)(2,1)S(1)}, bf16[8,7296]{1,0:T(8,128)(2,1)S(1)}, u32[]{:S(2)}, u32[]{:S(2)}) collective-permute-start(bf16[8,7296]{1,0:T(8,128)(2,1)S(1)} %pad_maximum_fusion), channel_id=1, source_target_pairs={{16,0},{65,1},{18,2},{67,3},{20,4},{69,5},{22,6},{71,7},{24,8},{73... | collective-permute-start | bytes 350216 | tf_op jit(solution)/shard_map/ppermute | solution.py:31
  14.7 2.6 %collective-permute-start.3 = (bf16[8,7296]{1,0:T(8,128)(2,1)S(1)}, bf16[8,7296]{1,0:T(8,128)(2,1)S(1)}, u32[]{:S(2)}, u32[]{:S(2)}) collective-permute-start(bf16[8,7296]{1,0:T(8,128)(2,1)S(1)} %pad_maximum_fusion), channel_id=1, source_target_pairs={{8,0},{33,1},{10,2},{35,3},{12,4},{37,5},{14,6},{39,7},{16,8},{41,... | collective-permute-start | bytes 350216 | tf_op jit(solution)/shard_map/ppermute | solution.py:31
  17.3 2.8 %collective-permute-done.4 = bf16[8,7296]{1,0:T(8,128)(2,1)S(1)} collective-permute-done((bf16[8,7296]{1,0:T(8,128)(2,1)S(1)}, bf16[8,7296]{1,0:T(8,128)(2,1)S(1)}, u32[]{:S(2)}, u32[]{:S(2)}) %collective-permute-start.4) | collective-permute-done | bytes 116768 | tf_op jit(solution)/shard_map/ppermute | solution.py:31
  20.3 4.0 %collective-permute-start.8 = (bf16[32,7296]{1,0:T(8,128)(2,1)S(1)}, bf16[32,7296]{1,0:T(8,128)(2,1)S(1)}, u32[]{:S(2)}, u32[]{:S(2)}) collective-permute-start(bf16[32,7296]{1,0:T(8,128)(2,1)S(1)} %concatenate.13.refs_0_), channel_id=1, source_target_pairs={{64,0},{5,1},{66,2},{7,3},{68,4},{1,5},{70,6},{3,7},{72,8},{13,9},... | collective-permute-start | bytes 1400840 | tf_op jit(solution)/shard_map/ppermute | solution.py:31
  24.3 1.0 %collective-permute-start.7 = (bf16[32,7296]{1,0:T(8,128)(2,1)S(1)}, bf16[32,7296]{1,0:T(8,128)(2,1)S(1)}, u32[]{:S(2)}, u32[]{:S(2)}) collective-permute-start(bf16[32,7296]{1,0:T(8,128)(2,1)S(1)} %concatenate.13.refs_0_), channel_id=1, source_target_pairs={{96,0},{7,1},{98,2},{1,3},{100,4},{3,5},{102,6},{5,7},{104,8},{15,... | collective-permute-start | bytes 1400840 | tf_op jit(solution)/shard_map/ppermute | solution.py:31
  25.3 2.2 %collective-permute-start.6 = (bf16[32,7296]{1,0:T(8,128)(2,1)S(1)}, bf16[32,7296]{1,0:T(8,128)(2,1)S(1)}, u32[]{:S(2)}, u32[]{:S(2)}) collective-permute-start(bf16[32,7296]{1,0:T(8,128)(2,1)S(1)} %concatenate.13.refs_0_), channel_id=1, source_target_pairs={{32,0},{3,1},{34,2},{5,3},{36,4},{7,5},{38,6},{1,7},{40,8},{11,9},... | collective-permute-start | bytes 1400840 | tf_op jit(solution)/shard_map/ppermute | solution.py:31
  27.5 3.4 %collective-permute-done.8.refs_3_ = bf16[32,7296]{1,0:T(8,128)(2,1)S(1)} collective-permute-done((bf16[32,7296]{1,0:T(8,128)(2,1)S(1)}, bf16[32,7296]{1,0:T(8,128)(2,1)S(1)}, u32[]{:S(2)}, u32[]{:S(2)}) %collective-permute-start.8) | collective-permute-done | bytes 466976 | tf_op jit(solution)/shard_map/ppermute | solution.py:31
  30.9 4.9 %collective-permute-done.7.refs_2_ = bf16[32,7296]{1,0:T(8,128)(2,1)S(1)} collective-permute-done((bf16[32,7296]{1,0:T(8,128)(2,1)S(1)}, bf16[32,7296]{1,0:T(8,128)(2,1)S(1)}, u32[]{:S(2)}, u32[]{:S(2)}) %collective-permute-start.7) | collective-permute-done | bytes 466976 | tf_op jit(solution)/shard_map/ppermute | solution.py:31
  35.8 1.1 %collective-permute-done.6.refs_1_ = bf16[32,7296]{1,0:T(8,128)(2,1)S(1)} collective-permute-done((bf16[32,7296]{1,0:T(8,128)(2,1)S(1)}, bf16[32,7296]{1,0:T(8,128)(2,1)S(1)}, u32[]{:S(2)}, u32[]{:S(2)}) %collective-permute-start.6) | collective-permute-done | bytes 466976 | tf_op jit(solution)/shard_map/ppermute | solution.py:31
  36.9 0.8 collective-permute-done.11.refs_6_
  37.6 1.2 %collective-permute-done.10.refs_5_ = bf16[32,7296]{1,0:T(8,128)(2,1)} collective-permute-done((bf16[32,7296]{1,0:T(8,128)(2,1)S(1)}, bf16[32,7296]{1,0:T(8,128)(2,1)}, u32[]{:S(2)}, u32[]{:S(2)}) %collective-permute-start.10) | collective-permute-done | bytes 466976 | tf_op jit(solution)/shard_map/ppermute | solution.py:39
  38.8 12.8 %layer.1 = (f32[128,7168]{1,0:T(8,128)S(1)}, bf16[128,7168]{1,0:T(8,128)(2,1)S(1)}) custom-call(s32[1,1]{1,0:T(1,128)} %bitcast.first_ref, bf16[32,7296]{1,0:T(8,128)(2,1)S(1)} %concatenate.13.refs_0_, bf16[32,7296]{1,0:T(8,128)(2,1)S(1)} %collective-permute-done.6.refs_1_, bf16[32,7296]{1,0:T(8,128)(2,1)S(1)} %collective-permute-done.7.refs_2_, ...), custom_call_target="tpu_custom_call" | custom-call | flops 5813305344 | bytes 31883264 | tf_op jit(solution)/shard_map/layer/pallas_call | solution.py:152
  51.9 3.6 %collective-permute-done.13 = bf16[128,7168]{1,0:T(8,128)(2,1)S(1)} collective-permute-done((bf16[128,7168]{1,0:T(8,128)(2,1)S(1)}, bf16[128,7168]{1,0:T(8,128)(2,1)S(1)}, u32[]{:S(2)}, u32[]{:S(2)}) %collective-permute-start.13) | collective-permute-done | bytes 1835040 | tf_op jit(solution)/shard_map/ppermute | solution.py:39
  56.2 1.7 %collective-permute-start.14 = (bf16[32,7168]{1,0:T(8,128)(2,1)S(1)}, bf16[32,7168]{1,0:T(8,128)(2,1)S(1)}, u32[]{:S(2)}, u32[]{:S(2)}) collective-permute-start(bf16[32,7168]{1,0:T(8,128)(2,1)S(1)} %get-tuple-element.13), channel_id=1, source_target_pairs={{0,32},{1,3},{2,34},{3,5},{4,36},{5,7},{6,38},{7,1},{8,40},{9,11},... | collective-permute-start | bytes 1376264 | tf_op jit(solution)/shard_map/ppermute | solution.py:35
  57.9 2.4 %collective-permute-start.16 = (bf16[32,7168]{1,0:T(8,128)(2,1)S(1)}, bf16[32,7168]{1,0:T(8,128)(2,1)S(1)}, u32[]{:S(2)}, u32[]{:S(2)}) collective-permute-start(bf16[32,7168]{1,0:T(8,128)(2,1)S(1)} %get-tuple-element.14), channel_id=1, source_target_pairs={{0,64},{1,5},{2,66},{3,7},{4,68},{5,1},{6,70},{7,3},{8,72},{9,13},... | collective-permute-start | bytes 1376264 | tf_op jit(solution)/shard_map/ppermute | solution.py:35
  60.3 1.2 %collective-permute-start.15 = (bf16[32,7168]{1,0:T(8,128)(2,1)S(1)}, bf16[32,7168]{1,0:T(8,128)(2,1)S(1)}, u32[]{:S(2)}, u32[]{:S(2)}) collective-permute-start(bf16[32,7168]{1,0:T(8,128)(2,1)S(1)} %get-tuple-element.15), channel_id=1, source_target_pairs={{0,96},{1,7},{2,98},{3,1},{4,100},{5,3},{6,102},{7,5},{8,104},{9,1... | collective-permute-start | bytes 1376264 | tf_op jit(solution)/shard_map/ppermute | solution.py:35
  61.6 4.4 %collective-permute-done.14 = bf16[32,7168]{1,0:T(8,128)(2,1)S(1)} collective-permute-done((bf16[32,7168]{1,0:T(8,128)(2,1)S(1)}, bf16[32,7168]{1,0:T(8,128)(2,1)S(1)}, u32[]{:S(2)}, u32[]{:S(2)}) %collective-permute-start.14) | collective-permute-done | bytes 458784 | tf_op jit(solution)/shard_map/ppermute | solution.py:35
  65.9 5.8 %collective-permute-done.16 = bf16[32,7168]{1,0:T(8,128)(2,1)S(1)} collective-permute-done((bf16[32,7168]{1,0:T(8,128)(2,1)S(1)}, bf16[32,7168]{1,0:T(8,128)(2,1)S(1)}, u32[]{:S(2)}, u32[]{:S(2)}) %collective-permute-start.16) | collective-permute-done | bytes 458784 | tf_op jit(solution)/shard_map/ppermute | solution.py:35
  72.1 4.6 %collective-permute-start.19 = (bf16[8,7168]{1,0:T(8,128)(2,1)S(1)}, bf16[8,7168]{1,0:T(8,128)(2,1)S(1)}, u32[]{:S(2)}, u32[]{:S(2)}) collective-permute-start(bf16[8,7168]{1,0:T(8,128)(2,1)S(1)} %get-tuple-element.17), channel_id=1, source_target_pairs={{0,16},{1,65},{2,18},{3,67},{4,20},{5,69},{6,22},{7,71},{8,24},{9,... | collective-permute-start | bytes 344072 | tf_op jit(solution)/shard_map/ppermute | solution.py:35
  76.7 1.3 %collective-permute-done.17 = bf16[8,7168]{1,0:T(8,128)(2,1)S(1)} collective-permute-done((bf16[8,7168]{1,0:T(8,128)(2,1)S(1)}, bf16[8,7168]{1,0:T(8,128)(2,1)S(1)}, u32[]{:S(2)}, u32[]{:S(2)}) %collective-permute-start.17) | collective-permute-done | bytes 114720 | tf_op jit(solution)/shard_map/ppermute | solution.py:35
  78.0 2.7 %collective-permute-done.19 = bf16[8,7168]{1,0:T(8,128)(2,1)S(1)} collective-permute-done((bf16[8,7168]{1,0:T(8,128)(2,1)S(1)}, bf16[8,7168]{1,0:T(8,128)(2,1)S(1)}, u32[]{:S(2)}, u32[]{:S(2)}) %collective-permute-start.19) | collective-permute-done | bytes 114720 | tf_op jit(solution)/shard_map/ppermute | solution.py:35
  80.7 0.8 collective-permute-done.18
  81.7 4.7 %collective-permute-start.22 = (f32[2,7168]{1,0:T(2,128)S(1)}, f32[2,7168]{1,0:T(2,128)S(1)}, u32[]{:S(2)}, u32[]{:S(2)}) collective-permute-start(f32[2,7168]{1,0:T(2,128)S(1)} %get-tuple-element.20), channel_id=1, source_target_pairs={{0,4},{1,17},{2,6},{3,19},{4,0},{5,21},{6,2},{7,23},{8,12},{9,25},... | collective-permute-start | bytes 172040 | tf_op jit(solution)/shard_map/ppermute | solution.py:35
  86.4 0.7 collective-permute-done.20
  87.1 2.1 %collective-permute-done.22 = f32[2,7168]{1,0:T(2,128)S(1)} collective-permute-done((f32[2,7168]{1,0:T(2,128)S(1)}, f32[2,7168]{1,0:T(2,128)S(1)}, u32[]{:S(2)}, u32[]{:S(2)}) %collective-permute-start.22) | collective-permute-done | bytes 57376 | tf_op jit(solution)/shard_map/ppermute | solution.py:35
  89.2 1.4 %collective-permute-done.21 = f32[2,7168]{1,0:T(2,128)S(1)} collective-permute-done((f32[2,7168]{1,0:T(2,128)S(1)}, f32[2,7168]{1,0:T(2,128)S(1)}, u32[]{:S(2)}, u32[]{:S(2)}) %collective-permute-start.21) | collective-permute-done | bytes 57376 | tf_op jit(solution)/shard_map/ppermute | solution.py:35
  (29 shorter events, 3.9 us)
Async XLA Ops:
  2.3 6.4 %collective-permute-start.2 = (bf16[2,7296]{1,0:T(2,128)(2,1)S(1)}, bf16[2,7296]{1,0:T(2,128)(2,1)S(1)}, u32[]{:S(2)}, u32[]{:S(2)}) collective-permute-start(bf16[2,7296]{1,0:T(2,128)(2,1)S(1)} %maximum_bitcast_fusion), channel_id=1, source_target_pairs={{4,0},{17,1},{6,2},{19,3},{0,4},{21,5},{2,6},{23,7},{12,8},{25,9},... | collective-permute-start | bytes 87560 | tf_op jit(solution)/shard_map/ppermute | solution.py:31
  5.5 5.1 %collective-permute-start.1 = (bf16[2,7296]{1,0:T(2,128)(2,1)S(1)}, bf16[2,7296]{1,0:T(2,128)(2,1)S(1)}, u32[]{:S(2)}, u32[]{:S(2)}) collective-permute-start(bf16[2,7296]{1,0:T(2,128)(2,1)S(1)} %maximum_bitcast_fusion), channel_id=1, source_target_pairs={{6,0},{25,1},{0,2},{27,3},{2,4},{29,5},{4,6},{31,7},{14,8},{1,9},{... | collective-permute-start | bytes 87560 | tf_op jit(solution)/shard_map/ppermute | solution.py:31
  6.1 4.5 %collective-permute-start = (bf16[2,7296]{1,0:T(2,128)(2,1)S(1)}, bf16[2,7296]{1,0:T(2,128)(2,1)S(1)}, u32[]{:S(2)}, u32[]{:S(2)}) collective-permute-start(bf16[2,7296]{1,0:T(2,128)(2,1)S(1)} %maximum_bitcast_fusion), channel_id=1, source_target_pairs={{2,0},{9,1},{4,2},{11,3},{6,4},{13,5},{0,6},{15,7},{10,8},{17,9},{... | collective-permute-start | bytes 87560 | tf_op jit(solution)/shard_map/ppermute | solution.py:31
  10.8 6.5 %collective-permute-start.5 = (bf16[8,7296]{1,0:T(8,128)(2,1)S(1)}, bf16[8,7296]{1,0:T(8,128)(2,1)S(1)}, u32[]{:S(2)}, u32[]{:S(2)}) collective-permute-start(bf16[8,7296]{1,0:T(8,128)(2,1)S(1)} %pad_maximum_fusion), channel_id=1, source_target_pairs={{16,0},{65,1},{18,2},{67,3},{20,4},{69,5},{22,6},{71,7},{24,8},{73... | collective-permute-start | bytes 350216 | tf_op jit(solution)/shard_map/ppermute | solution.py:31
  14.0 6.0 %collective-permute-start.4 = (bf16[8,7296]{1,0:T(8,128)(2,1)S(1)}, bf16[8,7296]{1,0:T(8,128)(2,1)S(1)}, u32[]{:S(2)}, u32[]{:S(2)}) collective-permute-start(bf16[8,7296]{1,0:T(8,128)(2,1)S(1)} %pad_maximum_fusion), channel_id=1, source_target_pairs={{24,0},{97,1},{26,2},{99,3},{28,4},{101,5},{30,6},{103,7},{0,8},{1... | collective-permute-start | bytes 350216 | tf_op jit(solution)/shard_map/ppermute | solution.py:31
  14.7 5.3 %collective-permute-start.3 = (bf16[8,7296]{1,0:T(8,128)(2,1)S(1)}, bf16[8,7296]{1,0:T(8,128)(2,1)S(1)}, u32[]{:S(2)}, u32[]{:S(2)}) collective-permute-start(bf16[8,7296]{1,0:T(8,128)(2,1)S(1)} %pad_maximum_fusion), channel_id=1, source_target_pairs={{8,0},{33,1},{10,2},{35,3},{12,4},{37,5},{14,6},{39,7},{16,8},{41,... | collective-permute-start | bytes 350216 | tf_op jit(solution)/shard_map/ppermute | solution.py:31
  20.3 10.6 %collective-permute-start.8 = (bf16[32,7296]{1,0:T(8,128)(2,1)S(1)}, bf16[32,7296]{1,0:T(8,128)(2,1)S(1)}, u32[]{:S(2)}, u32[]{:S(2)}) collective-permute-start(bf16[32,7296]{1,0:T(8,128)(2,1)S(1)} %concatenate.13.refs_0_), channel_id=1, source_target_pairs={{64,0},{5,1},{66,2},{7,3},{68,4},{1,5},{70,6},{3,7},{72,8},{13,9},... | collective-permute-start | bytes 1400840 | tf_op jit(solution)/shard_map/ppermute | solution.py:31
  24.3 11.5 %collective-permute-start.7 = (bf16[32,7296]{1,0:T(8,128)(2,1)S(1)}, bf16[32,7296]{1,0:T(8,128)(2,1)S(1)}, u32[]{:S(2)}, u32[]{:S(2)}) collective-permute-start(bf16[32,7296]{1,0:T(8,128)(2,1)S(1)} %concatenate.13.refs_0_), channel_id=1, source_target_pairs={{96,0},{7,1},{98,2},{1,3},{100,4},{3,5},{102,6},{5,7},{104,8},{15,... | collective-permute-start | bytes 1400840 | tf_op jit(solution)/shard_map/ppermute | solution.py:31
  25.3 11.6 %collective-permute-start.6 = (bf16[32,7296]{1,0:T(8,128)(2,1)S(1)}, bf16[32,7296]{1,0:T(8,128)(2,1)S(1)}, u32[]{:S(2)}, u32[]{:S(2)}) collective-permute-start(bf16[32,7296]{1,0:T(8,128)(2,1)S(1)} %concatenate.13.refs_0_), channel_id=1, source_target_pairs={{32,0},{3,1},{34,2},{5,3},{36,4},{7,5},{38,6},{1,7},{40,8},{11,9},... | collective-permute-start | bytes 1400840 | tf_op jit(solution)/shard_map/ppermute | solution.py:31
  27.5 9.4 %collective-permute-start.9 = (bf16[32,7296]{1,0:T(8,128)(2,1)S(1)}, bf16[32,7296]{1,0:T(8,128)(2,1)S(1)}, u32[]{:S(2)}, u32[]{:S(2)}) collective-permute-start(bf16[32,7296]{1,0:T(8,128)(2,1)S(1)} %concatenate.13.refs_0_), channel_id=1, source_target_pairs={{0,1},{1,0},{2,3},{3,2},{4,5},{5,4},{6,7},{7,6},{8,9},{9,8},{10,11... | collective-permute-start | bytes 1400840 | tf_op jit(solution)/shard_map/ppermute | solution.py:39
  30.9 6.0 %collective-permute-start.12 = (bf16[32,7296]{1,0:T(8,128)(2,1)S(1)}, bf16[32,7296]{1,0:T(8,128)(2,1)S(1)}, u32[]{:S(2)}, u32[]{:S(2)}) collective-permute-start(bf16[32,7296]{1,0:T(8,128)(2,1)S(1)} %collective-permute-done.8.refs_3_), channel_id=1, source_target_pairs={{0,1},{1,0},{2,3},{3,2},{4,5},{5,4},{6,7},{7,6},{8,9},{9,8},{10,11... | collective-permute-start | bytes 1400840 | tf_op jit(solution)/shard_map/ppermute | solution.py:39
  35.8 1.8 %collective-permute-start.11 = (bf16[32,7296]{1,0:T(8,128)(2,1)S(1)}, bf16[32,7296]{1,0:T(8,128)(2,1)S(1)}, u32[]{:S(2)}, u32[]{:S(2)}) collective-permute-start(bf16[32,7296]{1,0:T(8,128)(2,1)S(1)} %collective-permute-done.7.refs_2_), channel_id=1, source_target_pairs={{0,1},{1,0},{2,3},{3,2},{4,5},{5,4},{6,7},{7,6},{8,9},{9,8},{10,11... | collective-permute-start | bytes 1400840 | tf_op jit(solution)/shard_map/ppermute | solution.py:39
  36.9 2.0 %collective-permute-start.10 = (bf16[32,7296]{1,0:T(8,128)(2,1)S(1)}, bf16[32,7296]{1,0:T(8,128)(2,1)}, u32[]{:S(2)}, u32[]{:S(2)}) collective-permute-start(bf16[32,7296]{1,0:T(8,128)(2,1)S(1)} %collective-permute-done.6.refs_1_), channel_id=1, source_target_pairs={{0,1},{1,0},{2,3},{3,2},{4,5},{5,4},{6,7},{7,6},{8,9},{9,8},{10,11... | collective-permute-start | bytes 1400840 | tf_op jit(solution)/shard_map/ppermute | solution.py:39
  51.7 3.9 %collective-permute-start.13 = (bf16[128,7168]{1,0:T(8,128)(2,1)S(1)}, bf16[128,7168]{1,0:T(8,128)(2,1)S(1)}, u32[]{:S(2)}, u32[]{:S(2)}) collective-permute-start(bf16[128,7168]{1,0:T(8,128)(2,1)S(1)} %get-tuple-element.8), channel_id=1, source_target_pairs={{0,1},{1,0},{2,3},{3,2},{4,5},{5,4},{6,7},{7,6},{8,9},{9,8},{10,11... | collective-permute-start | bytes 5505032 | tf_op jit(solution)/shard_map/ppermute | solution.py:39
  56.2 9.8 %collective-permute-start.14 = (bf16[32,7168]{1,0:T(8,128)(2,1)S(1)}, bf16[32,7168]{1,0:T(8,128)(2,1)S(1)}, u32[]{:S(2)}, u32[]{:S(2)}) collective-permute-start(bf16[32,7168]{1,0:T(8,128)(2,1)S(1)} %get-tuple-element.13), channel_id=1, source_target_pairs={{0,32},{1,3},{2,34},{3,5},{4,36},{5,7},{6,38},{7,1},{8,40},{9,11},... | collective-permute-start | bytes 1376264 | tf_op jit(solution)/shard_map/ppermute | solution.py:35
  57.9 13.8 %collective-permute-start.16 = (bf16[32,7168]{1,0:T(8,128)(2,1)S(1)}, bf16[32,7168]{1,0:T(8,128)(2,1)S(1)}, u32[]{:S(2)}, u32[]{:S(2)}) collective-permute-start(bf16[32,7168]{1,0:T(8,128)(2,1)S(1)} %get-tuple-element.14), channel_id=1, source_target_pairs={{0,64},{1,5},{2,66},{3,7},{4,68},{5,1},{6,70},{7,3},{8,72},{9,13},... | collective-permute-start | bytes 1376264 | tf_op jit(solution)/shard_map/ppermute | solution.py:35
  60.3 11.4 %collective-permute-start.15 = (bf16[32,7168]{1,0:T(8,128)(2,1)S(1)}, bf16[32,7168]{1,0:T(8,128)(2,1)S(1)}, u32[]{:S(2)}, u32[]{:S(2)}) collective-permute-start(bf16[32,7168]{1,0:T(8,128)(2,1)S(1)} %get-tuple-element.15), channel_id=1, source_target_pairs={{0,96},{1,7},{2,98},{3,1},{4,100},{5,3},{6,102},{7,5},{8,104},{9,1... | collective-permute-start | bytes 1376264 | tf_op jit(solution)/shard_map/ppermute | solution.py:35
  72.0 6.1 %collective-permute-start.17 = (bf16[8,7168]{1,0:T(8,128)(2,1)S(1)}, bf16[8,7168]{1,0:T(8,128)(2,1)S(1)}, u32[]{:S(2)}, u32[]{:S(2)}) collective-permute-start(bf16[8,7168]{1,0:T(8,128)(2,1)S(1)} %get-tuple-element.16), channel_id=1, source_target_pairs={{0,8},{1,33},{2,10},{3,35},{4,12},{5,37},{6,14},{7,39},{8,16},{9,4... | collective-permute-start | bytes 344072 | tf_op jit(solution)/shard_map/ppermute | solution.py:35
  72.1 8.6 %collective-permute-start.19 = (bf16[8,7168]{1,0:T(8,128)(2,1)S(1)}, bf16[8,7168]{1,0:T(8,128)(2,1)S(1)}, u32[]{:S(2)}, u32[]{:S(2)}) collective-permute-start(bf16[8,7168]{1,0:T(8,128)(2,1)S(1)} %get-tuple-element.17), channel_id=1, source_target_pairs={{0,16},{1,65},{2,18},{3,67},{4,20},{5,69},{6,22},{7,71},{8,24},{9,... | collective-permute-start | bytes 344072 | tf_op jit(solution)/shard_map/ppermute | solution.py:35
  76.7 4.8 %collective-permute-start.18 = (bf16[8,7168]{1,0:T(8,128)(2,1)S(1)}, bf16[8,7168]{1,0:T(8,128)(2,1)S(1)}, u32[]{:S(2)}, u32[]{:S(2)}) collective-permute-start(bf16[8,7168]{1,0:T(8,128)(2,1)S(1)} %get-tuple-element.18), channel_id=1, source_target_pairs={{0,24},{1,97},{2,26},{3,99},{4,28},{5,101},{6,30},{7,103},{8,0},{9... | collective-permute-start | bytes 344072 | tf_op jit(solution)/shard_map/ppermute | solution.py:35
  81.7 5.5 %collective-permute-start.20 = (f32[2,7168]{1,0:T(2,128)S(1)}, f32[2,7168]{1,0:T(2,128)S(1)}, u32[]{:S(2)}, u32[]{:S(2)}) collective-permute-start(f32[2,7168]{1,0:T(2,128)S(1)} %get-tuple-element.19), channel_id=1, source_target_pairs={{0,2},{1,9},{2,4},{3,11},{4,6},{5,13},{6,0},{7,15},{8,10},{9,17},{... | collective-permute-start | bytes 172040 | tf_op jit(solution)/shard_map/ppermute | solution.py:35
  81.7 7.4 %collective-permute-start.22 = (f32[2,7168]{1,0:T(2,128)S(1)}, f32[2,7168]{1,0:T(2,128)S(1)}, u32[]{:S(2)}, u32[]{:S(2)}) collective-permute-start(f32[2,7168]{1,0:T(2,128)S(1)} %get-tuple-element.20), channel_id=1, source_target_pairs={{0,4},{1,17},{2,6},{3,19},{4,0},{5,21},{6,2},{7,23},{8,12},{9,25},... | collective-permute-start | bytes 172040 | tf_op jit(solution)/shard_map/ppermute | solution.py:35
  86.4 4.2 %collective-permute-start.21 = (f32[2,7168]{1,0:T(2,128)S(1)}, f32[2,7168]{1,0:T(2,128)S(1)}, u32[]{:S(2)}, u32[]{:S(2)}) collective-permute-start(f32[2,7168]{1,0:T(2,128)S(1)} %get-tuple-element.21), channel_id=1, source_target_pairs={{0,6},{1,25},{2,0},{3,27},{4,2},{5,29},{6,4},{7,31},{8,14},{9,1},{... | collective-permute-start | bytes 172040 | tf_op jit(solution)/shard_map/ppermute | solution.py:35

commit v3 on v2

--- a/solution.py
+++ b/solution.py
@@ -40,16 +40,17 @@
 
 
 KSTEP = 3584
-NSTEP = 1792
+NSTEP = 3584
 AHEAD = 4
 
 
 def layer_kernel(first_ref, *refs):
     pieces = refs[:8]
     gate, up, shared_gate, shared_up, down, shared_down = refs[8:14]
-    own, other = refs[14:16]
-    gate_buf, up_buf, down_buf, sgu_buf, sd_buf, acts, hid, shared_hid, scale, sems = refs[16:]
+    kept, other = refs[14:16]
+    gate_buf, up_buf, down_buf, sgu_buf, acts, hid, sems = refs[16:]
     width = shared_down.shape[1]
+    units = down.shape[1]
     shared = shared_down.shape[0]
     steps = width // KSTEP
     cuts = width // NSTEP
@@ -63,10 +64,12 @@
         if e == 0:
             loads.append((shared_gate, sgu_buf.at[:shared]))
             loads.append((shared_up, sgu_buf.at[shared:]))
-            loads.append((shared_down, sd_buf))
+            loads.append((shared_down, down_buf.at[2 * units :]))
     for n in range(cuts):
         columns = pl.ds(n * NSTEP, NSTEP)
-        loads.append((down.at[:, :, columns], down_buf.at[:, :, columns]))
+        for e in range(2):
+            rows = pl.ds(e * units, units)
+            loads.append((down.at[e, :, columns], down_buf.at[rows, columns]))
     copies = [pltpu.make_async_copy(s, t, sems.at[i]) for i, (s, t) in enumerate(loads)]
     for copy in copies[:AHEAD]:
         copy.start()
@@ -82,17 +85,9 @@
         return jnp.concatenate([p[:, k * size : (k + 1) * size] for p in pieces], axis=0)
 
     def silu_mul(g, u):
-        return (g / (1.0 + jnp.exp(-g)) * u).astype(jnp.bfloat16)
+        return g / (1.0 + jnp.exp(-g)) * u
 
     block = pl.when(first_ref[0, 0] >= 0)
-
-    @block
-    def _():
-        weights = jnp.concatenate([p[:, width:] for p in pieces], axis=0).astype(jnp.float32)
-        lane = lax.broadcasted_iota(jnp.int32, weights.shape, 1)
-        for e in range(2):
-            mine = jnp.where(lane == first_ref[0, 0] + e, weights, 0.0)
-            scale[e] = jnp.broadcast_to(jnp.sum(mine, axis=1, keepdims=True), weights.shape)
 
     for e in range(2):
         for m, buf in enumerate((gate_buf, up_buf)):
@@ -115,7 +110,12 @@
 
         @block
         def _(e=e):
-            hid[e] = silu_mul(acts[0], acts[1])
+            weights = jnp.concatenate([p[:, width:] for p in pieces], axis=0).astype(jnp.float32)
+            lane = lax.broadcasted_iota(jnp.int32, weights.shape, 1)
+            mine = jnp.where(lane == first_ref[0, 0] + e, weights, 0.0)
+            scale = jnp.sum(mine, axis=1, keepdims=True)
+            act = silu_mul(acts[0], acts[1]) * scale
+            hid[:, e * units : (e + 1) * units] = act.astype(jnp.bfloat16)
             if e == 0:
                 dims = (((1,), (1,)), ((), ()))
                 both = None
@@ -127,20 +127,20 @@
                         preferred_element_type=jnp.float32,
                     )
                     both = part if both is None else both + part
-                shared_hid[...] = silu_mul(both[:, :shared], both[:, shared:])
+                act = silu_mul(both[:, :shared], both[:, shared:])
+                hid[:, 2 * units :] = act.astype(jnp.bfloat16)
 
     for n in range(cuts):
+        arrived()
         arrived()
 
         @block
         def _(n=n):
             columns = slice(n * NSTEP, (n + 1) * NSTEP)
-            total = jnp.dot(shared_hid[...], sd_buf[:, columns], preferred_element_type=jnp.float32)
-            for e in range(2):
-                part = jnp.dot(hid[e], down_buf[e, :, columns], preferred_element_type=jnp.float32)
-                total = total + scale[e][:, :1] * part
-            own[:, columns] = total[:128]
-            other[:, columns] = total[128:].astype(jnp.bfloat16)
+            total = jnp.dot(hid[128:], down_buf[:, columns], preferred_element_type=jnp.float32)
+            other[:, columns] = total.astype(jnp.bfloat16)
+            if n == 0:
+                kept[...] = hid[:128]
 
 
 def layer(pieces, first, gate, up, down, shared_gate, shared_up, shared_down):
@@ -152,7 +152,7 @@
     return pl.pallas_call(
         layer_kernel,
         out_shape=(
-            jax.ShapeDtypeStruct((128, width), jnp.float32),
+            jax.ShapeDtypeStruct((128, 2 * units + shared), jnp.bfloat16),
             jax.ShapeDtypeStruct((128, width), jnp.bfloat16),
         ),
         in_specs=[pl.BlockSpec(memory_space=pltpu.SMEM)]
@@ -162,16 +162,13 @@
         scratch_shapes=[
             pltpu.VMEM(gate.shape, jnp.bfloat16),
             pltpu.VMEM(up.shape, jnp.bfloat16),
-            pltpu.VMEM(down.shape, jnp.bfloat16),
+            pltpu.VMEM((2 * units + shared, width), jnp.bfloat16),
             pltpu.VMEM((2 * shared, width), jnp.bfloat16),
-            pltpu.VMEM((shared, width), jnp.bfloat16),
             pltpu.VMEM((2, 256, units), jnp.float32),
-            pltpu.VMEM((2, 256, units), jnp.bfloat16),
-            pltpu.VMEM((256, shared), jnp.bfloat16),
-            pltpu.VMEM((2, 256, META), jnp.float32),
-            pltpu.SemaphoreType.DMA((4 * width // KSTEP + 3 + width // NSTEP,)),
+            pltpu.VMEM((256, 2 * units + shared), jnp.bfloat16),
+            pltpu.SemaphoreType.DMA((4 * width // KSTEP + 3 + 2 * width // NSTEP,)),
         ],
-        compiler_params=pltpu.CompilerParams(vmem_limit_bytes=32 * 1024 * 1024),
+        compiler_params=pltpu.CompilerParams(vmem_limit_bytes=28 * 1024 * 1024),
         cost_estimate=pl.CostEstimate(
             flops=6 * 256 * width * (2 * units + shared),
             bytes_accessed=6 * width * (2 * units + shared) + 10 * 128 * width,
@@ -188,6 +185,84 @@
     )
 
 
+OSTEP = 1792
+
+
+def down_kernel(hid, down, shared_down, out, buf, sems):
+    units, width = down.shape[1:]
+    cuts = width // OSTEP
+    copies = [pltpu.make_async_copy(shared_down, buf.at[2 * units :], sems.at[0])]
+    for n in range(cuts):
+        columns = pl.ds(n * OSTEP, OSTEP)
+        for e in range(2):
+            rows = pl.ds(e * units, units)
+            copies.append(
+                pltpu.make_async_copy(
+                    down.at[e, :, columns], buf.at[rows, columns], sems.at[1 + 2 * n + e]
+                )
+            )
+    for copy in copies:
+        copy.start()
+    copies[0].wait()
+    for n in range(cuts):
+        copies[1 + 2 * n].wait()
+        copies[2 + 2 * n].wait()
+
+        @pl.when(pl.program_id(0) >= 0)
+        def _(n=n):
+            columns = slice(n * OSTEP, (n + 1) * OSTEP)
+            out[:, columns] = jnp.dot(
+                hid[...], buf[:, columns], preferred_element_type=jnp.float32
+            )
+
+
+def down_own(hid, down, shared_down):
+    units, width = down.shape[1:]
+    shared = shared_down.shape[0]
+    vmem = pl.BlockSpec(memory_space=pltpu.VMEM)
+    hbm = pl.BlockSpec(memory_space=pl.ANY)
+    return pl.pallas_call(
+        down_kernel,
+        grid=(1,),
+        out_shape=jax.ShapeDtypeStruct((128, width), jnp.float32),
+        in_specs=[vmem, hbm, hbm],
+        out_specs=vmem,
+        scratch_shapes=[
+            pltpu.VMEM((2 * units + shared, width), jnp.bfloat16),
+            pltpu.SemaphoreType.DMA((1 + 2 * width // OSTEP,)),
+        ],
+        compiler_params=pltpu.CompilerParams(vmem_limit_bytes=16 * 1024 * 1024),
+        cost_estimate=pl.CostEstimate(
+            flops=2 * 128 * width * (2 * units + shared),
+            bytes_accessed=2 * width * (2 * units + shared) + 4 * 128 * width,
+            transcendentals=0,
+        ),
+        name="down",
+    )(hid, *[pltpu.with_memory_space_constraint(a, pltpu.HBM) for a in (down, shared_down)])
+
+
+def prepare_kernel(hidden, routes, slots, weight, out):
+    width = hidden.shape[2]
+    out[:, :width] = jnp.concatenate([hidden[0], hidden[1]], axis=0).astype(jnp.bfloat16)
+    experts = jnp.concatenate([routes[0], routes[1]], axis=0)
+    kept = jnp.concatenate([slots[0], slots[1]], axis=0) >= 0
+    weights = jnp.where(kept, weight[...].astype(jnp.float32), 0.0)
+    lane = lax.broadcasted_iota(jnp.int32, (2, META), 1)
+    dense = jnp.zeros((2, META), jnp.float32)
+    for k in range(experts.shape[1]):
+        dense += jnp.where(lane == experts[:, k : k + 1], weights[:, k : k + 1], 0.0)
+    out[:, width:] = dense.astype(jnp.bfloat16)
+
+
+def prepare(hidden, routes, slots, route_weight):
+    steps, _, width = hidden.shape
+    return pl.pallas_call(
+        prepare_kernel,
+        out_shape=pltpu.VMEM((steps, width + META), jnp.bfloat16),
+        name="prepare",
+    )(hidden, routes, slots, route_weight[:, 0])
+
+
 def body(
     hidden,
     routes,
@@ -200,23 +275,18 @@
     shared_up,
     shared_down,
 ):
-    experts = jnp.arange(META, dtype=jnp.int32)
-    weight = jnp.where(slots >= 0, route_weight.astype(jnp.float32), 0.0)
-    dense = jnp.sum(
-        jnp.where(routes[..., None] == experts, weight[..., None], 0.0), axis=2
-    )
-    block = jnp.concatenate([hidden, dense], axis=2)[:, 0].astype(jnp.bfloat16)
-
+    block = prepare(hidden, routes, slots, route_weight)
     for stage in range(2):
         block = jnp.concatenate([block] + [fetch(block, stage, by) for by in (1, 3, 2)], axis=0)
     mine = [block] + [fetch(block, 2, by) for by in (1, 3, 2)]
     pieces = mine + [swap(piece) for piece in mine]
 
     first = (2 * lax.axis_index("group")).astype(jnp.int32).reshape(1, 1)
-    own, other = layer(
+    kept, other = layer(
         pieces, first, expert_gate, expert_up, expert_down, shared_gate, shared_up, shared_down
     )
-    total = own + swap(other).astype(jnp.float32)
+    other = swap(other)
+    total = down_own(kept, expert_down, shared_down) + other.astype(jnp.float32)
     for stage, kind in ((2, jnp.bfloat16), (1, jnp.bfloat16), (0, jnp.float32)):
         count = total.shape[0] // 4
         parts = [total[i * count : (i + 1) * count] for i in range(4)]

time: 91.6 us -> 89 us (0.972)
  waiting for transfers between devices: 38.7 us -> 35.1 us
  Pallas kernels: 12.8 us -> 16.1 us
  other arithmetic: 2.44 us -> 0.99 us
    ppermute x5, waiting for transfers between devices: 5.6 us -> 1.95 us  [swap(): lax.ppermute(block, AXES, [(flat(p), flat(p[:3] + (1 - p[3],))) for p in...]
    pallas_call x1 -> x3, Pallas kernels: 12.8 us -> 16.1 us  [the longest x1 11.1 us: layer(): pl.pallas_call(layer_kernel, out_shape=(jax.ShapeDtypeStruct((128, 2 * un...]
  transfers between devices with their start and end apart: 23 -> 23, of which waited for: 16 -> 16; matrix products, arithmetic and copies ran while one was open for 0% -> 0% of each run, Pallas kernels for 0% -> 5%
where the time goes in v3:
time: 89 us; the launch traced here: 88.8 us
  starting transfers between devices  35.4 us (40%)
  waiting for transfers between devices  35.1 us (39%)
  Pallas kernels  16.1 us (18%)
  local copies, waits for them, and re-layouts  1.11 us (1%)
  other arithmetic  0.99 us (1%)
    ppermute x9, starting transfers between devices, fetch(): lax.ppermute(block, AXES, [(flat(moved(p, stage, by)), flat(p)) for p in...  20.1 us
    ppermute x9, waiting for transfers between devices, send(): lax.ppermute(block, AXES, [(flat(p), flat(moved(p, stage, by))) for p in...  19.1 us
    ppermute x9, starting transfers between devices, send(): lax.ppermute(block, AXES, [(flat(p), flat(moved(p, stage, by))) for p in...  14.9 us
    ppermute x9, waiting for transfers between devices, fetch(): lax.ppermute(block, AXES, [(flat(moved(p, stage, by)), flat(p)) for p in...  14 us
    pallas_call x1, Pallas kernels, layer(): pl.pallas_call(layer_kernel, out_shape=(jax.ShapeDtypeStruct((128, 2 * un...  11.1 us
    pallas_call x1, Pallas kernels, down_own(): pl.pallas_call(down_kernel, grid=(1,), out_shape=jax.ShapeDtypeStruct((12...  4.04 us
    ppermute x5, waiting for transfers between devices, swap(): lax.ppermute(block, AXES, [(flat(p), flat(p[:3] + (1 - p[3],))) for p in...  1.95 us
  transfers between devices with their start and end apart: 23, of which 16 were waited for; matrix products, arithmetic and copies ran while one was open for 0% of the time, Pallas kernels for 5%

profile of v3, /device:TPU:0, one launch (start us, length us, event | category | flops | bytes accessed | tf_op | source)
XLA Modules:
  0.0 88.8 jit_solution(15367946980320437793)
XLA Ops:
  0.0 0.9 %prepare.1 = bf16[2,7296]{1,0:T(2,128)(2,1)S(1)} custom-call(f32[2,1,7168]{2,1,0:T(1,128)} %hidden.1, s32[2,1,8]{2,1,0:T(1,128)} %routes.1, s32[2,1,8]{2,1,0:T(1,128)} %slots.1, bf16[2,8]{1,0:T(2,128)(2,1)} %bitcast.8), custom_call_target="tpu_custom_call" | custom-call | tf_op jit(solution)/shard_map/prepare/pallas_call | solution.py:259
  0.9 3.2 %collective-permute-start.2 = (bf16[2,7296]{1,0:T(2,128)(2,1)S(1)}, bf16[2,7296]{1,0:T(2,128)(2,1)S(1)}, u32[]{:S(2)}, u32[]{:S(2)}) collective-permute-start(bf16[2,7296]{1,0:T(2,128)(2,1)S(1)} %prepare.1), channel_id=1, source_target_pairs={{4,0},{17,1},{6,2},{19,3},{0,4},{21,5},{2,6},{23,7},{12,8},{25,9},... | collective-permute-start | bytes 87560 | tf_op jit(solution)/shard_map/ppermute | solution.py:31
  4.7 2.6 %collective-permute-start = (bf16[2,7296]{1,0:T(2,128)(2,1)S(1)}, bf16[2,7296]{1,0:T(2,128)(2,1)S(1)}, u32[]{:S(2)}, u32[]{:S(2)}) collective-permute-start(bf16[2,7296]{1,0:T(2,128)(2,1)S(1)} %prepare.1), channel_id=1, source_target_pairs={{2,0},{9,1},{4,2},{11,3},{6,4},{13,5},{0,6},{15,7},{10,8},{17,9},{... | collective-permute-start | bytes 87560 | tf_op jit(solution)/shard_map/ppermute | solution.py:31
  7.4 1.8 %collective-permute-done.1 = bf16[2,7296]{1,0:T(2,128)(2,1)S(1)} collective-permute-done((bf16[2,7296]{1,0:T(2,128)(2,1)S(1)}, bf16[2,7296]{1,0:T(2,128)(2,1)S(1)}, u32[]{:S(2)}, u32[]{:S(2)}) %collective-permute-start.1) | collective-permute-done | bytes 29216 | tf_op jit(solution)/shard_map/ppermute | solution.py:31
  9.4 3.3 %collective-permute-start.5 = (bf16[8,7296]{1,0:T(8,128)(2,1)S(1)}, bf16[8,7296]{1,0:T(8,128)(2,1)S(1)}, u32[]{:S(2)}, u32[]{:S(2)}) collective-permute-start(bf16[8,7296]{1,0:T(8,128)(2,1)S(1)} %pad_maximum_fusion), channel_id=1, source_target_pairs={{16,0},{65,1},{18,2},{67,3},{20,4},{69,5},{22,6},{71,7},{24,8},{73... | collective-permute-start | bytes 350216 | tf_op jit(solution)/shard_map/ppermute | solution.py:31
  12.6 0.7 collective-permute-start.4
  13.3 2.6 %collective-permute-start.3 = (bf16[8,7296]{1,0:T(8,128)(2,1)S(1)}, bf16[8,7296]{1,0:T(8,128)(2,1)S(1)}, u32[]{:S(2)}, u32[]{:S(2)}) collective-permute-start(bf16[8,7296]{1,0:T(8,128)(2,1)S(1)} %pad_maximum_fusion), channel_id=1, source_target_pairs={{8,0},{33,1},{10,2},{35,3},{12,4},{37,5},{14,6},{39,7},{16,8},{41,... | collective-permute-start | bytes 350216 | tf_op jit(solution)/shard_map/ppermute | solution.py:31
  15.9 2.8 %collective-permute-done.4 = bf16[8,7296]{1,0:T(8,128)(2,1)S(1)} collective-permute-done((bf16[8,7296]{1,0:T(8,128)(2,1)S(1)}, bf16[8,7296]{1,0:T(8,128)(2,1)S(1)}, u32[]{:S(2)}, u32[]{:S(2)}) %collective-permute-start.4) | collective-permute-done | bytes 116768 | tf_op jit(solution)/shard_map/ppermute | solution.py:31
  18.9 4.0 %collective-permute-start.8 = (bf16[32,7296]{1,0:T(8,128)(2,1)S(1)}, bf16[32,7296]{1,0:T(8,128)(2,1)S(1)}, u32[]{:S(2)}, u32[]{:S(2)}) collective-permute-start(bf16[32,7296]{1,0:T(8,128)(2,1)S(1)} %concatenate.8.refs_0_), channel_id=1, source_target_pairs={{64,0},{5,1},{66,2},{7,3},{68,4},{1,5},{70,6},{3,7},{72,8},{13,9},... | collective-permute-start | bytes 1400840 | tf_op jit(solution)/shard_map/ppermute | solution.py:31
  22.8 1.0 %collective-permute-start.7 = (bf16[32,7296]{1,0:T(8,128)(2,1)S(1)}, bf16[32,7296]{1,0:T(8,128)(2,1)S(1)}, u32[]{:S(2)}, u32[]{:S(2)}) collective-permute-start(bf16[32,7296]{1,0:T(8,128)(2,1)S(1)} %concatenate.8.refs_0_), channel_id=1, source_target_pairs={{96,0},{7,1},{98,2},{1,3},{100,4},{3,5},{102,6},{5,7},{104,8},{15,... | collective-permute-start | bytes 1400840 | tf_op jit(solution)/shard_map/ppermute | solution.py:31
  23.9 2.2 %collective-permute-start.6 = (bf16[32,7296]{1,0:T(8,128)(2,1)S(1)}, bf16[32,7296]{1,0:T(8,128)(2,1)S(1)}, u32[]{:S(2)}, u32[]{:S(2)}) collective-permute-start(bf16[32,7296]{1,0:T(8,128)(2,1)S(1)} %concatenate.8.refs_0_), channel_id=1, source_target_pairs={{32,0},{3,1},{34,2},{5,3},{36,4},{7,5},{38,6},{1,7},{40,8},{11,9},... | collective-permute-start | bytes 1400840 | tf_op jit(solution)/shard_map/ppermute | solution.py:31
  26.1 3.4 %collective-permute-done.8.refs_3_ = bf16[32,7296]{1,0:T(8,128)(2,1)S(1)} collective-permute-done((bf16[32,7296]{1,0:T(8,128)(2,1)S(1)}, bf16[32,7296]{1,0:T(8,128)(2,1)S(1)}, u32[]{:S(2)}, u32[]{:S(2)}) %collective-permute-start.8) | collective-permute-done | bytes 466976 | tf_op jit(solution)/shard_map/ppermute | solution.py:31
  29.5 4.9 %collective-permute-done.7.refs_2_ = bf16[32,7296]{1,0:T(8,128)(2,1)S(1)} collective-permute-done((bf16[32,7296]{1,0:T(8,128)(2,1)S(1)}, bf16[32,7296]{1,0:T(8,128)(2,1)S(1)}, u32[]{:S(2)}, u32[]{:S(2)}) %collective-permute-start.7) | collective-permute-done | bytes 466976 | tf_op jit(solution)/shard_map/ppermute | solution.py:31
  34.4 1.1 %collective-permute-done.6.refs_1_ = bf16[32,7296]{1,0:T(8,128)(2,1)S(1)} collective-permute-done((bf16[32,7296]{1,0:T(8,128)(2,1)S(1)}, bf16[32,7296]{1,0:T(8,128)(2,1)S(1)}, u32[]{:S(2)}, u32[]{:S(2)}) %collective-permute-start.6) | collective-permute-done | bytes 466976 | tf_op jit(solution)/shard_map/ppermute | solution.py:31
  35.5 0.8 collective-permute-done.11.refs_6_
  36.2 1.2 %collective-permute-done.10.refs_5_ = bf16[32,7296]{1,0:T(8,128)(2,1)} collective-permute-done((bf16[32,7296]{1,0:T(8,128)(2,1)S(1)}, bf16[32,7296]{1,0:T(8,128)(2,1)}, u32[]{:S(2)}, u32[]{:S(2)}) %collective-permute-start.10) | collective-permute-done | bytes 466976 | tf_op jit(solution)/shard_map/ppermute | solution.py:39
  37.4 11.1 %layer.1 = (bf16[128,528]{1,0:T(8,128)(2,1)S(1)}, bf16[128,7168]{1,0:T(8,128)(2,1)S(1)}) custom-call(s32[1,1]{1,0:T(1,128)} %bitcast.first_ref, bf16[32,7296]{1,0:T(8,128)(2,1)S(1)} %concatenate.8.refs_0_, bf16[32,7296]{1,0:T(8,128)(2,1)S(1)} %collective-permute-done.6.refs_1_, bf16[32,7296]{1,0:T(8,128)(2,1)S(1)} %collective-permute-done.7.refs_2_, ...), custom_call_target="tpu_custom_call" | custom-call | flops 5813305344 | bytes 31883264 | tf_op jit(solution)/shard_map/layer/pallas_call | solution.py:152
  48.9 4.0 %down.2 = f32[128,7168]{1,0:T(8,128)S(1)} custom-call(bf16[128,528]{1,0:T(8,128)(2,1)S(1)} %get-tuple-element.7.hid, bf16[2,256,7168]{2,1,0:T(8,128)(2,1)} %down.3, bf16[16,7168]{1,0:T(8,128)(2,1)} %shared_down.1), custom_call_target="tpu_custom_call" | custom-call | flops 968884224 | bytes 11239424 | tf_op jit(solution)/shard_map/down/pallas_call | solution.py:224
  53.6 1.7 %collective-permute-start.14 = (bf16[32,7168]{1,0:T(8,128)(2,1)S(1)}, bf16[32,7168]{1,0:T(8,128)(2,1)S(1)}, u32[]{:S(2)}, u32[]{:S(2)}) collective-permute-start(bf16[32,7168]{1,0:T(8,128)(2,1)S(1)} %get-tuple-element.13), channel_id=1, source_target_pairs={{0,32},{1,3},{2,34},{3,5},{4,36},{5,7},{6,38},{7,1},{8,40},{9,11},... | collective-permute-start | bytes 1376264 | tf_op jit(solution)/shard_map/ppermute | solution.py:35
  55.4 2.4 %collective-permute-start.16 = (bf16[32,7168]{1,0:T(8,128)(2,1)S(1)}, bf16[32,7168]{1,0:T(8,128)(2,1)S(1)}, u32[]{:S(2)}, u32[]{:S(2)}) collective-permute-start(bf16[32,7168]{1,0:T(8,128)(2,1)S(1)} %get-tuple-element.14), channel_id=1, source_target_pairs={{0,64},{1,5},{2,66},{3,7},{4,68},{5,1},{6,70},{7,3},{8,72},{9,13},... | collective-permute-start | bytes 1376264 | tf_op jit(solution)/shard_map/ppermute | solution.py:35
  57.8 1.2 %collective-permute-start.15 = (bf16[32,7168]{1,0:T(8,128)(2,1)S(1)}, bf16[32,7168]{1,0:T(8,128)(2,1)S(1)}, u32[]{:S(2)}, u32[]{:S(2)}) collective-permute-start(bf16[32,7168]{1,0:T(8,128)(2,1)S(1)} %get-tuple-element.15), channel_id=1, source_target_pairs={{0,96},{1,7},{2,98},{3,1},{4,100},{5,3},{6,102},{7,5},{8,104},{9,1... | collective-permute-start | bytes 1376264 | tf_op jit(solution)/shard_map/ppermute | solution.py:35
  59.0 4.4 %collective-permute-done.14 = bf16[32,7168]{1,0:T(8,128)(2,1)S(1)} collective-permute-done((bf16[32,7168]{1,0:T(8,128)(2,1)S(1)}, bf16[32,7168]{1,0:T(8,128)(2,1)S(1)}, u32[]{:S(2)}, u32[]{:S(2)}) %collective-permute-start.14) | collective-permute-done | bytes 458784 | tf_op jit(solution)/shard_map/ppermute | solution.py:35
  63.4 5.8 %collective-permute-done.16 = bf16[32,7168]{1,0:T(8,128)(2,1)S(1)} collective-permute-done((bf16[32,7168]{1,0:T(8,128)(2,1)S(1)}, bf16[32,7168]{1,0:T(8,128)(2,1)S(1)}, u32[]{:S(2)}, u32[]{:S(2)}) %collective-permute-start.16) | collective-permute-done | bytes 458784 | tf_op jit(solution)/shard_map/ppermute | solution.py:35
  69.6 4.6 %collective-permute-start.19 = (bf16[8,7168]{1,0:T(8,128)(2,1)S(1)}, bf16[8,7168]{1,0:T(8,128)(2,1)S(1)}, u32[]{:S(2)}, u32[]{:S(2)}) collective-permute-start(bf16[8,7168]{1,0:T(8,128)(2,1)S(1)} %get-tuple-element.17), channel_id=1, source_target_pairs={{0,16},{1,65},{2,18},{3,67},{4,20},{5,69},{6,22},{7,71},{8,24},{9,... | collective-permute-start | bytes 344072 | tf_op jit(solution)/shard_map/ppermute | solution.py:35
  74.2 1.3 %collective-permute-done.17 = bf16[8,7168]{1,0:T(8,128)(2,1)S(1)} collective-permute-done((bf16[8,7168]{1,0:T(8,128)(2,1)S(1)}, bf16[8,7168]{1,0:T(8,128)(2,1)S(1)}, u32[]{:S(2)}, u32[]{:S(2)}) %collective-permute-start.17) | collective-permute-done | bytes 114720 | tf_op jit(solution)/shard_map/ppermute | solution.py:35
  75.5 2.7 %collective-permute-done.19 = bf16[8,7168]{1,0:T(8,128)(2,1)S(1)} collective-permute-done((bf16[8,7168]{1,0:T(8,128)(2,1)S(1)}, bf16[8,7168]{1,0:T(8,128)(2,1)S(1)}, u32[]{:S(2)}, u32[]{:S(2)}) %collective-permute-start.19) | collective-permute-done | bytes 114720 | tf_op jit(solution)/shard_map/ppermute | solution.py:35
  78.2 0.8 collective-permute-done.18
  79.2 4.7 %collective-permute-start.22 = (f32[2,7168]{1,0:T(2,128)S(1)}, f32[2,7168]{1,0:T(2,128)S(1)}, u32[]{:S(2)}, u32[]{:S(2)}) collective-permute-start(f32[2,7168]{1,0:T(2,128)S(1)} %get-tuple-element.20), channel_id=1, source_target_pairs={{0,4},{1,17},{2,6},{3,19},{4,0},{5,21},{6,2},{7,23},{8,12},{9,25},... | collective-permute-start | bytes 172040 | tf_op jit(solution)/shard_map/ppermute | solution.py:35
  83.9 0.7 collective-permute-done.20
  84.6 2.1 %collective-permute-done.22 = f32[2,7168]{1,0:T(2,128)S(1)} collective-permute-done((f32[2,7168]{1,0:T(2,128)S(1)}, f32[2,7168]{1,0:T(2,128)S(1)}, u32[]{:S(2)}, u32[]{:S(2)}) %collective-permute-start.22) | collective-permute-done | bytes 57376 | tf_op jit(solution)/shard_map/ppermute | solution.py:35
  86.6 1.4 %collective-permute-done.21 = f32[2,7168]{1,0:T(2,128)S(1)} collective-permute-done((f32[2,7168]{1,0:T(2,128)S(1)}, f32[2,7168]{1,0:T(2,128)S(1)}, u32[]{:S(2)}, u32[]{:S(2)}) %collective-permute-start.21) | collective-permute-done | bytes 57376 | tf_op jit(solution)/shard_map/ppermute | solution.py:35
  88.1 0.7 copy.11
  (27 shorter events, 2.7 us)
Async XLA Ops:
  0.9 6.4 %collective-permute-start.2 = (bf16[2,7296]{1,0:T(2,128)(2,1)S(1)}, bf16[2,7296]{1,0:T(2,128)(2,1)S(1)}, u32[]{:S(2)}, u32[]{:S(2)}) collective-permute-start(bf16[2,7296]{1,0:T(2,128)(2,1)S(1)} %prepare.1), channel_id=1, source_target_pairs={{4,0},{17,1},{6,2},{19,3},{0,4},{21,5},{2,6},{23,7},{12,8},{25,9},... | collective-permute-start | bytes 87560 | tf_op jit(solution)/shard_map/ppermute | solution.py:31
  4.1 5.1 %collective-permute-start.1 = (bf16[2,7296]{1,0:T(2,128)(2,1)S(1)}, bf16[2,7296]{1,0:T(2,128)(2,1)S(1)}, u32[]{:S(2)}, u32[]{:S(2)}) collective-permute-start(bf16[2,7296]{1,0:T(2,128)(2,1)S(1)} %prepare.1), channel_id=1, source_target_pairs={{6,0},{25,1},{0,2},{27,3},{2,4},{29,5},{4,6},{31,7},{14,8},{1,9},{... | collective-permute-start | bytes 87560 | tf_op jit(solution)/shard_map/ppermute | solution.py:31
  4.7 4.5 %collective-permute-start = (bf16[2,7296]{1,0:T(2,128)(2,1)S(1)}, bf16[2,7296]{1,0:T(2,128)(2,1)S(1)}, u32[]{:S(2)}, u32[]{:S(2)}) collective-permute-start(bf16[2,7296]{1,0:T(2,128)(2,1)S(1)} %prepare.1), channel_id=1, source_target_pairs={{2,0},{9,1},{4,2},{11,3},{6,4},{13,5},{0,6},{15,7},{10,8},{17,9},{... | collective-permute-start | bytes 87560 | tf_op jit(solution)/shard_map/ppermute | solution.py:31
  9.4 6.5 %collective-permute-start.5 = (bf16[8,7296]{1,0:T(8,128)(2,1)S(1)}, bf16[8,7296]{1,0:T(8,128)(2,1)S(1)}, u32[]{:S(2)}, u32[]{:S(2)}) collective-permute-start(bf16[8,7296]{1,0:T(8,128)(2,1)S(1)} %pad_maximum_fusion), channel_id=1, source_target_pairs={{16,0},{65,1},{18,2},{67,3},{20,4},{69,5},{22,6},{71,7},{24,8},{73... | collective-permute-start | bytes 350216 | tf_op jit(solution)/shard_map/ppermute | solution.py:31
  12.6 6.0 %collective-permute-start.4 = (bf16[8,7296]{1,0:T(8,128)(2,1)S(1)}, bf16[8,7296]{1,0:T(8,128)(2,1)S(1)}, u32[]{:S(2)}, u32[]{:S(2)}) collective-permute-start(bf16[8,7296]{1,0:T(8,128)(2,1)S(1)} %pad_maximum_fusion), channel_id=1, source_target_pairs={{24,0},{97,1},{26,2},{99,3},{28,4},{101,5},{30,6},{103,7},{0,8},{1... | collective-permute-start | bytes 350216 | tf_op jit(solution)/shard_map/ppermute | solution.py:31
  13.3 5.3 %collective-permute-start.3 = (bf16[8,7296]{1,0:T(8,128)(2,1)S(1)}, bf16[8,7296]{1,0:T(8,128)(2,1)S(1)}, u32[]{:S(2)}, u32[]{:S(2)}) collective-permute-start(bf16[8,7296]{1,0:T(8,128)(2,1)S(1)} %pad_maximum_fusion), channel_id=1, source_target_pairs={{8,0},{33,1},{10,2},{35,3},{12,4},{37,5},{14,6},{39,7},{16,8},{41,... | collective-permute-start | bytes 350216 | tf_op jit(solution)/shard_map/ppermute | solution.py:31
  18.9 10.6 %collective-permute-start.8 = (bf16[32,7296]{1,0:T(8,128)(2,1)S(1)}, bf16[32,7296]{1,0:T(8,128)(2,1)S(1)}, u32[]{:S(2)}, u32[]{:S(2)}) collective-permute-start(bf16[32,7296]{1,0:T(8,128)(2,1)S(1)} %concatenate.8.refs_0_), channel_id=1, source_target_pairs={{64,0},{5,1},{66,2},{7,3},{68,4},{1,5},{70,6},{3,7},{72,8},{13,9},... | collective-permute-start | bytes 1400840 | tf_op jit(solution)/shard_map/ppermute | solution.py:31
  22.8 11.5 %collective-permute-start.7 = (bf16[32,7296]{1,0:T(8,128)(2,1)S(1)}, bf16[32,7296]{1,0:T(8,128)(2,1)S(1)}, u32[]{:S(2)}, u32[]{:S(2)}) collective-permute-start(bf16[32,7296]{1,0:T(8,128)(2,1)S(1)} %concatenate.8.refs_0_), channel_id=1, source_target_pairs={{96,0},{7,1},{98,2},{1,3},{100,4},{3,5},{102,6},{5,7},{104,8},{15,... | collective-permute-start | bytes 1400840 | tf_op jit(solution)/shard_map/ppermute | solution.py:31
  23.9 11.6 %collective-permute-start.6 = (bf16[32,7296]{1,0:T(8,128)(2,1)S(1)}, bf16[32,7296]{1,0:T(8,128)(2,1)S(1)}, u32[]{:S(2)}, u32[]{:S(2)}) collective-permute-start(bf16[32,7296]{1,0:T(8,128)(2,1)S(1)} %concatenate.8.refs_0_), channel_id=1, source_target_pairs={{32,0},{3,1},{34,2},{5,3},{36,4},{7,5},{38,6},{1,7},{40,8},{11,9},... | collective-permute-start | bytes 1400840 | tf_op jit(solution)/shard_map/ppermute | solution.py:31
  26.1 9.4 %collective-permute-start.9 = (bf16[32,7296]{1,0:T(8,128)(2,1)S(1)}, bf16[32,7296]{1,0:T(8,128)(2,1)S(1)}, u32[]{:S(2)}, u32[]{:S(2)}) collective-permute-start(bf16[32,7296]{1,0:T(8,128)(2,1)S(1)} %concatenate.8.refs_0_), channel_id=1, source_target_pairs={{0,1},{1,0},{2,3},{3,2},{4,5},{5,4},{6,7},{7,6},{8,9},{9,8},{10,11... | collective-permute-start | bytes 1400840 | tf_op jit(solution)/shard_map/ppermute | solution.py:39
  29.5 6.0 %collective-permute-start.12 = (bf16[32,7296]{1,0:T(8,128)(2,1)S(1)}, bf16[32,7296]{1,0:T(8,128)(2,1)S(1)}, u32[]{:S(2)}, u32[]{:S(2)}) collective-permute-start(bf16[32,7296]{1,0:T(8,128)(2,1)S(1)} %collective-permute-done.8.refs_3_), channel_id=1, source_target_pairs={{0,1},{1,0},{2,3},{3,2},{4,5},{5,4},{6,7},{7,6},{8,9},{9,8},{10,11... | collective-permute-start | bytes 1400840 | tf_op jit(solution)/shard_map/ppermute | solution.py:39
  34.4 1.8 %collective-permute-start.11 = (bf16[32,7296]{1,0:T(8,128)(2,1)S(1)}, bf16[32,7296]{1,0:T(8,128)(2,1)S(1)}, u32[]{:S(2)}, u32[]{:S(2)}) collective-permute-start(bf16[32,7296]{1,0:T(8,128)(2,1)S(1)} %collective-permute-done.7.refs_2_), channel_id=1, source_target_pairs={{0,1},{1,0},{2,3},{3,2},{4,5},{5,4},{6,7},{7,6},{8,9},{9,8},{10,11... | collective-permute-start | bytes 1400840 | tf_op jit(solution)/shard_map/ppermute | solution.py:39
  35.5 2.0 %collective-permute-start.10 = (bf16[32,7296]{1,0:T(8,128)(2,1)S(1)}, bf16[32,7296]{1,0:T(8,128)(2,1)}, u32[]{:S(2)}, u32[]{:S(2)}) collective-permute-start(bf16[32,7296]{1,0:T(8,128)(2,1)S(1)} %collective-permute-done.6.refs_1_), channel_id=1, source_target_pairs={{0,1},{1,0},{2,3},{3,2},{4,5},{5,4},{6,7},{7,6},{8,9},{9,8},{10,11... | collective-permute-start | bytes 1400840 | tf_op jit(solution)/shard_map/ppermute | solution.py:39
  48.5 4.4 %collective-permute-start.13 = (bf16[128,7168]{1,0:T(8,128)(2,1)S(1)}, bf16[128,7168]{1,0:T(8,128)(2,1)S(1)}, u32[]{:S(2)}, u32[]{:S(2)}) collective-permute-start(bf16[128,7168]{1,0:T(8,128)(2,1)S(1)} %get-tuple-element.8), channel_id=1, source_target_pairs={{0,1},{1,0},{2,3},{3,2},{4,5},{5,4},{6,7},{7,6},{8,9},{9,8},{10,11... | collective-permute-start | bytes 5505032 | tf_op jit(solution)/shard_map/ppermute | solution.py:39
  53.6 9.8 %collective-permute-start.14 = (bf16[32,7168]{1,0:T(8,128)(2,1)S(1)}, bf16[32,7168]{1,0:T(8,128)(2,1)S(1)}, u32[]{:S(2)}, u32[]{:S(2)}) collective-permute-start(bf16[32,7168]{1,0:T(8,128)(2,1)S(1)} %get-tuple-element.13), channel_id=1, source_target_pairs={{0,32},{1,3},{2,34},{3,5},{4,36},{5,7},{6,38},{7,1},{8,40},{9,11},... | collective-permute-start | bytes 1376264 | tf_op jit(solution)/shard_map/ppermute | solution.py:35
  55.4 13.8 %collective-permute-start.16 = (bf16[32,7168]{1,0:T(8,128)(2,1)S(1)}, bf16[32,7168]{1,0:T(8,128)(2,1)S(1)}, u32[]{:S(2)}, u32[]{:S(2)}) collective-permute-start(bf16[32,7168]{1,0:T(8,128)(2,1)S(1)} %get-tuple-element.14), channel_id=1, source_target_pairs={{0,64},{1,5},{2,66},{3,7},{4,68},{5,1},{6,70},{7,3},{8,72},{9,13},... | collective-permute-start | bytes 1376264 | tf_op jit(solution)/shard_map/ppermute | solution.py:35
  57.8 11.4 %collective-permute-start.15 = (bf16[32,7168]{1,0:T(8,128)(2,1)S(1)}, bf16[32,7168]{1,0:T(8,128)(2,1)S(1)}, u32[]{:S(2)}, u32[]{:S(2)}) collective-permute-start(bf16[32,7168]{1,0:T(8,128)(2,1)S(1)} %get-tuple-element.15), channel_id=1, source_target_pairs={{0,96},{1,7},{2,98},{3,1},{4,100},{5,3},{6,102},{7,5},{8,104},{9,1... | collective-permute-start | bytes 1376264 | tf_op jit(solution)/shard_map/ppermute | solution.py:35
  69.4 6.1 %collective-permute-start.17 = (bf16[8,7168]{1,0:T(8,128)(2,1)S(1)}, bf16[8,7168]{1,0:T(8,128)(2,1)S(1)}, u32[]{:S(2)}, u32[]{:S(2)}) collective-permute-start(bf16[8,7168]{1,0:T(8,128)(2,1)S(1)} %get-tuple-element.16), channel_id=1, source_target_pairs={{0,8},{1,33},{2,10},{3,35},{4,12},{5,37},{6,14},{7,39},{8,16},{9,4... | collective-permute-start | bytes 344072 | tf_op jit(solution)/shard_map/ppermute | solution.py:35
  69.6 8.6 %collective-permute-start.19 = (bf16[8,7168]{1,0:T(8,128)(2,1)S(1)}, bf16[8,7168]{1,0:T(8,128)(2,1)S(1)}, u32[]{:S(2)}, u32[]{:S(2)}) collective-permute-start(bf16[8,7168]{1,0:T(8,128)(2,1)S(1)} %get-tuple-element.17), channel_id=1, source_target_pairs={{0,16},{1,65},{2,18},{3,67},{4,20},{5,69},{6,22},{7,71},{8,24},{9,... | collective-permute-start | bytes 344072 | tf_op jit(solution)/shard_map/ppermute | solution.py:35
  74.2 4.8 %collective-permute-start.18 = (bf16[8,7168]{1,0:T(8,128)(2,1)S(1)}, bf16[8,7168]{1,0:T(8,128)(2,1)S(1)}, u32[]{:S(2)}, u32[]{:S(2)}) collective-permute-start(bf16[8,7168]{1,0:T(8,128)(2,1)S(1)} %get-tuple-element.18), channel_id=1, source_target_pairs={{0,24},{1,97},{2,26},{3,99},{4,28},{5,101},{6,30},{7,103},{8,0},{9... | collective-permute-start | bytes 344072 | tf_op jit(solution)/shard_map/ppermute | solution.py:35
  79.1 5.5 %collective-permute-start.20 = (f32[2,7168]{1,0:T(2,128)S(1)}, f32[2,7168]{1,0:T(2,128)S(1)}, u32[]{:S(2)}, u32[]{:S(2)}) collective-permute-start(f32[2,7168]{1,0:T(2,128)S(1)} %get-tuple-element.19), channel_id=1, source_target_pairs={{0,2},{1,9},{2,4},{3,11},{4,6},{5,13},{6,0},{7,15},{8,10},{9,17},{... | collective-permute-start | bytes 172040 | tf_op jit(solution)/shard_map/ppermute | solution.py:35
  79.2 7.4 %collective-permute-start.22 = (f32[2,7168]{1,0:T(2,128)S(1)}, f32[2,7168]{1,0:T(2,128)S(1)}, u32[]{:S(2)}, u32[]{:S(2)}) collective-permute-start(f32[2,7168]{1,0:T(2,128)S(1)} %get-tuple-element.20), channel_id=1, source_target_pairs={{0,4},{1,17},{2,6},{3,19},{4,0},{5,21},{6,2},{7,23},{8,12},{9,25},... | collective-permute-start | bytes 172040 | tf_op jit(solution)/shard_map/ppermute | solution.py:35
  83.9 4.2 %collective-permute-start.21 = (f32[2,7168]{1,0:T(2,128)S(1)}, f32[2,7168]{1,0:T(2,128)S(1)}, u32[]{:S(2)}, u32[]{:S(2)}) collective-permute-start(f32[2,7168]{1,0:T(2,128)S(1)} %get-tuple-element.21), channel_id=1, source_target_pairs={{0,6},{1,25},{2,0},{3,27},{4,2},{5,29},{6,4},{7,31},{8,14},{9,1},{... | collective-permute-start | bytes 172040 | tf_op jit(solution)/shard_map/ppermute | solution.py:35

commit v4 on v3

--- a/solution.py
+++ b/solution.py
@@ -39,9 +39,9 @@
     return lax.ppermute(block, AXES, [(flat(p), flat(p[:3] + (1 - p[3],))) for p in places()])
 
 
-KSTEP = 3584
+SPLIT = 4
 NSTEP = 3584
-AHEAD = 4
+AHEAD = 12
 
 
 def layer_kernel(first_ref, *refs):
@@ -49,89 +49,79 @@
     gate, up, shared_gate, shared_up, down, shared_down = refs[8:14]
     kept, other = refs[14:16]
     gate_buf, up_buf, down_buf, sgu_buf, acts, hid, sems = refs[16:]
-    width = shared_down.shape[1]
-    units = down.shape[1]
+    units, width = down.shape[1:]
     shared = shared_down.shape[0]
-    steps = width // KSTEP
     cuts = width // NSTEP
 
-    loads = []
+    groups = [[(shared_gate, sgu_buf.at[:shared]), (shared_up, sgu_buf.at[shared:])]]
     for e in range(2):
         for source, target in ((gate, gate_buf), (up, up_buf)):
-            for k in range(steps):
-                rows = pl.ds(k * KSTEP, KSTEP)
-                loads.append((source.at[e, rows], target.at[e, rows]))
-        if e == 0:
-            loads.append((shared_gate, sgu_buf.at[:shared]))
-            loads.append((shared_up, sgu_buf.at[shared:]))
-            loads.append((shared_down, down_buf.at[2 * units :]))
+            size = width // SPLIT
+            parts = [pl.ds(i * size, size) for i in range(SPLIT)]
+            groups.append([(source.at[e, rows], target.at[e, rows]) for rows in parts])
     for n in range(cuts):
         columns = pl.ds(n * NSTEP, NSTEP)
+        group = [(shared_down, down_buf.at[2 * units :])] if n == 0 else []
         for e in range(2):
-            rows = pl.ds(e * units, units)
-            loads.append((down.at[e, :, columns], down_buf.at[rows, columns]))
+            size = 2 * units // SPLIT
+            for i in range(SPLIT // 2):
+                rows = pl.ds(e * units + i * size, size)
+                group.append(
+                    (down.at[e, pl.ds(i * size, size), columns], down_buf.at[rows, columns])
+                )
+        groups.append(group)
+    loads = [load for group in groups for load in group]
     copies = [pltpu.make_async_copy(s, t, sems.at[i]) for i, (s, t) in enumerate(loads)]
     for copy in copies[:AHEAD]:
         copy.start()
-    waited = [0]
+    waited = [0, 0]
 
     def arrived():
-        copies[waited[0]].wait()
-        if waited[0] + AHEAD < len(copies):
-            copies[waited[0] + AHEAD].start()
+        for _ in groups[waited[0]]:
+            copies[waited[1]].wait()
+            if waited[1] + AHEAD < len(copies):
+                copies[waited[1] + AHEAD].start()
+            waited[1] += 1
         waited[0] += 1
 
-    def rows_of(k, size):
-        return jnp.concatenate([p[:, k * size : (k + 1) * size] for p in pieces], axis=0)
+    def rows_of():
+        return jnp.concatenate([p[:, :width] for p in pieces], axis=0)
 
     def silu_mul(g, u):
         return g / (1.0 + jnp.exp(-g)) * u
 
     block = pl.when(first_ref[0, 0] >= 0)
 
+    arrived()
+
+    @block
+    def _():
+        both = lax.dot_general(
+            rows_of(), sgu_buf[...], (((1,), (1,)), ((), ())), preferred_element_type=jnp.float32
+        )
+        act = silu_mul(both[:, :shared], both[:, shared:])
+        hid[:, 2 * units :] = act.astype(jnp.bfloat16)
+
     for e in range(2):
-        for m, buf in enumerate((gate_buf, up_buf)):
-            for k in range(steps):
-                arrived()
-
-                @block
-                def _(e=e, m=m, k=k, buf=buf):
-                    part = jnp.dot(
-                        rows_of(k, KSTEP),
-                        buf[e, k * KSTEP : (k + 1) * KSTEP],
-                        preferred_element_type=jnp.float32,
-                    )
-                    acts[m] = part if k == 0 else acts[m] + part
-
-        if e == 0:
-            arrived()
-            arrived()
-            arrived()
+        arrived()
 
         @block
         def _(e=e):
+            acts[...] = jnp.dot(rows_of(), gate_buf[e], preferred_element_type=jnp.float32)
+
+        arrived()
+
+        @block
+        def _(e=e):
+            up_act = jnp.dot(rows_of(), up_buf[e], preferred_element_type=jnp.float32)
             weights = jnp.concatenate([p[:, width:] for p in pieces], axis=0).astype(jnp.float32)
             lane = lax.broadcasted_iota(jnp.int32, weights.shape, 1)
             mine = jnp.where(lane == first_ref[0, 0] + e, weights, 0.0)
             scale = jnp.sum(mine, axis=1, keepdims=True)
-            act = silu_mul(acts[0], acts[1]) * scale
+            act = silu_mul(acts[...], up_act) * scale
             hid[:, e * units : (e + 1) * units] = act.astype(jnp.bfloat16)
-            if e == 0:
-                dims = (((1,), (1,)), ((), ()))
-                both = None
-                for k in range(steps):
-                    part = lax.dot_general(
-                        rows_of(k, KSTEP),
-                        sgu_buf[:, k * KSTEP : (k + 1) * KSTEP],
-                        dims,
-                        preferred_element_type=jnp.float32,
-                    )
-                    both = part if both is None else both + part
-                act = silu_mul(both[:, :shared], both[:, shared:])
-                hid[:, 2 * units :] = act.astype(jnp.bfloat16)
 
     for n in range(cuts):
-        arrived()
         arrived()
 
         @block
@@ -164,9 +154,9 @@
             pltpu.VMEM(up.shape, jnp.bfloat16),
             pltpu.VMEM((2 * units + shared, width), jnp.bfloat16),
             pltpu.VMEM((2 * shared, width), jnp.bfloat16),
-            pltpu.VMEM((2, 256, units), jnp.float32),
+            pltpu.VMEM((256, units), jnp.float32),
             pltpu.VMEM((256, 2 * units + shared), jnp.bfloat16),
-            pltpu.SemaphoreType.DMA((4 * width // KSTEP + 3 + 2 * width // NSTEP,)),
+            pltpu.SemaphoreType.DMA((3 + SPLIT * (4 + width // NSTEP),)),
         ],
         compiler_params=pltpu.CompilerParams(vmem_limit_bytes=28 * 1024 * 1024),
         cost_estimate=pl.CostEstimate(
@@ -290,7 +280,7 @@
     for stage, kind in ((2, jnp.bfloat16), (1, jnp.bfloat16), (0, jnp.float32)):
         count = total.shape[0] // 4
         parts = [total[i * count : (i + 1) * count] for i in range(4)]
-        got = [send(part.astype(kind), stage, by) for part, by in zip(parts[1:], (1, 3, 2))]
+        got = [send(part.astype(kind), stage, by) for part, by in zip(parts[:0:-1], (2, 3, 1))]
         total = parts[0]
         for part in got:
             total = total + part.astype(jnp.float32)

time: 89 us -> 86 us (0.966)
  waiting for transfers between devices: 35.1 us -> 32.7 us
  Pallas kernels: 16.1 us -> 14.9 us
    ppermute x9, waiting for transfers between devices: 19.1 us -> 16.7 us  [send(): lax.ppermute(block, AXES, [(flat(p), flat(moved(p, stage, by))) for p in...]
    pallas_call x1, Pallas kernels: 11.1 us -> 9.9 us  [layer(): pl.pallas_call(layer_kernel, out_shape=(jax.ShapeDtypeStruct((128, 2 * un...]
  transfers between devices with their start and end apart: 23 -> 23, of which waited for: 16 -> 15; matrix products, arithmetic and copies ran while one was open for 0% -> 0% of each run, Pallas kernels for 5% -> 5%
where the time goes in v4:
time: 86 us; the launch traced here: 85.8 us
  starting transfers between devices  36.1 us (42%)
  waiting for transfers between devices  32.7 us (38%)
  Pallas kernels  14.9 us (17%)
  local copies, waits for them, and re-layouts  1.11 us (1%)
  other arithmetic  0.99 us (1%)
    ppermute x9, starting transfers between devices, fetch(): lax.ppermute(block, AXES, [(flat(moved(p, stage, by)), flat(p)) for p in...  20.1 us
    ppermute x9, waiting for transfers between devices, send(): lax.ppermute(block, AXES, [(flat(p), flat(moved(p, stage, by))) for p in...  16.7 us
    ppermute x9, starting transfers between devices, send(): lax.ppermute(block, AXES, [(flat(p), flat(moved(p, stage, by))) for p in...  15.8 us
    ppermute x9, waiting for transfers between devices, fetch(): lax.ppermute(block, AXES, [(flat(moved(p, stage, by)), flat(p)) for p in...  14 us
    pallas_call x1, Pallas kernels, layer(): pl.pallas_call(layer_kernel, out_shape=(jax.ShapeDtypeStruct((128, 2 * un...  9.9 us
    pallas_call x1, Pallas kernels, down_own(): pl.pallas_call(down_kernel, grid=(1,), out_shape=jax.ShapeDtypeStruct((12...  4.03 us
    ppermute x5, waiting for transfers between devices, swap(): lax.ppermute(block, AXES, [(flat(p), flat(p[:3] + (1 - p[3],))) for p in...  1.95 us
  transfers between devices with their start and end apart: 23, of which 15 were waited for; matrix products, arithmetic and copies ran while one was open for 0% of the time, Pallas kernels for 5%

profile of v4, /device:TPU:0, one launch (start us, length us, event | category | flops | bytes accessed | tf_op | source)
XLA Modules:
  0.0 85.8 jit_solution(16986255338384935805)
XLA Ops:
  0.0 0.9 %prepare.1 = bf16[2,7296]{1,0:T(2,128)(2,1)S(1)} custom-call(f32[2,1,7168]{2,1,0:T(1,128)} %hidden.1, s32[2,1,8]{2,1,0:T(1,128)} %routes.1, s32[2,1,8]{2,1,0:T(1,128)} %slots.1, bf16[2,8]{1,0:T(2,128)(2,1)} %bitcast.8), custom_call_target="tpu_custom_call" | custom-call | tf_op jit(solution)/shard_map/prepare/pallas_call | solution.py:249
  0.9 3.2 %collective-permute-start.2 = (bf16[2,7296]{1,0:T(2,128)(2,1)S(1)}, bf16[2,7296]{1,0:T(2,128)(2,1)S(1)}, u32[]{:S(2)}, u32[]{:S(2)}) collective-permute-start(bf16[2,7296]{1,0:T(2,128)(2,1)S(1)} %prepare.1), channel_id=1, source_target_pairs={{4,0},{17,1},{6,2},{19,3},{0,4},{21,5},{2,6},{23,7},{12,8},{25,9},... | collective-permute-start | bytes 87560 | tf_op jit(solution)/shard_map/ppermute | solution.py:31
  4.7 2.6 %collective-permute-start = (bf16[2,7296]{1,0:T(2,128)(2,1)S(1)}, bf16[2,7296]{1,0:T(2,128)(2,1)S(1)}, u32[]{:S(2)}, u32[]{:S(2)}) collective-permute-start(bf16[2,7296]{1,0:T(2,128)(2,1)S(1)} %prepare.1), channel_id=1, source_target_pairs={{2,0},{9,1},{4,2},{11,3},{6,4},{13,5},{0,6},{15,7},{10,8},{17,9},{... | collective-permute-start | bytes 87560 | tf_op jit(solution)/shard_map/ppermute | solution.py:31
  7.4 1.8 %collective-permute-done.1 = bf16[2,7296]{1,0:T(2,128)(2,1)S(1)} collective-permute-done((bf16[2,7296]{1,0:T(2,128)(2,1)S(1)}, bf16[2,7296]{1,0:T(2,128)(2,1)S(1)}, u32[]{:S(2)}, u32[]{:S(2)}) %collective-permute-start.1) | collective-permute-done | bytes 29216 | tf_op jit(solution)/shard_map/ppermute | solution.py:31
  9.4 3.3 %collective-permute-start.5 = (bf16[8,7296]{1,0:T(8,128)(2,1)S(1)}, bf16[8,7296]{1,0:T(8,128)(2,1)S(1)}, u32[]{:S(2)}, u32[]{:S(2)}) collective-permute-start(bf16[8,7296]{1,0:T(8,128)(2,1)S(1)} %pad_maximum_fusion), channel_id=1, source_target_pairs={{16,0},{65,1},{18,2},{67,3},{20,4},{69,5},{22,6},{71,7},{24,8},{73... | collective-permute-start | bytes 350216 | tf_op jit(solution)/shard_map/ppermute | solution.py:31
  13.3 2.6 %collective-permute-start.3 = (bf16[8,7296]{1,0:T(8,128)(2,1)S(1)}, bf16[8,7296]{1,0:T(8,128)(2,1)S(1)}, u32[]{:S(2)}, u32[]{:S(2)}) collective-permute-start(bf16[8,7296]{1,0:T(8,128)(2,1)S(1)} %pad_maximum_fusion), channel_id=1, source_target_pairs={{8,0},{33,1},{10,2},{35,3},{12,4},{37,5},{14,6},{39,7},{16,8},{41,... | collective-permute-start | bytes 350216 | tf_op jit(solution)/shard_map/ppermute | solution.py:31
  15.9 2.8 %collective-permute-done.4 = bf16[8,7296]{1,0:T(8,128)(2,1)S(1)} collective-permute-done((bf16[8,7296]{1,0:T(8,128)(2,1)S(1)}, bf16[8,7296]{1,0:T(8,128)(2,1)S(1)}, u32[]{:S(2)}, u32[]{:S(2)}) %collective-permute-start.4) | collective-permute-done | bytes 116768 | tf_op jit(solution)/shard_map/ppermute | solution.py:31
  18.9 4.0 %collective-permute-start.8 = (bf16[32,7296]{1,0:T(8,128)(2,1)S(1)}, bf16[32,7296]{1,0:T(8,128)(2,1)S(1)}, u32[]{:S(2)}, u32[]{:S(2)}) collective-permute-start(bf16[32,7296]{1,0:T(8,128)(2,1)S(1)} %concatenate.8.refs_0_), channel_id=1, source_target_pairs={{64,0},{5,1},{66,2},{7,3},{68,4},{1,5},{70,6},{3,7},{72,8},{13,9},... | collective-permute-start | bytes 1400840 | tf_op jit(solution)/shard_map/ppermute | solution.py:31
  22.8 1.0 %collective-permute-start.7 = (bf16[32,7296]{1,0:T(8,128)(2,1)S(1)}, bf16[32,7296]{1,0:T(8,128)(2,1)S(1)}, u32[]{:S(2)}, u32[]{:S(2)}) collective-permute-start(bf16[32,7296]{1,0:T(8,128)(2,1)S(1)} %concatenate.8.refs_0_), channel_id=1, source_target_pairs={{96,0},{7,1},{98,2},{1,3},{100,4},{3,5},{102,6},{5,7},{104,8},{15,... | collective-permute-start | bytes 1400840 | tf_op jit(solution)/shard_map/ppermute | solution.py:31
  23.9 2.2 %collective-permute-start.6 = (bf16[32,7296]{1,0:T(8,128)(2,1)S(1)}, bf16[32,7296]{1,0:T(8,128)(2,1)S(1)}, u32[]{:S(2)}, u32[]{:S(2)}) collective-permute-start(bf16[32,7296]{1,0:T(8,128)(2,1)S(1)} %concatenate.8.refs_0_), channel_id=1, source_target_pairs={{32,0},{3,1},{34,2},{5,3},{36,4},{7,5},{38,6},{1,7},{40,8},{11,9},... | collective-permute-start | bytes 1400840 | tf_op jit(solution)/shard_map/ppermute | solution.py:31
  26.1 3.4 %collective-permute-done.8.refs_3_ = bf16[32,7296]{1,0:T(8,128)(2,1)S(1)} collective-permute-done((bf16[32,7296]{1,0:T(8,128)(2,1)S(1)}, bf16[32,7296]{1,0:T(8,128)(2,1)S(1)}, u32[]{:S(2)}, u32[]{:S(2)}) %collective-permute-start.8) | collective-permute-done | bytes 466976 | tf_op jit(solution)/shard_map/ppermute | solution.py:31
  29.5 4.9 %collective-permute-done.7.refs_2_ = bf16[32,7296]{1,0:T(8,128)(2,1)S(1)} collective-permute-done((bf16[32,7296]{1,0:T(8,128)(2,1)S(1)}, bf16[32,7296]{1,0:T(8,128)(2,1)S(1)}, u32[]{:S(2)}, u32[]{:S(2)}) %collective-permute-start.7) | collective-permute-done | bytes 466976 | tf_op jit(solution)/shard_map/ppermute | solution.py:31
  34.4 1.1 %collective-permute-done.6.refs_1_ = bf16[32,7296]{1,0:T(8,128)(2,1)S(1)} collective-permute-done((bf16[32,7296]{1,0:T(8,128)(2,1)S(1)}, bf16[32,7296]{1,0:T(8,128)(2,1)S(1)}, u32[]{:S(2)}, u32[]{:S(2)}) %collective-permute-start.6) | collective-permute-done | bytes 466976 | tf_op jit(solution)/shard_map/ppermute | solution.py:31
  35.5 0.8 collective-permute-done.11.refs_6_
  36.2 1.2 %collective-permute-done.10.refs_5_ = bf16[32,7296]{1,0:T(8,128)(2,1)} collective-permute-done((bf16[32,7296]{1,0:T(8,128)(2,1)S(1)}, bf16[32,7296]{1,0:T(8,128)(2,1)}, u32[]{:S(2)}, u32[]{:S(2)}) %collective-permute-start.10) | collective-permute-done | bytes 466976 | tf_op jit(solution)/shard_map/ppermute | solution.py:39
  37.4 9.9 %layer.1 = (bf16[128,528]{1,0:T(8,128)(2,1)S(1)}, bf16[128,7168]{1,0:T(8,128)(2,1)S(1)}) custom-call(s32[1,1]{1,0:T(1,128)} %bitcast.first_ref, bf16[32,7296]{1,0:T(8,128)(2,1)S(1)} %concatenate.8.refs_0_, bf16[32,7296]{1,0:T(8,128)(2,1)S(1)} %collective-permute-done.6.refs_1_, bf16[32,7296]{1,0:T(8,128)(2,1)S(1)} %collective-permute-done.7.refs_2_, ...), custom_call_target="tpu_custom_call" | custom-call | flops 5813305344 | bytes 31883264 | tf_op jit(solution)/shard_map/layer/pallas_call | solution.py:142
  47.5 4.0 %down.2 = f32[128,7168]{1,0:T(8,128)S(1)} custom-call(bf16[128,528]{1,0:T(8,128)(2,1)S(1)} %get-tuple-element.7.hid, bf16[2,256,7168]{2,1,0:T(8,128)(2,1)} %down.3, bf16[16,7168]{1,0:T(8,128)(2,1)} %shared_down.1), custom_call_target="tpu_custom_call" | custom-call | flops 968884224 | bytes 11239424 | tf_op jit(solution)/shard_map/down/pallas_call | solution.py:214
  52.3 3.0 %collective-permute-start.14 = (bf16[32,7168]{1,0:T(8,128)(2,1)S(1)}, bf16[32,7168]{1,0:T(8,128)(2,1)S(1)}, u32[]{:S(2)}, u32[]{:S(2)}) collective-permute-start(bf16[32,7168]{1,0:T(8,128)(2,1)S(1)} %get-tuple-element.13), channel_id=1, source_target_pairs={{0,64},{1,5},{2,66},{3,7},{4,68},{5,1},{6,70},{7,3},{8,72},{9,13},... | collective-permute-start | bytes 1376264 | tf_op jit(solution)/shard_map/ppermute | solution.py:35
  55.2 0.8 collective-permute-start.16
  56.0 2.4 %collective-permute-start.15 = (bf16[32,7168]{1,0:T(8,128)(2,1)S(1)}, bf16[32,7168]{1,0:T(8,128)(2,1)S(1)}, u32[]{:S(2)}, u32[]{:S(2)}) collective-permute-start(bf16[32,7168]{1,0:T(8,128)(2,1)S(1)} %get-tuple-element.15), channel_id=1, source_target_pairs={{0,96},{1,7},{2,98},{3,1},{4,100},{5,3},{6,102},{7,5},{8,104},{9,1... | collective-permute-start | bytes 1376264 | tf_op jit(solution)/shard_map/ppermute | solution.py:35
  58.4 4.2 %collective-permute-done.14 = bf16[32,7168]{1,0:T(8,128)(2,1)S(1)} collective-permute-done((bf16[32,7168]{1,0:T(8,128)(2,1)S(1)}, bf16[32,7168]{1,0:T(8,128)(2,1)S(1)}, u32[]{:S(2)}, u32[]{:S(2)}) %collective-permute-start.14) | collective-permute-done | bytes 458784 | tf_op jit(solution)/shard_map/ppermute | solution.py:35
  62.6 4.8 %collective-permute-done.16 = bf16[32,7168]{1,0:T(8,128)(2,1)S(1)} collective-permute-done((bf16[32,7168]{1,0:T(8,128)(2,1)S(1)}, bf16[32,7168]{1,0:T(8,128)(2,1)S(1)}, u32[]{:S(2)}, u32[]{:S(2)}) %collective-permute-start.16) | collective-permute-done | bytes 458784 | tf_op jit(solution)/shard_map/ppermute | solution.py:35
  67.7 1.5 %collective-permute-start.17 = (bf16[8,7168]{1,0:T(8,128)(2,1)S(1)}, bf16[8,7168]{1,0:T(8,128)(2,1)S(1)}, u32[]{:S(2)}, u32[]{:S(2)}) collective-permute-start(bf16[8,7168]{1,0:T(8,128)(2,1)S(1)} %get-tuple-element.16), channel_id=1, source_target_pairs={{0,16},{1,65},{2,18},{3,67},{4,20},{5,69},{6,22},{7,71},{8,24},{9,... | collective-permute-start | bytes 344072 | tf_op jit(solution)/shard_map/ppermute | solution.py:35
  69.2 2.6 %collective-permute-start.19 = (bf16[8,7168]{1,0:T(8,128)(2,1)S(1)}, bf16[8,7168]{1,0:T(8,128)(2,1)S(1)}, u32[]{:S(2)}, u32[]{:S(2)}) collective-permute-start(bf16[8,7168]{1,0:T(8,128)(2,1)S(1)} %get-tuple-element.17), channel_id=1, source_target_pairs={{0,8},{1,33},{2,10},{3,35},{4,12},{5,37},{6,14},{7,39},{8,16},{9,4... | collective-permute-start | bytes 344072 | tf_op jit(solution)/shard_map/ppermute | solution.py:35
  72.4 1.6 %collective-permute-done.17 = bf16[8,7168]{1,0:T(8,128)(2,1)S(1)} collective-permute-done((bf16[8,7168]{1,0:T(8,128)(2,1)S(1)}, bf16[8,7168]{1,0:T(8,128)(2,1)S(1)}, u32[]{:S(2)}, u32[]{:S(2)}) %collective-permute-start.17) | collective-permute-done | bytes 114720 | tf_op jit(solution)/shard_map/ppermute | solution.py:35
  74.0 1.2 %collective-permute-done.19 = bf16[8,7168]{1,0:T(8,128)(2,1)S(1)} collective-permute-done((bf16[8,7168]{1,0:T(8,128)(2,1)S(1)}, bf16[8,7168]{1,0:T(8,128)(2,1)S(1)}, u32[]{:S(2)}, u32[]{:S(2)}) %collective-permute-start.19) | collective-permute-done | bytes 114720 | tf_op jit(solution)/shard_map/ppermute | solution.py:35
  75.3 1.4 %collective-permute-done.18 = bf16[8,7168]{1,0:T(8,128)(2,1)S(1)} collective-permute-done((bf16[8,7168]{1,0:T(8,128)(2,1)S(1)}, bf16[8,7168]{1,0:T(8,128)(2,1)S(1)}, u32[]{:S(2)}, u32[]{:S(2)}) %collective-permute-start.18) | collective-permute-done | bytes 114720 | tf_op jit(solution)/shard_map/ppermute | solution.py:35
  76.8 1.5 %collective-permute-start.20 = (f32[2,7168]{1,0:T(2,128)S(1)}, f32[2,7168]{1,0:T(2,128)S(1)}, u32[]{:S(2)}, u32[]{:S(2)}) collective-permute-start(f32[2,7168]{1,0:T(2,128)S(1)} %get-tuple-element.19), channel_id=1, source_target_pairs={{0,4},{1,17},{2,6},{3,19},{4,0},{5,21},{6,2},{7,23},{8,12},{9,25},... | collective-permute-start | bytes 172040 | tf_op jit(solution)/shard_map/ppermute | solution.py:35
  78.3 2.6 %collective-permute-start.22 = (f32[2,7168]{1,0:T(2,128)S(1)}, f32[2,7168]{1,0:T(2,128)S(1)}, u32[]{:S(2)}, u32[]{:S(2)}) collective-permute-start(f32[2,7168]{1,0:T(2,128)S(1)} %get-tuple-element.20), channel_id=1, source_target_pairs={{0,2},{1,9},{2,4},{3,11},{4,6},{5,13},{6,0},{7,15},{8,10},{9,17},{... | collective-permute-start | bytes 172040 | tf_op jit(solution)/shard_map/ppermute | solution.py:35
  81.5 1.0 %collective-permute-done.20 = f32[2,7168]{1,0:T(2,128)S(1)} collective-permute-done((f32[2,7168]{1,0:T(2,128)S(1)}, f32[2,7168]{1,0:T(2,128)S(1)}, u32[]{:S(2)}, u32[]{:S(2)}) %collective-permute-start.20) | collective-permute-done | bytes 57376 | tf_op jit(solution)/shard_map/ppermute | solution.py:35
  82.5 1.2 %collective-permute-done.22 = f32[2,7168]{1,0:T(2,128)S(1)} collective-permute-done((f32[2,7168]{1,0:T(2,128)S(1)}, f32[2,7168]{1,0:T(2,128)S(1)}, u32[]{:S(2)}, u32[]{:S(2)}) %collective-permute-start.22) | collective-permute-done | bytes 57376 | tf_op jit(solution)/shard_map/ppermute | solution.py:35
  83.7 1.4 %collective-permute-done.21 = f32[2,7168]{1,0:T(2,128)S(1)} collective-permute-done((f32[2,7168]{1,0:T(2,128)S(1)}, f32[2,7168]{1,0:T(2,128)S(1)}, u32[]{:S(2)}, u32[]{:S(2)}) %collective-permute-start.21) | collective-permute-done | bytes 57376 | tf_op jit(solution)/shard_map/ppermute | solution.py:35
  (27 shorter events, 4.8 us)
Async XLA Ops:
  0.9 6.4 %collective-permute-start.2 = (bf16[2,7296]{1,0:T(2,128)(2,1)S(1)}, bf16[2,7296]{1,0:T(2,128)(2,1)S(1)}, u32[]{:S(2)}, u32[]{:S(2)}) collective-permute-start(bf16[2,7296]{1,0:T(2,128)(2,1)S(1)} %prepare.1), channel_id=1, source_target_pairs={{4,0},{17,1},{6,2},{19,3},{0,4},{21,5},{2,6},{23,7},{12,8},{25,9},... | collective-permute-start | bytes 87560 | tf_op jit(solution)/shard_map/ppermute | solution.py:31
  4.1 5.1 %collective-permute-start.1 = (bf16[2,7296]{1,0:T(2,128)(2,1)S(1)}, bf16[2,7296]{1,0:T(2,128)(2,1)S(1)}, u32[]{:S(2)}, u32[]{:S(2)}) collective-permute-start(bf16[2,7296]{1,0:T(2,128)(2,1)S(1)} %prepare.1), channel_id=1, source_target_pairs={{6,0},{25,1},{0,2},{27,3},{2,4},{29,5},{4,6},{31,7},{14,8},{1,9},{... | collective-permute-start | bytes 87560 | tf_op jit(solution)/shard_map/ppermute | solution.py:31
  4.7 4.5 %collective-permute-start = (bf16[2,7296]{1,0:T(2,128)(2,1)S(1)}, bf16[2,7296]{1,0:T(2,128)(2,1)S(1)}, u32[]{:S(2)}, u32[]{:S(2)}) collective-permute-start(bf16[2,7296]{1,0:T(2,128)(2,1)S(1)} %prepare.1), channel_id=1, source_target_pairs={{2,0},{9,1},{4,2},{11,3},{6,4},{13,5},{0,6},{15,7},{10,8},{17,9},{... | collective-permute-start | bytes 87560 | tf_op jit(solution)/shard_map/ppermute | solution.py:31
  9.4 6.5 %collective-permute-start.5 = (bf16[8,7296]{1,0:T(8,128)(2,1)S(1)}, bf16[8,7296]{1,0:T(8,128)(2,1)S(1)}, u32[]{:S(2)}, u32[]{:S(2)}) collective-permute-start(bf16[8,7296]{1,0:T(8,128)(2,1)S(1)} %pad_maximum_fusion), channel_id=1, source_target_pairs={{16,0},{65,1},{18,2},{67,3},{20,4},{69,5},{22,6},{71,7},{24,8},{73... | collective-permute-start | bytes 350216 | tf_op jit(solution)/shard_map/ppermute | solution.py:31
  12.6 6.0 %collective-permute-start.4 = (bf16[8,7296]{1,0:T(8,128)(2,1)S(1)}, bf16[8,7296]{1,0:T(8,128)(2,1)S(1)}, u32[]{:S(2)}, u32[]{:S(2)}) collective-permute-start(bf16[8,7296]{1,0:T(8,128)(2,1)S(1)} %pad_maximum_fusion), channel_id=1, source_target_pairs={{24,0},{97,1},{26,2},{99,3},{28,4},{101,5},{30,6},{103,7},{0,8},{1... | collective-permute-start | bytes 350216 | tf_op jit(solution)/shard_map/ppermute | solution.py:31
  13.3 5.3 %collective-permute-start.3 = (bf16[8,7296]{1,0:T(8,128)(2,1)S(1)}, bf16[8,7296]{1,0:T(8,128)(2,1)S(1)}, u32[]{:S(2)}, u32[]{:S(2)}) collective-permute-start(bf16[8,7296]{1,0:T(8,128)(2,1)S(1)} %pad_maximum_fusion), channel_id=1, source_target_pairs={{8,0},{33,1},{10,2},{35,3},{12,4},{37,5},{14,6},{39,7},{16,8},{41,... | collective-permute-start | bytes 350216 | tf_op jit(solution)/shard_map/ppermute | solution.py:31
  18.9 10.6 %collective-permute-start.8 = (bf16[32,7296]{1,0:T(8,128)(2,1)S(1)}, bf16[32,7296]{1,0:T(8,128)(2,1)S(1)}, u32[]{:S(2)}, u32[]{:S(2)}) collective-permute-start(bf16[32,7296]{1,0:T(8,128)(2,1)S(1)} %concatenate.8.refs_0_), channel_id=1, source_target_pairs={{64,0},{5,1},{66,2},{7,3},{68,4},{1,5},{70,6},{3,7},{72,8},{13,9},... | collective-permute-start | bytes 1400840 | tf_op jit(solution)/shard_map/ppermute | solution.py:31
  22.8 11.5 %collective-permute-start.7 = (bf16[32,7296]{1,0:T(8,128)(2,1)S(1)}, bf16[32,7296]{1,0:T(8,128)(2,1)S(1)}, u32[]{:S(2)}, u32[]{:S(2)}) collective-permute-start(bf16[32,7296]{1,0:T(8,128)(2,1)S(1)} %concatenate.8.refs_0_), channel_id=1, source_target_pairs={{96,0},{7,1},{98,2},{1,3},{100,4},{3,5},{102,6},{5,7},{104,8},{15,... | collective-permute-start | bytes 1400840 | tf_op jit(solution)/shard_map/ppermute | solution.py:31
  23.9 11.6 %collective-permute-start.6 = (bf16[32,7296]{1,0:T(8,128)(2,1)S(1)}, bf16[32,7296]{1,0:T(8,128)(2,1)S(1)}, u32[]{:S(2)}, u32[]{:S(2)}) collective-permute-start(bf16[32,7296]{1,0:T(8,128)(2,1)S(1)} %concatenate.8.refs_0_), channel_id=1, source_target_pairs={{32,0},{3,1},{34,2},{5,3},{36,4},{7,5},{38,6},{1,7},{40,8},{11,9},... | collective-permute-start | bytes 1400840 | tf_op jit(solution)/shard_map/ppermute | solution.py:31
  26.1 9.4 %collective-permute-start.9 = (bf16[32,7296]{1,0:T(8,128)(2,1)S(1)}, bf16[32,7296]{1,0:T(8,128)(2,1)S(1)}, u32[]{:S(2)}, u32[]{:S(2)}) collective-permute-start(bf16[32,7296]{1,0:T(8,128)(2,1)S(1)} %concatenate.8.refs_0_), channel_id=1, source_target_pairs={{0,1},{1,0},{2,3},{3,2},{4,5},{5,4},{6,7},{7,6},{8,9},{9,8},{10,11... | collective-permute-start | bytes 1400840 | tf_op jit(solution)/shard_map/ppermute | solution.py:39
  29.5 6.0 %collective-permute-start.12 = (bf16[32,7296]{1,0:T(8,128)(2,1)S(1)}, bf16[32,7296]{1,0:T(8,128)(2,1)S(1)}, u32[]{:S(2)}, u32[]{:S(2)}) collective-permute-start(bf16[32,7296]{1,0:T(8,128)(2,1)S(1)} %collective-permute-done.8.refs_3_), channel_id=1, source_target_pairs={{0,1},{1,0},{2,3},{3,2},{4,5},{5,4},{6,7},{7,6},{8,9},{9,8},{10,11... | collective-permute-start | bytes 1400840 | tf_op jit(solution)/shard_map/ppermute | solution.py:39
  34.4 1.8 %collective-permute-start.11 = (bf16[32,7296]{1,0:T(8,128)(2,1)S(1)}, bf16[32,7296]{1,0:T(8,128)(2,1)S(1)}, u32[]{:S(2)}, u32[]{:S(2)}) collective-permute-start(bf16[32,7296]{1,0:T(8,128)(2,1)S(1)} %collective-permute-done.7.refs_2_), channel_id=1, source_target_pairs={{0,1},{1,0},{2,3},{3,2},{4,5},{5,4},{6,7},{7,6},{8,9},{9,8},{10,11... | collective-permute-start | bytes 1400840 | tf_op jit(solution)/shard_map/ppermute | solution.py:39
  35.5 2.0 %collective-permute-start.10 = (bf16[32,7296]{1,0:T(8,128)(2,1)S(1)}, bf16[32,7296]{1,0:T(8,128)(2,1)}, u32[]{:S(2)}, u32[]{:S(2)}) collective-permute-start(bf16[32,7296]{1,0:T(8,128)(2,1)S(1)} %collective-permute-done.6.refs_1_), channel_id=1, source_target_pairs={{0,1},{1,0},{2,3},{3,2},{4,5},{5,4},{6,7},{7,6},{8,9},{9,8},{10,11... | collective-permute-start | bytes 1400840 | tf_op jit(solution)/shard_map/ppermute | solution.py:39
  47.3 4.3 %collective-permute-start.13 = (bf16[128,7168]{1,0:T(8,128)(2,1)S(1)}, bf16[128,7168]{1,0:T(8,128)(2,1)S(1)}, u32[]{:S(2)}, u32[]{:S(2)}) collective-permute-start(bf16[128,7168]{1,0:T(8,128)(2,1)S(1)} %get-tuple-element.8), channel_id=1, source_target_pairs={{0,1},{1,0},{2,3},{3,2},{4,5},{5,4},{6,7},{7,6},{8,9},{9,8},{10,11... | collective-permute-start | bytes 5505032 | tf_op jit(solution)/shard_map/ppermute | solution.py:39
  52.3 10.3 %collective-permute-start.14 = (bf16[32,7168]{1,0:T(8,128)(2,1)S(1)}, bf16[32,7168]{1,0:T(8,128)(2,1)S(1)}, u32[]{:S(2)}, u32[]{:S(2)}) collective-permute-start(bf16[32,7168]{1,0:T(8,128)(2,1)S(1)} %get-tuple-element.13), channel_id=1, source_target_pairs={{0,64},{1,5},{2,66},{3,7},{4,68},{5,1},{6,70},{7,3},{8,72},{9,13},... | collective-permute-start | bytes 1376264 | tf_op jit(solution)/shard_map/ppermute | solution.py:35
  55.2 12.2 %collective-permute-start.16 = (bf16[32,7168]{1,0:T(8,128)(2,1)S(1)}, bf16[32,7168]{1,0:T(8,128)(2,1)S(1)}, u32[]{:S(2)}, u32[]{:S(2)}) collective-permute-start(bf16[32,7168]{1,0:T(8,128)(2,1)S(1)} %get-tuple-element.14), channel_id=1, source_target_pairs={{0,32},{1,3},{2,34},{3,5},{4,36},{5,7},{6,38},{7,1},{8,40},{9,11},... | collective-permute-start | bytes 1376264 | tf_op jit(solution)/shard_map/ppermute | solution.py:35
  56.0 11.4 %collective-permute-start.15 = (bf16[32,7168]{1,0:T(8,128)(2,1)S(1)}, bf16[32,7168]{1,0:T(8,128)(2,1)S(1)}, u32[]{:S(2)}, u32[]{:S(2)}) collective-permute-start(bf16[32,7168]{1,0:T(8,128)(2,1)S(1)} %get-tuple-element.15), channel_id=1, source_target_pairs={{0,96},{1,7},{2,98},{3,1},{4,100},{5,3},{6,102},{7,5},{8,104},{9,1... | collective-permute-start | bytes 1376264 | tf_op jit(solution)/shard_map/ppermute | solution.py:35
  67.7 6.4 %collective-permute-start.17 = (bf16[8,7168]{1,0:T(8,128)(2,1)S(1)}, bf16[8,7168]{1,0:T(8,128)(2,1)S(1)}, u32[]{:S(2)}, u32[]{:S(2)}) collective-permute-start(bf16[8,7168]{1,0:T(8,128)(2,1)S(1)} %get-tuple-element.16), channel_id=1, source_target_pairs={{0,16},{1,65},{2,18},{3,67},{4,20},{5,69},{6,22},{7,71},{8,24},{9,... | collective-permute-start | bytes 344072 | tf_op jit(solution)/shard_map/ppermute | solution.py:35
  69.2 6.1 %collective-permute-start.19 = (bf16[8,7168]{1,0:T(8,128)(2,1)S(1)}, bf16[8,7168]{1,0:T(8,128)(2,1)S(1)}, u32[]{:S(2)}, u32[]{:S(2)}) collective-permute-start(bf16[8,7168]{1,0:T(8,128)(2,1)S(1)} %get-tuple-element.17), channel_id=1, source_target_pairs={{0,8},{1,33},{2,10},{3,35},{4,12},{5,37},{6,14},{7,39},{8,16},{9,4... | collective-permute-start | bytes 344072 | tf_op jit(solution)/shard_map/ppermute | solution.py:35
  71.8 4.8 %collective-permute-start.18 = (bf16[8,7168]{1,0:T(8,128)(2,1)S(1)}, bf16[8,7168]{1,0:T(8,128)(2,1)S(1)}, u32[]{:S(2)}, u32[]{:S(2)}) collective-permute-start(bf16[8,7168]{1,0:T(8,128)(2,1)S(1)} %get-tuple-element.18), channel_id=1, source_target_pairs={{0,24},{1,97},{2,26},{3,99},{4,28},{5,101},{6,30},{7,103},{8,0},{9... | collective-permute-start | bytes 344072 | tf_op jit(solution)/shard_map/ppermute | solution.py:35
  76.8 5.8 %collective-permute-start.20 = (f32[2,7168]{1,0:T(2,128)S(1)}, f32[2,7168]{1,0:T(2,128)S(1)}, u32[]{:S(2)}, u32[]{:S(2)}) collective-permute-start(f32[2,7168]{1,0:T(2,128)S(1)} %get-tuple-element.19), channel_id=1, source_target_pairs={{0,4},{1,17},{2,6},{3,19},{4,0},{5,21},{6,2},{7,23},{8,12},{9,25},... | collective-permute-start | bytes 172040 | tf_op jit(solution)/shard_map/ppermute | solution.py:35
  78.3 5.4 %collective-permute-start.22 = (f32[2,7168]{1,0:T(2,128)S(1)}, f32[2,7168]{1,0:T(2,128)S(1)}, u32[]{:S(2)}, u32[]{:S(2)}) collective-permute-start(f32[2,7168]{1,0:T(2,128)S(1)} %get-tuple-element.20), channel_id=1, source_target_pairs={{0,2},{1,9},{2,4},{3,11},{4,6},{5,13},{6,0},{7,15},{8,10},{9,17},{... | collective-permute-start | bytes 172040 | tf_op jit(solution)/shard_map/ppermute | solution.py:35
  80.9 4.2 %collective-permute-start.21 = (f32[2,7168]{1,0:T(2,128)S(1)}, f32[2,7168]{1,0:T(2,128)S(1)}, u32[]{:S(2)}, u32[]{:S(2)}) collective-permute-start(f32[2,7168]{1,0:T(2,128)S(1)} %get-tuple-element.21), channel_id=1, source_target_pairs={{0,6},{1,25},{2,0},{3,27},{4,2},{5,29},{6,4},{7,31},{8,14},{9,1},{... | collective-permute-start | bytes 172040 | tf_op jit(solution)/shard_map/ppermute | solution.py:35

commit v5 on v4

--- a/solution.py
+++ b/solution.py
@@ -277,7 +277,7 @@
     )
     other = swap(other)
     total = down_own(kept, expert_down, shared_down) + other.astype(jnp.float32)
-    for stage, kind in ((2, jnp.bfloat16), (1, jnp.bfloat16), (0, jnp.float32)):
+    for stage, kind in ((2, jnp.bfloat16), (1, jnp.bfloat16), (0, jnp.bfloat16)):
         count = total.shape[0] // 4
         parts = [total[i * count : (i + 1) * count] for i in range(4)]
         got = [send(part.astype(kind), stage, by) for part, by in zip(parts[:0:-1], (2, 3, 1))]

time: 86 us -> 85.8 us (level)
  no operation moved by 1% of the time
where the time goes in v5:
time: 85.8 us; the launch traced here: 85.5 us
  starting transfers between devices  36.1 us (42%)
  waiting for transfers between devices  32.4 us (38%)
  Pallas kernels  14.9 us (17%)
  local copies, waits for them, and re-layouts  1.12 us (1%)
  other arithmetic  1 us (1%)
    ppermute x9, starting transfers between devices, fetch(): lax.ppermute(block, AXES, [(flat(moved(p, stage, by)), flat(p)) for p in...  20.1 us
    ppermute x9, waiting for transfers between devices, send(): lax.ppermute(block, AXES, [(flat(p), flat(moved(p, stage, by))) for p in...  16.4 us
    ppermute x9, starting transfers between devices, send(): lax.ppermute(block, AXES, [(flat(p), flat(moved(p, stage, by))) for p in...  15.8 us
    ppermute x9, waiting for transfers between devices, fetch(): lax.ppermute(block, AXES, [(flat(moved(p, stage, by)), flat(p)) for p in...  14 us
    pallas_call x1, Pallas kernels, layer(): pl.pallas_call(layer_kernel, out_shape=(jax.ShapeDtypeStruct((128, 2 * un...  9.9 us
    pallas_call x1, Pallas kernels, down_own(): pl.pallas_call(down_kernel, grid=(1,), out_shape=jax.ShapeDtypeStruct((12...  4.03 us
    ppermute x5, waiting for transfers between devices, swap(): lax.ppermute(block, AXES, [(flat(p), flat(p[:3] + (1 - p[3],))) for p in...  1.95 us
  transfers between devices with their start and end apart: 23, of which 15 were waited for; matrix products, arithmetic and copies ran while one was open for 0% of the time, Pallas kernels for 5%

profile of v5, /device:TPU:0, one launch (start us, length us, event | category | flops | bytes accessed | tf_op | source)
XLA Modules:
  0.0 85.5 jit_solution(11471754737336616115)
XLA Ops:
  0.0 0.9 %prepare.1 = bf16[2,7296]{1,0:T(2,128)(2,1)S(1)} custom-call(f32[2,1,7168]{2,1,0:T(1,128)} %hidden.1, s32[2,1,8]{2,1,0:T(1,128)} %routes.1, s32[2,1,8]{2,1,0:T(1,128)} %slots.1, bf16[2,8]{1,0:T(2,128)(2,1)} %bitcast.8), custom_call_target="tpu_custom_call" | custom-call | tf_op jit(solution)/shard_map/prepare/pallas_call | solution.py:249
  0.9 3.2 %collective-permute-start.2 = (bf16[2,7296]{1,0:T(2,128)(2,1)S(1)}, bf16[2,7296]{1,0:T(2,128)(2,1)S(1)}, u32[]{:S(2)}, u32[]{:S(2)}) collective-permute-start(bf16[2,7296]{1,0:T(2,128)(2,1)S(1)} %prepare.1), channel_id=1, source_target_pairs={{4,0},{17,1},{6,2},{19,3},{0,4},{21,5},{2,6},{23,7},{12,8},{25,9},... | collective-permute-start | bytes 87560 | tf_op jit(solution)/shard_map/ppermute | solution.py:31
  4.7 2.6 %collective-permute-start = (bf16[2,7296]{1,0:T(2,128)(2,1)S(1)}, bf16[2,7296]{1,0:T(2,128)(2,1)S(1)}, u32[]{:S(2)}, u32[]{:S(2)}) collective-permute-start(bf16[2,7296]{1,0:T(2,128)(2,1)S(1)} %prepare.1), channel_id=1, source_target_pairs={{2,0},{9,1},{4,2},{11,3},{6,4},{13,5},{0,6},{15,7},{10,8},{17,9},{... | collective-permute-start | bytes 87560 | tf_op jit(solution)/shard_map/ppermute | solution.py:31
  7.4 1.8 %collective-permute-done.1 = bf16[2,7296]{1,0:T(2,128)(2,1)S(1)} collective-permute-done((bf16[2,7296]{1,0:T(2,128)(2,1)S(1)}, bf16[2,7296]{1,0:T(2,128)(2,1)S(1)}, u32[]{:S(2)}, u32[]{:S(2)}) %collective-permute-start.1) | collective-permute-done | bytes 29216 | tf_op jit(solution)/shard_map/ppermute | solution.py:31
  9.4 3.3 %collective-permute-start.5 = (bf16[8,7296]{1,0:T(8,128)(2,1)S(1)}, bf16[8,7296]{1,0:T(8,128)(2,1)S(1)}, u32[]{:S(2)}, u32[]{:S(2)}) collective-permute-start(bf16[8,7296]{1,0:T(8,128)(2,1)S(1)} %pad_maximum_fusion), channel_id=1, source_target_pairs={{16,0},{65,1},{18,2},{67,3},{20,4},{69,5},{22,6},{71,7},{24,8},{73... | collective-permute-start | bytes 350216 | tf_op jit(solution)/shard_map/ppermute | solution.py:31
  13.3 2.6 %collective-permute-start.3 = (bf16[8,7296]{1,0:T(8,128)(2,1)S(1)}, bf16[8,7296]{1,0:T(8,128)(2,1)S(1)}, u32[]{:S(2)}, u32[]{:S(2)}) collective-permute-start(bf16[8,7296]{1,0:T(8,128)(2,1)S(1)} %pad_maximum_fusion), channel_id=1, source_target_pairs={{8,0},{33,1},{10,2},{35,3},{12,4},{37,5},{14,6},{39,7},{16,8},{41,... | collective-permute-start | bytes 350216 | tf_op jit(solution)/shard_map/ppermute | solution.py:31
  15.9 2.8 %collective-permute-done.4 = bf16[8,7296]{1,0:T(8,128)(2,1)S(1)} collective-permute-done((bf16[8,7296]{1,0:T(8,128)(2,1)S(1)}, bf16[8,7296]{1,0:T(8,128)(2,1)S(1)}, u32[]{:S(2)}, u32[]{:S(2)}) %collective-permute-start.4) | collective-permute-done | bytes 116768 | tf_op jit(solution)/shard_map/ppermute | solution.py:31
  18.9 4.0 %collective-permute-start.8 = (bf16[32,7296]{1,0:T(8,128)(2,1)S(1)}, bf16[32,7296]{1,0:T(8,128)(2,1)S(1)}, u32[]{:S(2)}, u32[]{:S(2)}) collective-permute-start(bf16[32,7296]{1,0:T(8,128)(2,1)S(1)} %concatenate.8.refs_0_), channel_id=1, source_target_pairs={{64,0},{5,1},{66,2},{7,3},{68,4},{1,5},{70,6},{3,7},{72,8},{13,9},... | collective-permute-start | bytes 1400840 | tf_op jit(solution)/shard_map/ppermute | solution.py:31
  22.8 1.0 %collective-permute-start.7 = (bf16[32,7296]{1,0:T(8,128)(2,1)S(1)}, bf16[32,7296]{1,0:T(8,128)(2,1)S(1)}, u32[]{:S(2)}, u32[]{:S(2)}) collective-permute-start(bf16[32,7296]{1,0:T(8,128)(2,1)S(1)} %concatenate.8.refs_0_), channel_id=1, source_target_pairs={{96,0},{7,1},{98,2},{1,3},{100,4},{3,5},{102,6},{5,7},{104,8},{15,... | collective-permute-start | bytes 1400840 | tf_op jit(solution)/shard_map/ppermute | solution.py:31
  23.9 2.2 %collective-permute-start.6 = (bf16[32,7296]{1,0:T(8,128)(2,1)S(1)}, bf16[32,7296]{1,0:T(8,128)(2,1)S(1)}, u32[]{:S(2)}, u32[]{:S(2)}) collective-permute-start(bf16[32,7296]{1,0:T(8,128)(2,1)S(1)} %concatenate.8.refs_0_), channel_id=1, source_target_pairs={{32,0},{3,1},{34,2},{5,3},{36,4},{7,5},{38,6},{1,7},{40,8},{11,9},... | collective-permute-start | bytes 1400840 | tf_op jit(solution)/shard_map/ppermute | solution.py:31
  26.1 3.4 %collective-permute-done.8.refs_3_ = bf16[32,7296]{1,0:T(8,128)(2,1)S(1)} collective-permute-done((bf16[32,7296]{1,0:T(8,128)(2,1)S(1)}, bf16[32,7296]{1,0:T(8,128)(2,1)S(1)}, u32[]{:S(2)}, u32[]{:S(2)}) %collective-permute-start.8) | collective-permute-done | bytes 466976 | tf_op jit(solution)/shard_map/ppermute | solution.py:31
  29.5 4.9 %collective-permute-done.7.refs_2_ = bf16[32,7296]{1,0:T(8,128)(2,1)S(1)} collective-permute-done((bf16[32,7296]{1,0:T(8,128)(2,1)S(1)}, bf16[32,7296]{1,0:T(8,128)(2,1)S(1)}, u32[]{:S(2)}, u32[]{:S(2)}) %collective-permute-start.7) | collective-permute-done | bytes 466976 | tf_op jit(solution)/shard_map/ppermute | solution.py:31
  34.4 1.1 %collective-permute-done.6.refs_1_ = bf16[32,7296]{1,0:T(8,128)(2,1)S(1)} collective-permute-done((bf16[32,7296]{1,0:T(8,128)(2,1)S(1)}, bf16[32,7296]{1,0:T(8,128)(2,1)S(1)}, u32[]{:S(2)}, u32[]{:S(2)}) %collective-permute-start.6) | collective-permute-done | bytes 466976 | tf_op jit(solution)/shard_map/ppermute | solution.py:31
  35.5 0.8 collective-permute-done.11.refs_6_
  36.2 1.2 %collective-permute-done.10.refs_5_ = bf16[32,7296]{1,0:T(8,128)(2,1)} collective-permute-done((bf16[32,7296]{1,0:T(8,128)(2,1)S(1)}, bf16[32,7296]{1,0:T(8,128)(2,1)}, u32[]{:S(2)}, u32[]{:S(2)}) %collective-permute-start.10) | collective-permute-done | bytes 466976 | tf_op jit(solution)/shard_map/ppermute | solution.py:39
  37.4 9.9 %layer.1 = (bf16[128,528]{1,0:T(8,128)(2,1)S(1)}, bf16[128,7168]{1,0:T(8,128)(2,1)S(1)}) custom-call(s32[1,1]{1,0:T(1,128)} %bitcast.first_ref, bf16[32,7296]{1,0:T(8,128)(2,1)S(1)} %concatenate.8.refs_0_, bf16[32,7296]{1,0:T(8,128)(2,1)S(1)} %collective-permute-done.6.refs_1_, bf16[32,7296]{1,0:T(8,128)(2,1)S(1)} %collective-permute-done.7.refs_2_, ...), custom_call_target="tpu_custom_call" | custom-call | flops 5813305344 | bytes 31883264 | tf_op jit(solution)/shard_map/layer/pallas_call | solution.py:142
  47.5 4.0 %down.2 = f32[128,7168]{1,0:T(8,128)S(1)} custom-call(bf16[128,528]{1,0:T(8,128)(2,1)S(1)} %get-tuple-element.7.hid, bf16[2,256,7168]{2,1,0:T(8,128)(2,1)} %down.3, bf16[16,7168]{1,0:T(8,128)(2,1)} %shared_down.1), custom_call_target="tpu_custom_call" | custom-call | flops 968884224 | bytes 11239424 | tf_op jit(solution)/shard_map/down/pallas_call | solution.py:214
  52.3 3.0 %collective-permute-start.14 = (bf16[32,7168]{1,0:T(8,128)(2,1)S(1)}, bf16[32,7168]{1,0:T(8,128)(2,1)S(1)}, u32[]{:S(2)}, u32[]{:S(2)}) collective-permute-start(bf16[32,7168]{1,0:T(8,128)(2,1)S(1)} %get-tuple-element.15), channel_id=1, source_target_pairs={{0,64},{1,5},{2,66},{3,7},{4,68},{5,1},{6,70},{7,3},{8,72},{9,13},... | collective-permute-start | bytes 1376264 | tf_op jit(solution)/shard_map/ppermute | solution.py:35
  55.2 0.8 collective-permute-start.16
  56.0 2.4 %collective-permute-start.15 = (bf16[32,7168]{1,0:T(8,128)(2,1)S(1)}, bf16[32,7168]{1,0:T(8,128)(2,1)S(1)}, u32[]{:S(2)}, u32[]{:S(2)}) collective-permute-start(bf16[32,7168]{1,0:T(8,128)(2,1)S(1)} %get-tuple-element.17), channel_id=1, source_target_pairs={{0,96},{1,7},{2,98},{3,1},{4,100},{5,3},{6,102},{7,5},{8,104},{9,1... | collective-permute-start | bytes 1376264 | tf_op jit(solution)/shard_map/ppermute | solution.py:35
  58.4 4.2 %collective-permute-done.14 = bf16[32,7168]{1,0:T(8,128)(2,1)S(1)} collective-permute-done((bf16[32,7168]{1,0:T(8,128)(2,1)S(1)}, bf16[32,7168]{1,0:T(8,128)(2,1)S(1)}, u32[]{:S(2)}, u32[]{:S(2)}) %collective-permute-start.14) | collective-permute-done | bytes 458784 | tf_op jit(solution)/shard_map/ppermute | solution.py:35
  62.6 4.8 %collective-permute-done.16 = bf16[32,7168]{1,0:T(8,128)(2,1)S(1)} collective-permute-done((bf16[32,7168]{1,0:T(8,128)(2,1)S(1)}, bf16[32,7168]{1,0:T(8,128)(2,1)S(1)}, u32[]{:S(2)}, u32[]{:S(2)}) %collective-permute-start.16) | collective-permute-done | bytes 458784 | tf_op jit(solution)/shard_map/ppermute | solution.py:35
  67.7 1.5 %collective-permute-start.17 = (bf16[8,7168]{1,0:T(8,128)(2,1)S(1)}, bf16[8,7168]{1,0:T(8,128)(2,1)S(1)}, u32[]{:S(2)}, u32[]{:S(2)}) collective-permute-start(bf16[8,7168]{1,0:T(8,128)(2,1)S(1)} %get-tuple-element.18), channel_id=1, source_target_pairs={{0,16},{1,65},{2,18},{3,67},{4,20},{5,69},{6,22},{7,71},{8,24},{9,... | collective-permute-start | bytes 344072 | tf_op jit(solution)/shard_map/ppermute | solution.py:35
  69.2 2.6 %collective-permute-start.19 = (bf16[8,7168]{1,0:T(8,128)(2,1)S(1)}, bf16[8,7168]{1,0:T(8,128)(2,1)S(1)}, u32[]{:S(2)}, u32[]{:S(2)}) collective-permute-start(bf16[8,7168]{1,0:T(8,128)(2,1)S(1)} %get-tuple-element.19), channel_id=1, source_target_pairs={{0,8},{1,33},{2,10},{3,35},{4,12},{5,37},{6,14},{7,39},{8,16},{9,4... | collective-permute-start | bytes 344072 | tf_op jit(solution)/shard_map/ppermute | solution.py:35
  72.4 1.6 %collective-permute-done.17 = bf16[8,7168]{1,0:T(8,128)(2,1)S(1)} collective-permute-done((bf16[8,7168]{1,0:T(8,128)(2,1)S(1)}, bf16[8,7168]{1,0:T(8,128)(2,1)S(1)}, u32[]{:S(2)}, u32[]{:S(2)}) %collective-permute-start.17) | collective-permute-done | bytes 114720 | tf_op jit(solution)/shard_map/ppermute | solution.py:35
  74.0 1.2 %collective-permute-done.19 = bf16[8,7168]{1,0:T(8,128)(2,1)S(1)} collective-permute-done((bf16[8,7168]{1,0:T(8,128)(2,1)S(1)}, bf16[8,7168]{1,0:T(8,128)(2,1)S(1)}, u32[]{:S(2)}, u32[]{:S(2)}) %collective-permute-start.19) | collective-permute-done | bytes 114720 | tf_op jit(solution)/shard_map/ppermute | solution.py:35
  75.3 1.4 %collective-permute-done.18 = bf16[8,7168]{1,0:T(8,128)(2,1)S(1)} collective-permute-done((bf16[8,7168]{1,0:T(8,128)(2,1)S(1)}, bf16[8,7168]{1,0:T(8,128)(2,1)S(1)}, u32[]{:S(2)}, u32[]{:S(2)}) %collective-permute-start.18) | collective-permute-done | bytes 114720 | tf_op jit(solution)/shard_map/ppermute | solution.py:35
  76.8 1.5 %collective-permute-start.20 = (bf16[2,7168]{1,0:T(2,128)(2,1)S(1)}, bf16[2,7168]{1,0:T(2,128)(2,1)S(1)}, u32[]{:S(2)}, u32[]{:S(2)}) collective-permute-start(bf16[2,7168]{1,0:T(2,128)(2,1)S(1)} %get-tuple-element.21), channel_id=1, source_target_pairs={{0,4},{1,17},{2,6},{3,19},{4,0},{5,21},{6,2},{7,23},{8,12},{9,25},... | collective-permute-start | bytes 86024 | tf_op jit(solution)/shard_map/ppermute | solution.py:35
  78.3 2.6 %collective-permute-start.22 = (bf16[2,7168]{1,0:T(2,128)(2,1)S(1)}, bf16[2,7168]{1,0:T(2,128)(2,1)S(1)}, u32[]{:S(2)}, u32[]{:S(2)}) collective-permute-start(bf16[2,7168]{1,0:T(2,128)(2,1)S(1)} %get-tuple-element.22), channel_id=1, source_target_pairs={{0,2},{1,9},{2,4},{3,11},{4,6},{5,13},{6,0},{7,15},{8,10},{9,17},{... | collective-permute-start | bytes 86024 | tf_op jit(solution)/shard_map/ppermute | solution.py:35
  82.2 1.2 %collective-permute-done.22 = bf16[2,7168]{1,0:T(2,128)(2,1)S(1)} collective-permute-done((bf16[2,7168]{1,0:T(2,128)(2,1)S(1)}, bf16[2,7168]{1,0:T(2,128)(2,1)S(1)}, u32[]{:S(2)}, u32[]{:S(2)}) %collective-permute-start.22) | collective-permute-done | bytes 28704 | tf_op jit(solution)/shard_map/ppermute | solution.py:35
  83.4 1.4 %collective-permute-done.21 = bf16[2,7168]{1,0:T(2,128)(2,1)S(1)} collective-permute-done((bf16[2,7168]{1,0:T(2,128)(2,1)S(1)}, bf16[2,7168]{1,0:T(2,128)(2,1)S(1)}, u32[]{:S(2)}, u32[]{:S(2)}) %collective-permute-start.21) | collective-permute-done | bytes 28704 | tf_op jit(solution)/shard_map/ppermute | solution.py:35
  84.9 0.7 copy.11
  (27 shorter events, 4.9 us)
Async XLA Ops:
  0.9 6.4 %collective-permute-start.2 = (bf16[2,7296]{1,0:T(2,128)(2,1)S(1)}, bf16[2,7296]{1,0:T(2,128)(2,1)S(1)}, u32[]{:S(2)}, u32[]{:S(2)}) collective-permute-start(bf16[2,7296]{1,0:T(2,128)(2,1)S(1)} %prepare.1), channel_id=1, source_target_pairs={{4,0},{17,1},{6,2},{19,3},{0,4},{21,5},{2,6},{23,7},{12,8},{25,9},... | collective-permute-start | bytes 87560 | tf_op jit(solution)/shard_map/ppermute | solution.py:31
  4.1 5.1 %collective-permute-start.1 = (bf16[2,7296]{1,0:T(2,128)(2,1)S(1)}, bf16[2,7296]{1,0:T(2,128)(2,1)S(1)}, u32[]{:S(2)}, u32[]{:S(2)}) collective-permute-start(bf16[2,7296]{1,0:T(2,128)(2,1)S(1)} %prepare.1), channel_id=1, source_target_pairs={{6,0},{25,1},{0,2},{27,3},{2,4},{29,5},{4,6},{31,7},{14,8},{1,9},{... | collective-permute-start | bytes 87560 | tf_op jit(solution)/shard_map/ppermute | solution.py:31
  4.7 4.5 %collective-permute-start = (bf16[2,7296]{1,0:T(2,128)(2,1)S(1)}, bf16[2,7296]{1,0:T(2,128)(2,1)S(1)}, u32[]{:S(2)}, u32[]{:S(2)}) collective-permute-start(bf16[2,7296]{1,0:T(2,128)(2,1)S(1)} %prepare.1), channel_id=1, source_target_pairs={{2,0},{9,1},{4,2},{11,3},{6,4},{13,5},{0,6},{15,7},{10,8},{17,9},{... | collective-permute-start | bytes 87560 | tf_op jit(solution)/shard_map/ppermute | solution.py:31
  9.4 6.5 %collective-permute-start.5 = (bf16[8,7296]{1,0:T(8,128)(2,1)S(1)}, bf16[8,7296]{1,0:T(8,128)(2,1)S(1)}, u32[]{:S(2)}, u32[]{:S(2)}) collective-permute-start(bf16[8,7296]{1,0:T(8,128)(2,1)S(1)} %pad_maximum_fusion), channel_id=1, source_target_pairs={{16,0},{65,1},{18,2},{67,3},{20,4},{69,5},{22,6},{71,7},{24,8},{73... | collective-permute-start | bytes 350216 | tf_op jit(solution)/shard_map/ppermute | solution.py:31
  12.6 6.0 %collective-permute-start.4 = (bf16[8,7296]{1,0:T(8,128)(2,1)S(1)}, bf16[8,7296]{1,0:T(8,128)(2,1)S(1)}, u32[]{:S(2)}, u32[]{:S(2)}) collective-permute-start(bf16[8,7296]{1,0:T(8,128)(2,1)S(1)} %pad_maximum_fusion), channel_id=1, source_target_pairs={{24,0},{97,1},{26,2},{99,3},{28,4},{101,5},{30,6},{103,7},{0,8},{1... | collective-permute-start | bytes 350216 | tf_op jit(solution)/shard_map/ppermute | solution.py:31
  13.3 5.3 %collective-permute-start.3 = (bf16[8,7296]{1,0:T(8,128)(2,1)S(1)}, bf16[8,7296]{1,0:T(8,128)(2,1)S(1)}, u32[]{:S(2)}, u32[]{:S(2)}) collective-permute-start(bf16[8,7296]{1,0:T(8,128)(2,1)S(1)} %pad_maximum_fusion), channel_id=1, source_target_pairs={{8,0},{33,1},{10,2},{35,3},{12,4},{37,5},{14,6},{39,7},{16,8},{41,... | collective-permute-start | bytes 350216 | tf_op jit(solution)/shard_map/ppermute | solution.py:31
  18.9 10.6 %collective-permute-start.8 = (bf16[32,7296]{1,0:T(8,128)(2,1)S(1)}, bf16[32,7296]{1,0:T(8,128)(2,1)S(1)}, u32[]{:S(2)}, u32[]{:S(2)}) collective-permute-start(bf16[32,7296]{1,0:T(8,128)(2,1)S(1)} %concatenate.8.refs_0_), channel_id=1, source_target_pairs={{64,0},{5,1},{66,2},{7,3},{68,4},{1,5},{70,6},{3,7},{72,8},{13,9},... | collective-permute-start | bytes 1400840 | tf_op jit(solution)/shard_map/ppermute | solution.py:31
  22.8 11.5 %collective-permute-start.7 = (bf16[32,7296]{1,0:T(8,128)(2,1)S(1)}, bf16[32,7296]{1,0:T(8,128)(2,1)S(1)}, u32[]{:S(2)}, u32[]{:S(2)}) collective-permute-start(bf16[32,7296]{1,0:T(8,128)(2,1)S(1)} %concatenate.8.refs_0_), channel_id=1, source_target_pairs={{96,0},{7,1},{98,2},{1,3},{100,4},{3,5},{102,6},{5,7},{104,8},{15,... | collective-permute-start | bytes 1400840 | tf_op jit(solution)/shard_map/ppermute | solution.py:31
  23.9 11.6 %collective-permute-start.6 = (bf16[32,7296]{1,0:T(8,128)(2,1)S(1)}, bf16[32,7296]{1,0:T(8,128)(2,1)S(1)}, u32[]{:S(2)}, u32[]{:S(2)}) collective-permute-start(bf16[32,7296]{1,0:T(8,128)(2,1)S(1)} %concatenate.8.refs_0_), channel_id=1, source_target_pairs={{32,0},{3,1},{34,2},{5,3},{36,4},{7,5},{38,6},{1,7},{40,8},{11,9},... | collective-permute-start | bytes 1400840 | tf_op jit(solution)/shard_map/ppermute | solution.py:31
  26.1 9.4 %collective-permute-start.9 = (bf16[32,7296]{1,0:T(8,128)(2,1)S(1)}, bf16[32,7296]{1,0:T(8,128)(2,1)S(1)}, u32[]{:S(2)}, u32[]{:S(2)}) collective-permute-start(bf16[32,7296]{1,0:T(8,128)(2,1)S(1)} %concatenate.8.refs_0_), channel_id=1, source_target_pairs={{0,1},{1,0},{2,3},{3,2},{4,5},{5,4},{6,7},{7,6},{8,9},{9,8},{10,11... | collective-permute-start | bytes 1400840 | tf_op jit(solution)/shard_map/ppermute | solution.py:39
  29.5 6.0 %collective-permute-start.12 = (bf16[32,7296]{1,0:T(8,128)(2,1)S(1)}, bf16[32,7296]{1,0:T(8,128)(2,1)S(1)}, u32[]{:S(2)}, u32[]{:S(2)}) collective-permute-start(bf16[32,7296]{1,0:T(8,128)(2,1)S(1)} %collective-permute-done.8.refs_3_), channel_id=1, source_target_pairs={{0,1},{1,0},{2,3},{3,2},{4,5},{5,4},{6,7},{7,6},{8,9},{9,8},{10,11... | collective-permute-start | bytes 1400840 | tf_op jit(solution)/shard_map/ppermute | solution.py:39
  34.4 1.8 %collective-permute-start.11 = (bf16[32,7296]{1,0:T(8,128)(2,1)S(1)}, bf16[32,7296]{1,0:T(8,128)(2,1)S(1)}, u32[]{:S(2)}, u32[]{:S(2)}) collective-permute-start(bf16[32,7296]{1,0:T(8,128)(2,1)S(1)} %collective-permute-done.7.refs_2_), channel_id=1, source_target_pairs={{0,1},{1,0},{2,3},{3,2},{4,5},{5,4},{6,7},{7,6},{8,9},{9,8},{10,11... | collective-permute-start | bytes 1400840 | tf_op jit(solution)/shard_map/ppermute | solution.py:39
  35.5 2.0 %collective-permute-start.10 = (bf16[32,7296]{1,0:T(8,128)(2,1)S(1)}, bf16[32,7296]{1,0:T(8,128)(2,1)}, u32[]{:S(2)}, u32[]{:S(2)}) collective-permute-start(bf16[32,7296]{1,0:T(8,128)(2,1)S(1)} %collective-permute-done.6.refs_1_), channel_id=1, source_target_pairs={{0,1},{1,0},{2,3},{3,2},{4,5},{5,4},{6,7},{7,6},{8,9},{9,8},{10,11... | collective-permute-start | bytes 1400840 | tf_op jit(solution)/shard_map/ppermute | solution.py:39
  47.3 4.3 %collective-permute-start.13 = (bf16[128,7168]{1,0:T(8,128)(2,1)S(1)}, bf16[128,7168]{1,0:T(8,128)(2,1)S(1)}, u32[]{:S(2)}, u32[]{:S(2)}) collective-permute-start(bf16[128,7168]{1,0:T(8,128)(2,1)S(1)} %get-tuple-element.8), channel_id=1, source_target_pairs={{0,1},{1,0},{2,3},{3,2},{4,5},{5,4},{6,7},{7,6},{8,9},{9,8},{10,11... | collective-permute-start | bytes 5505032 | tf_op jit(solution)/shard_map/ppermute | solution.py:39
  52.3 10.3 %collective-permute-start.14 = (bf16[32,7168]{1,0:T(8,128)(2,1)S(1)}, bf16[32,7168]{1,0:T(8,128)(2,1)S(1)}, u32[]{:S(2)}, u32[]{:S(2)}) collective-permute-start(bf16[32,7168]{1,0:T(8,128)(2,1)S(1)} %get-tuple-element.15), channel_id=1, source_target_pairs={{0,64},{1,5},{2,66},{3,7},{4,68},{5,1},{6,70},{7,3},{8,72},{9,13},... | collective-permute-start | bytes 1376264 | tf_op jit(solution)/shard_map/ppermute | solution.py:35
  55.2 12.2 %collective-permute-start.16 = (bf16[32,7168]{1,0:T(8,128)(2,1)S(1)}, bf16[32,7168]{1,0:T(8,128)(2,1)S(1)}, u32[]{:S(2)}, u32[]{:S(2)}) collective-permute-start(bf16[32,7168]{1,0:T(8,128)(2,1)S(1)} %get-tuple-element.16), channel_id=1, source_target_pairs={{0,32},{1,3},{2,34},{3,5},{4,36},{5,7},{6,38},{7,1},{8,40},{9,11},... | collective-permute-start | bytes 1376264 | tf_op jit(solution)/shard_map/ppermute | solution.py:35
  56.0 11.4 %collective-permute-start.15 = (bf16[32,7168]{1,0:T(8,128)(2,1)S(1)}, bf16[32,7168]{1,0:T(8,128)(2,1)S(1)}, u32[]{:S(2)}, u32[]{:S(2)}) collective-permute-start(bf16[32,7168]{1,0:T(8,128)(2,1)S(1)} %get-tuple-element.17), channel_id=1, source_target_pairs={{0,96},{1,7},{2,98},{3,1},{4,100},{5,3},{6,102},{7,5},{8,104},{9,1... | collective-permute-start | bytes 1376264 | tf_op jit(solution)/shard_map/ppermute | solution.py:35
  67.7 6.4 %collective-permute-start.17 = (bf16[8,7168]{1,0:T(8,128)(2,1)S(1)}, bf16[8,7168]{1,0:T(8,128)(2,1)S(1)}, u32[]{:S(2)}, u32[]{:S(2)}) collective-permute-start(bf16[8,7168]{1,0:T(8,128)(2,1)S(1)} %get-tuple-element.18), channel_id=1, source_target_pairs={{0,16},{1,65},{2,18},{3,67},{4,20},{5,69},{6,22},{7,71},{8,24},{9,... | collective-permute-start | bytes 344072 | tf_op jit(solution)/shard_map/ppermute | solution.py:35
  69.2 6.1 %collective-permute-start.19 = (bf16[8,7168]{1,0:T(8,128)(2,1)S(1)}, bf16[8,7168]{1,0:T(8,128)(2,1)S(1)}, u32[]{:S(2)}, u32[]{:S(2)}) collective-permute-start(bf16[8,7168]{1,0:T(8,128)(2,1)S(1)} %get-tuple-element.19), channel_id=1, source_target_pairs={{0,8},{1,33},{2,10},{3,35},{4,12},{5,37},{6,14},{7,39},{8,16},{9,4... | collective-permute-start | bytes 344072 | tf_op jit(solution)/shard_map/ppermute | solution.py:35
  71.8 4.8 %collective-permute-start.18 = (bf16[8,7168]{1,0:T(8,128)(2,1)S(1)}, bf16[8,7168]{1,0:T(8,128)(2,1)S(1)}, u32[]{:S(2)}, u32[]{:S(2)}) collective-permute-start(bf16[8,7168]{1,0:T(8,128)(2,1)S(1)} %get-tuple-element.20), channel_id=1, source_target_pairs={{0,24},{1,97},{2,26},{3,99},{4,28},{5,101},{6,30},{7,103},{8,0},{9... | collective-permute-start | bytes 344072 | tf_op jit(solution)/shard_map/ppermute | solution.py:35
  76.8 5.5 %collective-permute-start.20 = (bf16[2,7168]{1,0:T(2,128)(2,1)S(1)}, bf16[2,7168]{1,0:T(2,128)(2,1)S(1)}, u32[]{:S(2)}, u32[]{:S(2)}) collective-permute-start(bf16[2,7168]{1,0:T(2,128)(2,1)S(1)} %get-tuple-element.21), channel_id=1, source_target_pairs={{0,4},{1,17},{2,6},{3,19},{4,0},{5,21},{6,2},{7,23},{8,12},{9,25},... | collective-permute-start | bytes 86024 | tf_op jit(solution)/shard_map/ppermute | solution.py:35
  78.3 5.1 %collective-permute-start.22 = (bf16[2,7168]{1,0:T(2,128)(2,1)S(1)}, bf16[2,7168]{1,0:T(2,128)(2,1)S(1)}, u32[]{:S(2)}, u32[]{:S(2)}) collective-permute-start(bf16[2,7168]{1,0:T(2,128)(2,1)S(1)} %get-tuple-element.22), channel_id=1, source_target_pairs={{0,2},{1,9},{2,4},{3,11},{4,6},{5,13},{6,0},{7,15},{8,10},{9,17},{... | collective-permute-start | bytes 86024 | tf_op jit(solution)/shard_map/ppermute | solution.py:35
  80.9 3.9 %collective-permute-start.21 = (bf16[2,7168]{1,0:T(2,128)(2,1)S(1)}, bf16[2,7168]{1,0:T(2,128)(2,1)S(1)}, u32[]{:S(2)}, u32[]{:S(2)}) collective-permute-start(bf16[2,7168]{1,0:T(2,128)(2,1)S(1)} %get-tuple-element.23), channel_id=1, source_target_pairs={{0,6},{1,25},{2,0},{3,27},{4,2},{5,29},{6,4},{7,31},{8,14},{9,1},{... | collective-permute-start | bytes 86024 | tf_op jit(solution)/shard_map/ppermute | solution.py:35

commit v6 on v4

--- a/solution.py
+++ b/solution.py
@@ -175,7 +175,7 @@
     )
 
 
-OSTEP = 1792
+OSTEP = 1024
 
 
 def down_kernel(hid, down, shared_down, out, buf, sems):

time: 86 us -> 86.1 us (level)
  no operation moved by 1% of the time
where the time goes in v6:
time: 86.1 us; the launch traced here: 85.9 us
  starting transfers between devices  36.1 us (42%)
  waiting for transfers between devices  32.7 us (38%)
  Pallas kernels  14.9 us (17%)
  local copies, waits for them, and re-layouts  1.11 us (1%)
  other arithmetic  0.99 us (1%)
    ppermute x9, starting transfers between devices, fetch(): lax.ppermute(block, AXES, [(flat(moved(p, stage, by)), flat(p)) for p in...  20.1 us
    ppermute x9, waiting for transfers between devices, send(): lax.ppermute(block, AXES, [(flat(p), flat(moved(p, stage, by))) for p in...  16.7 us
    ppermute x9, starting transfers between devices, send(): lax.ppermute(block, AXES, [(flat(p), flat(moved(p, stage, by))) for p in...  15.7 us
    ppermute x9, waiting for transfers between devices, fetch(): lax.ppermute(block, AXES, [(flat(moved(p, stage, by)), flat(p)) for p in...  14 us
    pallas_call x1, Pallas kernels, layer(): pl.pallas_call(layer_kernel, out_shape=(jax.ShapeDtypeStruct((128, 2 * un...  9.9 us
    pallas_call x1, Pallas kernels, down_own(): pl.pallas_call(down_kernel, grid=(1,), out_shape=jax.ShapeDtypeStruct((12...  4.08 us
    ppermute x5, waiting for transfers between devices, swap(): lax.ppermute(block, AXES, [(flat(p), flat(p[:3] + (1 - p[3],))) for p in...  1.95 us
  transfers between devices with their start and end apart: 23, of which 15 were waited for; matrix products, arithmetic and copies ran while one was open for 0% of the time, Pallas kernels for 5%

profile of v6, /device:TPU:0, one launch (start us, length us, event | category | flops | bytes accessed | tf_op | source)
XLA Modules:
  0.0 85.9 jit_solution(17273122952647435995)
XLA Ops:
  0.0 0.9 %prepare.1 = bf16[2,7296]{1,0:T(2,128)(2,1)S(1)} custom-call(f32[2,1,7168]{2,1,0:T(1,128)} %hidden.1, s32[2,1,8]{2,1,0:T(1,128)} %routes.1, s32[2,1,8]{2,1,0:T(1,128)} %slots.1, bf16[2,8]{1,0:T(2,128)(2,1)} %bitcast.8), custom_call_target="tpu_custom_call" | custom-call | tf_op jit(solution)/shard_map/prepare/pallas_call | solution.py:249
  0.9 3.2 %collective-permute-start.2 = (bf16[2,7296]{1,0:T(2,128)(2,1)S(1)}, bf16[2,7296]{1,0:T(2,128)(2,1)S(1)}, u32[]{:S(2)}, u32[]{:S(2)}) collective-permute-start(bf16[2,7296]{1,0:T(2,128)(2,1)S(1)} %prepare.1), channel_id=1, source_target_pairs={{4,0},{17,1},{6,2},{19,3},{0,4},{21,5},{2,6},{23,7},{12,8},{25,9},... | collective-permute-start | bytes 87560 | tf_op jit(solution)/shard_map/ppermute | solution.py:31
  4.7 2.6 %collective-permute-start = (bf16[2,7296]{1,0:T(2,128)(2,1)S(1)}, bf16[2,7296]{1,0:T(2,128)(2,1)S(1)}, u32[]{:S(2)}, u32[]{:S(2)}) collective-permute-start(bf16[2,7296]{1,0:T(2,128)(2,1)S(1)} %prepare.1), channel_id=1, source_target_pairs={{2,0},{9,1},{4,2},{11,3},{6,4},{13,5},{0,6},{15,7},{10,8},{17,9},{... | collective-permute-start | bytes 87560 | tf_op jit(solution)/shard_map/ppermute | solution.py:31
  7.4 1.8 %collective-permute-done.1 = bf16[2,7296]{1,0:T(2,128)(2,1)S(1)} collective-permute-done((bf16[2,7296]{1,0:T(2,128)(2,1)S(1)}, bf16[2,7296]{1,0:T(2,128)(2,1)S(1)}, u32[]{:S(2)}, u32[]{:S(2)}) %collective-permute-start.1) | collective-permute-done | bytes 29216 | tf_op jit(solution)/shard_map/ppermute | solution.py:31
  9.4 3.3 %collective-permute-start.5 = (bf16[8,7296]{1,0:T(8,128)(2,1)S(1)}, bf16[8,7296]{1,0:T(8,128)(2,1)S(1)}, u32[]{:S(2)}, u32[]{:S(2)}) collective-permute-start(bf16[8,7296]{1,0:T(8,128)(2,1)S(1)} %pad_maximum_fusion), channel_id=1, source_target_pairs={{16,0},{65,1},{18,2},{67,3},{20,4},{69,5},{22,6},{71,7},{24,8},{73... | collective-permute-start | bytes 350216 | tf_op jit(solution)/shard_map/ppermute | solution.py:31
  13.3 2.6 %collective-permute-start.3 = (bf16[8,7296]{1,0:T(8,128)(2,1)S(1)}, bf16[8,7296]{1,0:T(8,128)(2,1)S(1)}, u32[]{:S(2)}, u32[]{:S(2)}) collective-permute-start(bf16[8,7296]{1,0:T(8,128)(2,1)S(1)} %pad_maximum_fusion), channel_id=1, source_target_pairs={{8,0},{33,1},{10,2},{35,3},{12,4},{37,5},{14,6},{39,7},{16,8},{41,... | collective-permute-start | bytes 350216 | tf_op jit(solution)/shard_map/ppermute | solution.py:31
  15.9 2.8 %collective-permute-done.4 = bf16[8,7296]{1,0:T(8,128)(2,1)S(1)} collective-permute-done((bf16[8,7296]{1,0:T(8,128)(2,1)S(1)}, bf16[8,7296]{1,0:T(8,128)(2,1)S(1)}, u32[]{:S(2)}, u32[]{:S(2)}) %collective-permute-start.4) | collective-permute-done | bytes 116768 | tf_op jit(solution)/shard_map/ppermute | solution.py:31
  18.9 4.0 %collective-permute-start.8 = (bf16[32,7296]{1,0:T(8,128)(2,1)S(1)}, bf16[32,7296]{1,0:T(8,128)(2,1)S(1)}, u32[]{:S(2)}, u32[]{:S(2)}) collective-permute-start(bf16[32,7296]{1,0:T(8,128)(2,1)S(1)} %concatenate.8.refs_0_), channel_id=1, source_target_pairs={{64,0},{5,1},{66,2},{7,3},{68,4},{1,5},{70,6},{3,7},{72,8},{13,9},... | collective-permute-start | bytes 1400840 | tf_op jit(solution)/shard_map/ppermute | solution.py:31
  22.8 1.0 %collective-permute-start.7 = (bf16[32,7296]{1,0:T(8,128)(2,1)S(1)}, bf16[32,7296]{1,0:T(8,128)(2,1)S(1)}, u32[]{:S(2)}, u32[]{:S(2)}) collective-permute-start(bf16[32,7296]{1,0:T(8,128)(2,1)S(1)} %concatenate.8.refs_0_), channel_id=1, source_target_pairs={{96,0},{7,1},{98,2},{1,3},{100,4},{3,5},{102,6},{5,7},{104,8},{15,... | collective-permute-start | bytes 1400840 | tf_op jit(solution)/shard_map/ppermute | solution.py:31
  23.9 2.2 %collective-permute-start.6 = (bf16[32,7296]{1,0:T(8,128)(2,1)S(1)}, bf16[32,7296]{1,0:T(8,128)(2,1)S(1)}, u32[]{:S(2)}, u32[]{:S(2)}) collective-permute-start(bf16[32,7296]{1,0:T(8,128)(2,1)S(1)} %concatenate.8.refs_0_), channel_id=1, source_target_pairs={{32,0},{3,1},{34,2},{5,3},{36,4},{7,5},{38,6},{1,7},{40,8},{11,9},... | collective-permute-start | bytes 1400840 | tf_op jit(solution)/shard_map/ppermute | solution.py:31
  26.1 3.4 %collective-permute-done.8.refs_3_ = bf16[32,7296]{1,0:T(8,128)(2,1)S(1)} collective-permute-done((bf16[32,7296]{1,0:T(8,128)(2,1)S(1)}, bf16[32,7296]{1,0:T(8,128)(2,1)S(1)}, u32[]{:S(2)}, u32[]{:S(2)}) %collective-permute-start.8) | collective-permute-done | bytes 466976 | tf_op jit(solution)/shard_map/ppermute | solution.py:31
  29.5 4.9 %collective-permute-done.7.refs_2_ = bf16[32,7296]{1,0:T(8,128)(2,1)S(1)} collective-permute-done((bf16[32,7296]{1,0:T(8,128)(2,1)S(1)}, bf16[32,7296]{1,0:T(8,128)(2,1)S(1)}, u32[]{:S(2)}, u32[]{:S(2)}) %collective-permute-start.7) | collective-permute-done | bytes 466976 | tf_op jit(solution)/shard_map/ppermute | solution.py:31
  34.4 1.1 %collective-permute-done.6.refs_1_ = bf16[32,7296]{1,0:T(8,128)(2,1)S(1)} collective-permute-done((bf16[32,7296]{1,0:T(8,128)(2,1)S(1)}, bf16[32,7296]{1,0:T(8,128)(2,1)S(1)}, u32[]{:S(2)}, u32[]{:S(2)}) %collective-permute-start.6) | collective-permute-done | bytes 466976 | tf_op jit(solution)/shard_map/ppermute | solution.py:31
  35.5 0.8 collective-permute-done.11.refs_6_
  36.2 1.2 %collective-permute-done.10.refs_5_ = bf16[32,7296]{1,0:T(8,128)(2,1)} collective-permute-done((bf16[32,7296]{1,0:T(8,128)(2,1)S(1)}, bf16[32,7296]{1,0:T(8,128)(2,1)}, u32[]{:S(2)}, u32[]{:S(2)}) %collective-permute-start.10) | collective-permute-done | bytes 466976 | tf_op jit(solution)/shard_map/ppermute | solution.py:39
  37.4 9.9 %layer.1 = (bf16[128,528]{1,0:T(8,128)(2,1)S(1)}, bf16[128,7168]{1,0:T(8,128)(2,1)S(1)}) custom-call(s32[1,1]{1,0:T(1,128)} %bitcast.first_ref, bf16[32,7296]{1,0:T(8,128)(2,1)S(1)} %concatenate.8.refs_0_, bf16[32,7296]{1,0:T(8,128)(2,1)S(1)} %collective-permute-done.6.refs_1_, bf16[32,7296]{1,0:T(8,128)(2,1)S(1)} %collective-permute-done.7.refs_2_, ...), custom_call_target="tpu_custom_call" | custom-call | flops 5813305344 | bytes 31883264 | tf_op jit(solution)/shard_map/layer/pallas_call | solution.py:142
  47.5 4.1 %down.2 = f32[128,7168]{1,0:T(8,128)S(1)} custom-call(bf16[128,528]{1,0:T(8,128)(2,1)S(1)} %get-tuple-element.7.hid, bf16[2,256,7168]{2,1,0:T(8,128)(2,1)} %down.3, bf16[16,7168]{1,0:T(8,128)(2,1)} %shared_down.1), custom_call_target="tpu_custom_call" | custom-call | flops 968884224 | bytes 11239424 | tf_op jit(solution)/shard_map/down/pallas_call | solution.py:214
  52.3 3.0 %collective-permute-start.14 = (bf16[32,7168]{1,0:T(8,128)(2,1)S(1)}, bf16[32,7168]{1,0:T(8,128)(2,1)S(1)}, u32[]{:S(2)}, u32[]{:S(2)}) collective-permute-start(bf16[32,7168]{1,0:T(8,128)(2,1)S(1)} %get-tuple-element.13), channel_id=1, source_target_pairs={{0,64},{1,5},{2,66},{3,7},{4,68},{5,1},{6,70},{7,3},{8,72},{9,13},... | collective-permute-start | bytes 1376264 | tf_op jit(solution)/shard_map/ppermute | solution.py:35
  55.3 0.8 collective-permute-start.16
  56.0 2.4 %collective-permute-start.15 = (bf16[32,7168]{1,0:T(8,128)(2,1)S(1)}, bf16[32,7168]{1,0:T(8,128)(2,1)S(1)}, u32[]{:S(2)}, u32[]{:S(2)}) collective-permute-start(bf16[32,7168]{1,0:T(8,128)(2,1)S(1)} %get-tuple-element.15), channel_id=1, source_target_pairs={{0,96},{1,7},{2,98},{3,1},{4,100},{5,3},{6,102},{7,5},{8,104},{9,1... | collective-permute-start | bytes 1376264 | tf_op jit(solution)/shard_map/ppermute | solution.py:35
  58.5 4.2 %collective-permute-done.14 = bf16[32,7168]{1,0:T(8,128)(2,1)S(1)} collective-permute-done((bf16[32,7168]{1,0:T(8,128)(2,1)S(1)}, bf16[32,7168]{1,0:T(8,128)(2,1)S(1)}, u32[]{:S(2)}, u32[]{:S(2)}) %collective-permute-start.14) | collective-permute-done | bytes 458784 | tf_op jit(solution)/shard_map/ppermute | solution.py:35
  62.6 4.8 %collective-permute-done.16 = bf16[32,7168]{1,0:T(8,128)(2,1)S(1)} collective-permute-done((bf16[32,7168]{1,0:T(8,128)(2,1)S(1)}, bf16[32,7168]{1,0:T(8,128)(2,1)S(1)}, u32[]{:S(2)}, u32[]{:S(2)}) %collective-permute-start.16) | collective-permute-done | bytes 458784 | tf_op jit(solution)/shard_map/ppermute | solution.py:35
  67.7 1.5 %collective-permute-start.17 = (bf16[8,7168]{1,0:T(8,128)(2,1)S(1)}, bf16[8,7168]{1,0:T(8,128)(2,1)S(1)}, u32[]{:S(2)}, u32[]{:S(2)}) collective-permute-start(bf16[8,7168]{1,0:T(8,128)(2,1)S(1)} %get-tuple-element.16), channel_id=1, source_target_pairs={{0,16},{1,65},{2,18},{3,67},{4,20},{5,69},{6,22},{7,71},{8,24},{9,... | collective-permute-start | bytes 344072 | tf_op jit(solution)/shard_map/ppermute | solution.py:35
  69.2 2.6 %collective-permute-start.19 = (bf16[8,7168]{1,0:T(8,128)(2,1)S(1)}, bf16[8,7168]{1,0:T(8,128)(2,1)S(1)}, u32[]{:S(2)}, u32[]{:S(2)}) collective-permute-start(bf16[8,7168]{1,0:T(8,128)(2,1)S(1)} %get-tuple-element.17), channel_id=1, source_target_pairs={{0,8},{1,33},{2,10},{3,35},{4,12},{5,37},{6,14},{7,39},{8,16},{9,4... | collective-permute-start | bytes 344072 | tf_op jit(solution)/shard_map/ppermute | solution.py:35
  72.5 1.6 %collective-permute-done.17 = bf16[8,7168]{1,0:T(8,128)(2,1)S(1)} collective-permute-done((bf16[8,7168]{1,0:T(8,128)(2,1)S(1)}, bf16[8,7168]{1,0:T(8,128)(2,1)S(1)}, u32[]{:S(2)}, u32[]{:S(2)}) %collective-permute-start.17) | collective-permute-done | bytes 114720 | tf_op jit(solution)/shard_map/ppermute | solution.py:35
  74.1 1.2 %collective-permute-done.19 = bf16[8,7168]{1,0:T(8,128)(2,1)S(1)} collective-permute-done((bf16[8,7168]{1,0:T(8,128)(2,1)S(1)}, bf16[8,7168]{1,0:T(8,128)(2,1)S(1)}, u32[]{:S(2)}, u32[]{:S(2)}) %collective-permute-start.19) | collective-permute-done | bytes 114720 | tf_op jit(solution)/shard_map/ppermute | solution.py:35
  75.3 1.4 %collective-permute-done.18 = bf16[8,7168]{1,0:T(8,128)(2,1)S(1)} collective-permute-done((bf16[8,7168]{1,0:T(8,128)(2,1)S(1)}, bf16[8,7168]{1,0:T(8,128)(2,1)S(1)}, u32[]{:S(2)}, u32[]{:S(2)}) %collective-permute-start.18) | collective-permute-done | bytes 114720 | tf_op jit(solution)/shard_map/ppermute | solution.py:35
  76.8 1.5 %collective-permute-start.20 = (f32[2,7168]{1,0:T(2,128)S(1)}, f32[2,7168]{1,0:T(2,128)S(1)}, u32[]{:S(2)}, u32[]{:S(2)}) collective-permute-start(f32[2,7168]{1,0:T(2,128)S(1)} %get-tuple-element.19), channel_id=1, source_target_pairs={{0,4},{1,17},{2,6},{3,19},{4,0},{5,21},{6,2},{7,23},{8,12},{9,25},... | collective-permute-start | bytes 172040 | tf_op jit(solution)/shard_map/ppermute | solution.py:35
  78.3 2.6 %collective-permute-start.22 = (f32[2,7168]{1,0:T(2,128)S(1)}, f32[2,7168]{1,0:T(2,128)S(1)}, u32[]{:S(2)}, u32[]{:S(2)}) collective-permute-start(f32[2,7168]{1,0:T(2,128)S(1)} %get-tuple-element.20), channel_id=1, source_target_pairs={{0,2},{1,9},{2,4},{3,11},{4,6},{5,13},{6,0},{7,15},{8,10},{9,17},{... | collective-permute-start | bytes 172040 | tf_op jit(solution)/shard_map/ppermute | solution.py:35
  81.6 1.0 %collective-permute-done.20 = f32[2,7168]{1,0:T(2,128)S(1)} collective-permute-done((f32[2,7168]{1,0:T(2,128)S(1)}, f32[2,7168]{1,0:T(2,128)S(1)}, u32[]{:S(2)}, u32[]{:S(2)}) %collective-permute-start.20) | collective-permute-done | bytes 57376 | tf_op jit(solution)/shard_map/ppermute | solution.py:35
  82.5 1.2 %collective-permute-done.22 = f32[2,7168]{1,0:T(2,128)S(1)} collective-permute-done((f32[2,7168]{1,0:T(2,128)S(1)}, f32[2,7168]{1,0:T(2,128)S(1)}, u32[]{:S(2)}, u32[]{:S(2)}) %collective-permute-start.22) | collective-permute-done | bytes 57376 | tf_op jit(solution)/shard_map/ppermute | solution.py:35
  83.7 1.4 %collective-permute-done.21 = f32[2,7168]{1,0:T(2,128)S(1)} collective-permute-done((f32[2,7168]{1,0:T(2,128)S(1)}, f32[2,7168]{1,0:T(2,128)S(1)}, u32[]{:S(2)}, u32[]{:S(2)}) %collective-permute-start.21) | collective-permute-done | bytes 57376 | tf_op jit(solution)/shard_map/ppermute | solution.py:35
  (27 shorter events, 4.8 us)
Async XLA Ops:
  0.9 6.4 %collective-permute-start.2 = (bf16[2,7296]{1,0:T(2,128)(2,1)S(1)}, bf16[2,7296]{1,0:T(2,128)(2,1)S(1)}, u32[]{:S(2)}, u32[]{:S(2)}) collective-permute-start(bf16[2,7296]{1,0:T(2,128)(2,1)S(1)} %prepare.1), channel_id=1, source_target_pairs={{4,0},{17,1},{6,2},{19,3},{0,4},{21,5},{2,6},{23,7},{12,8},{25,9},... | collective-permute-start | bytes 87560 | tf_op jit(solution)/shard_map/ppermute | solution.py:31
  4.1 5.1 %collective-permute-start.1 = (bf16[2,7296]{1,0:T(2,128)(2,1)S(1)}, bf16[2,7296]{1,0:T(2,128)(2,1)S(1)}, u32[]{:S(2)}, u32[]{:S(2)}) collective-permute-start(bf16[2,7296]{1,0:T(2,128)(2,1)S(1)} %prepare.1), channel_id=1, source_target_pairs={{6,0},{25,1},{0,2},{27,3},{2,4},{29,5},{4,6},{31,7},{14,8},{1,9},{... | collective-permute-start | bytes 87560 | tf_op jit(solution)/shard_map/ppermute | solution.py:31
  4.7 4.5 %collective-permute-start = (bf16[2,7296]{1,0:T(2,128)(2,1)S(1)}, bf16[2,7296]{1,0:T(2,128)(2,1)S(1)}, u32[]{:S(2)}, u32[]{:S(2)}) collective-permute-start(bf16[2,7296]{1,0:T(2,128)(2,1)S(1)} %prepare.1), channel_id=1, source_target_pairs={{2,0},{9,1},{4,2},{11,3},{6,4},{13,5},{0,6},{15,7},{10,8},{17,9},{... | collective-permute-start | bytes 87560 | tf_op jit(solution)/shard_map/ppermute | solution.py:31
  9.4 6.5 %collective-permute-start.5 = (bf16[8,7296]{1,0:T(8,128)(2,1)S(1)}, bf16[8,7296]{1,0:T(8,128)(2,1)S(1)}, u32[]{:S(2)}, u32[]{:S(2)}) collective-permute-start(bf16[8,7296]{1,0:T(8,128)(2,1)S(1)} %pad_maximum_fusion), channel_id=1, source_target_pairs={{16,0},{65,1},{18,2},{67,3},{20,4},{69,5},{22,6},{71,7},{24,8},{73... | collective-permute-start | bytes 350216 | tf_op jit(solution)/shard_map/ppermute | solution.py:31
  12.6 6.0 %collective-permute-start.4 = (bf16[8,7296]{1,0:T(8,128)(2,1)S(1)}, bf16[8,7296]{1,0:T(8,128)(2,1)S(1)}, u32[]{:S(2)}, u32[]{:S(2)}) collective-permute-start(bf16[8,7296]{1,0:T(8,128)(2,1)S(1)} %pad_maximum_fusion), channel_id=1, source_target_pairs={{24,0},{97,1},{26,2},{99,3},{28,4},{101,5},{30,6},{103,7},{0,8},{1... | collective-permute-start | bytes 350216 | tf_op jit(solution)/shard_map/ppermute | solution.py:31
  13.3 5.3 %collective-permute-start.3 = (bf16[8,7296]{1,0:T(8,128)(2,1)S(1)}, bf16[8,7296]{1,0:T(8,128)(2,1)S(1)}, u32[]{:S(2)}, u32[]{:S(2)}) collective-permute-start(bf16[8,7296]{1,0:T(8,128)(2,1)S(1)} %pad_maximum_fusion), channel_id=1, source_target_pairs={{8,0},{33,1},{10,2},{35,3},{12,4},{37,5},{14,6},{39,7},{16,8},{41,... | collective-permute-start | bytes 350216 | tf_op jit(solution)/shard_map/ppermute | solution.py:31
  18.9 10.6 %collective-permute-start.8 = (bf16[32,7296]{1,0:T(8,128)(2,1)S(1)}, bf16[32,7296]{1,0:T(8,128)(2,1)S(1)}, u32[]{:S(2)}, u32[]{:S(2)}) collective-permute-start(bf16[32,7296]{1,0:T(8,128)(2,1)S(1)} %concatenate.8.refs_0_), channel_id=1, source_target_pairs={{64,0},{5,1},{66,2},{7,3},{68,4},{1,5},{70,6},{3,7},{72,8},{13,9},... | collective-permute-start | bytes 1400840 | tf_op jit(solution)/shard_map/ppermute | solution.py:31
  22.8 11.5 %collective-permute-start.7 = (bf16[32,7296]{1,0:T(8,128)(2,1)S(1)}, bf16[32,7296]{1,0:T(8,128)(2,1)S(1)}, u32[]{:S(2)}, u32[]{:S(2)}) collective-permute-start(bf16[32,7296]{1,0:T(8,128)(2,1)S(1)} %concatenate.8.refs_0_), channel_id=1, source_target_pairs={{96,0},{7,1},{98,2},{1,3},{100,4},{3,5},{102,6},{5,7},{104,8},{15,... | collective-permute-start | bytes 1400840 | tf_op jit(solution)/shard_map/ppermute | solution.py:31
  23.9 11.6 %collective-permute-start.6 = (bf16[32,7296]{1,0:T(8,128)(2,1)S(1)}, bf16[32,7296]{1,0:T(8,128)(2,1)S(1)}, u32[]{:S(2)}, u32[]{:S(2)}) collective-permute-start(bf16[32,7296]{1,0:T(8,128)(2,1)S(1)} %concatenate.8.refs_0_), channel_id=1, source_target_pairs={{32,0},{3,1},{34,2},{5,3},{36,4},{7,5},{38,6},{1,7},{40,8},{11,9},... | collective-permute-start | bytes 1400840 | tf_op jit(solution)/shard_map/ppermute | solution.py:31
  26.1 9.4 %collective-permute-start.9 = (bf16[32,7296]{1,0:T(8,128)(2,1)S(1)}, bf16[32,7296]{1,0:T(8,128)(2,1)S(1)}, u32[]{:S(2)}, u32[]{:S(2)}) collective-permute-start(bf16[32,7296]{1,0:T(8,128)(2,1)S(1)} %concatenate.8.refs_0_), channel_id=1, source_target_pairs={{0,1},{1,0},{2,3},{3,2},{4,5},{5,4},{6,7},{7,6},{8,9},{9,8},{10,11... | collective-permute-start | bytes 1400840 | tf_op jit(solution)/shard_map/ppermute | solution.py:39
  29.5 6.0 %collective-permute-start.12 = (bf16[32,7296]{1,0:T(8,128)(2,1)S(1)}, bf16[32,7296]{1,0:T(8,128)(2,1)S(1)}, u32[]{:S(2)}, u32[]{:S(2)}) collective-permute-start(bf16[32,7296]{1,0:T(8,128)(2,1)S(1)} %collective-permute-done.8.refs_3_), channel_id=1, source_target_pairs={{0,1},{1,0},{2,3},{3,2},{4,5},{5,4},{6,7},{7,6},{8,9},{9,8},{10,11... | collective-permute-start | bytes 1400840 | tf_op jit(solution)/shard_map/ppermute | solution.py:39
  34.4 1.8 %collective-permute-start.11 = (bf16[32,7296]{1,0:T(8,128)(2,1)S(1)}, bf16[32,7296]{1,0:T(8,128)(2,1)S(1)}, u32[]{:S(2)}, u32[]{:S(2)}) collective-permute-start(bf16[32,7296]{1,0:T(8,128)(2,1)S(1)} %collective-permute-done.7.refs_2_), channel_id=1, source_target_pairs={{0,1},{1,0},{2,3},{3,2},{4,5},{5,4},{6,7},{7,6},{8,9},{9,8},{10,11... | collective-permute-start | bytes 1400840 | tf_op jit(solution)/shard_map/ppermute | solution.py:39
  35.5 2.0 %collective-permute-start.10 = (bf16[32,7296]{1,0:T(8,128)(2,1)S(1)}, bf16[32,7296]{1,0:T(8,128)(2,1)}, u32[]{:S(2)}, u32[]{:S(2)}) collective-permute-start(bf16[32,7296]{1,0:T(8,128)(2,1)S(1)} %collective-permute-done.6.refs_1_), channel_id=1, source_target_pairs={{0,1},{1,0},{2,3},{3,2},{4,5},{5,4},{6,7},{7,6},{8,9},{9,8},{10,11... | collective-permute-start | bytes 1400840 | tf_op jit(solution)/shard_map/ppermute | solution.py:39
  47.3 4.3 %collective-permute-start.13 = (bf16[128,7168]{1,0:T(8,128)(2,1)S(1)}, bf16[128,7168]{1,0:T(8,128)(2,1)S(1)}, u32[]{:S(2)}, u32[]{:S(2)}) collective-permute-start(bf16[128,7168]{1,0:T(8,128)(2,1)S(1)} %get-tuple-element.8), channel_id=1, source_target_pairs={{0,1},{1,0},{2,3},{3,2},{4,5},{5,4},{6,7},{7,6},{8,9},{9,8},{10,11... | collective-permute-start | bytes 5505032 | tf_op jit(solution)/shard_map/ppermute | solution.py:39
  52.3 10.3 %collective-permute-start.14 = (bf16[32,7168]{1,0:T(8,128)(2,1)S(1)}, bf16[32,7168]{1,0:T(8,128)(2,1)S(1)}, u32[]{:S(2)}, u32[]{:S(2)}) collective-permute-start(bf16[32,7168]{1,0:T(8,128)(2,1)S(1)} %get-tuple-element.13), channel_id=1, source_target_pairs={{0,64},{1,5},{2,66},{3,7},{4,68},{5,1},{6,70},{7,3},{8,72},{9,13},... | collective-permute-start | bytes 1376264 | tf_op jit(solution)/shard_map/ppermute | solution.py:35
  55.3 12.2 %collective-permute-start.16 = (bf16[32,7168]{1,0:T(8,128)(2,1)S(1)}, bf16[32,7168]{1,0:T(8,128)(2,1)S(1)}, u32[]{:S(2)}, u32[]{:S(2)}) collective-permute-start(bf16[32,7168]{1,0:T(8,128)(2,1)S(1)} %get-tuple-element.14), channel_id=1, source_target_pairs={{0,32},{1,3},{2,34},{3,5},{4,36},{5,7},{6,38},{7,1},{8,40},{9,11},... | collective-permute-start | bytes 1376264 | tf_op jit(solution)/shard_map/ppermute | solution.py:35
  56.0 11.4 %collective-permute-start.15 = (bf16[32,7168]{1,0:T(8,128)(2,1)S(1)}, bf16[32,7168]{1,0:T(8,128)(2,1)S(1)}, u32[]{:S(2)}, u32[]{:S(2)}) collective-permute-start(bf16[32,7168]{1,0:T(8,128)(2,1)S(1)} %get-tuple-element.15), channel_id=1, source_target_pairs={{0,96},{1,7},{2,98},{3,1},{4,100},{5,3},{6,102},{7,5},{8,104},{9,1... | collective-permute-start | bytes 1376264 | tf_op jit(solution)/shard_map/ppermute | solution.py:35
  67.7 6.4 %collective-permute-start.17 = (bf16[8,7168]{1,0:T(8,128)(2,1)S(1)}, bf16[8,7168]{1,0:T(8,128)(2,1)S(1)}, u32[]{:S(2)}, u32[]{:S(2)}) collective-permute-start(bf16[8,7168]{1,0:T(8,128)(2,1)S(1)} %get-tuple-element.16), channel_id=1, source_target_pairs={{0,16},{1,65},{2,18},{3,67},{4,20},{5,69},{6,22},{7,71},{8,24},{9,... | collective-permute-start | bytes 344072 | tf_op jit(solution)/shard_map/ppermute | solution.py:35
  69.2 6.1 %collective-permute-start.19 = (bf16[8,7168]{1,0:T(8,128)(2,1)S(1)}, bf16[8,7168]{1,0:T(8,128)(2,1)S(1)}, u32[]{:S(2)}, u32[]{:S(2)}) collective-permute-start(bf16[8,7168]{1,0:T(8,128)(2,1)S(1)} %get-tuple-element.17), channel_id=1, source_target_pairs={{0,8},{1,33},{2,10},{3,35},{4,12},{5,37},{6,14},{7,39},{8,16},{9,4... | collective-permute-start | bytes 344072 | tf_op jit(solution)/shard_map/ppermute | solution.py:35
  71.9 4.8 %collective-permute-start.18 = (bf16[8,7168]{1,0:T(8,128)(2,1)S(1)}, bf16[8,7168]{1,0:T(8,128)(2,1)S(1)}, u32[]{:S(2)}, u32[]{:S(2)}) collective-permute-start(bf16[8,7168]{1,0:T(8,128)(2,1)S(1)} %get-tuple-element.18), channel_id=1, source_target_pairs={{0,24},{1,97},{2,26},{3,99},{4,28},{5,101},{6,30},{7,103},{8,0},{9... | collective-permute-start | bytes 344072 | tf_op jit(solution)/shard_map/ppermute | solution.py:35
  76.8 5.8 %collective-permute-start.20 = (f32[2,7168]{1,0:T(2,128)S(1)}, f32[2,7168]{1,0:T(2,128)S(1)}, u32[]{:S(2)}, u32[]{:S(2)}) collective-permute-start(f32[2,7168]{1,0:T(2,128)S(1)} %get-tuple-element.19), channel_id=1, source_target_pairs={{0,4},{1,17},{2,6},{3,19},{4,0},{5,21},{6,2},{7,23},{8,12},{9,25},... | collective-permute-start | bytes 172040 | tf_op jit(solution)/shard_map/ppermute | solution.py:35
  78.3 5.4 %collective-permute-start.22 = (f32[2,7168]{1,0:T(2,128)S(1)}, f32[2,7168]{1,0:T(2,128)S(1)}, u32[]{:S(2)}, u32[]{:S(2)}) collective-permute-start(f32[2,7168]{1,0:T(2,128)S(1)} %get-tuple-element.20), channel_id=1, source_target_pairs={{0,2},{1,9},{2,4},{3,11},{4,6},{5,13},{6,0},{7,15},{8,10},{9,17},{... | collective-permute-start | bytes 172040 | tf_op jit(solution)/shard_map/ppermute | solution.py:35
  81.0 4.2 %collective-permute-start.21 = (f32[2,7168]{1,0:T(2,128)S(1)}, f32[2,7168]{1,0:T(2,128)S(1)}, u32[]{:S(2)}, u32[]{:S(2)}) collective-permute-start(f32[2,7168]{1,0:T(2,128)S(1)} %get-tuple-element.21), channel_id=1, source_target_pairs={{0,6},{1,25},{2,0},{3,27},{4,2},{5,29},{6,4},{7,31},{8,14},{9,1},{... | collective-permute-start | bytes 172040 | tf_op jit(solution)/shard_map/ppermute | solution.py:35
